TPU v7x, 256 devices: a whole 4x4x8 slice. The times are simulated.
256 devices in a mesh: seg: 16 (over y, x_lo, core), head: 16 (over z, x_hi).
Axes of the slice: x: 4 (x_hi: 2, x_lo: 2; x = x_hi * 2 + x_lo), y: 4, z: 8, core: 2. Of those that a mesh axis runs over, the one named last changes fastest.
Arguments:
- queries: bfloat16 [2048, 73728], P('seg', 'head')
- leaf_latent: bfloat16 [2048, 576], P('seg'), may hold values from -5 to 5
- ancestor_latent: bfloat16 [2048, 576], P('seg')
- ancestor_parent: int32 [16], replicated, may hold values from -1 to 14, as said below
- leaf_parent: int32 [16], P('seg'), may hold values from 7 to 15, as said below
- leaf_length: int32 [16], P('seg'), may hold values from 1 to 128
- value_up: bfloat16 [128, 512, 128], P('head'), may hold values from -0.25 to 0.25
- out_weight: bfloat16 [128, 128, 7168], P('head', 'seg'), may hold values from -0.0625 to 0.0625
Outputs:
- mixed: bfloat16 [2048, 7168], P('seg', 'head')
Inputs may be any that keep to these rules, and one draw needn't show every extreme that they name: ancestor_parent[0] = -1; for 0 < i < 8 the parent is i - 1; beyond, the parent lies in [7, i - 1], and the last segment's parent is the one before it. `leaf_parent`: each leaf's parent is an ancestor segment of index 7 or more.
All inputs are finite; a program needn't handle non-finite values.
Results may differ from a plain program's by a relative error of at most 0.023.
Values may be sent and summed in bfloat16 or wider, within the bound.
No kernel may reach another device: no remote copies, remote signals or barrier semaphores. Data moves between devices by JAX's collectives and lax.ppermute only.
A program may use at most 128 MiB of HBM per device.

v0:
```python
import jax
import jax.numpy as jnp
from jax import lax
from jax.sharding import PartitionSpec as P

LATENT = 512
ROPE = 64
NOPE = 128
SEG_LEN = 128


NEG = -1e30


def chains(parents, start):
    count = parents.shape[0]
    ids = jnp.arange(count, dtype=jnp.int32)

    def advance(step, state):
        marked, current = state
        match = ids[None, :] == current[:, None]
        marked = marked | match
        nxt = jnp.sum(jnp.where(match, parents[None, :], 0), axis=1)
        current = jnp.where(current >= 0, nxt, -1)
        return (marked, current)

    marked = jnp.zeros((start.shape[0], count), dtype=bool)
    marked, current = lax.fori_loop(0, count, advance, (marked, start))
    return marked


def per_device(
    queries,
    leaf_latent,
    ancestor_latent,
    ancestor_parent,
    leaf_parent,
    leaf_length,
    value_up,
    out_weight,
):
    width = LATENT + ROPE
    scale = (NOPE + ROPE) ** (-0.5)
    leaves = leaf_parent.shape[0]
    heads_dev = queries.shape[1] // width
    query = queries.reshape(leaves, SEG_LEN, heads_dev, width)
    own = leaf_latent.reshape(leaves, SEG_LEN, width)
    pos = jnp.arange(SEG_LEN, dtype=jnp.int32)
    used = chains(ancestor_parent, leaf_parent)
    seg_ids_all = jnp.arange(ancestor_parent.shape[0], dtype=jnp.int32)
    s_own = jnp.einsum("lqhc,lkc->lhqk", query, own, preferred_element_type=jnp.float32) * scale
    keep_own = (pos[None, :, None] >= pos[None, None, :]) & (
        pos[None, None, :] < leaf_length[:, None, None]
    )
    s_own = jnp.where(keep_own[:, None], s_own, NEG)
    top = jnp.max(s_own, axis=3)
    expo = jnp.exp(s_own - top[..., None])
    total = jnp.sum(expo, axis=3)
    accum = jnp.einsum(
        "lhqk,lkc->lhqc",
        expo.astype(jnp.bfloat16),
        own[:, :, :LATENT],
        preferred_element_type=jnp.float32,
    )
    piece = lax.all_gather(ancestor_latent, "seg", axis=0, tiled=True)
    rows = jnp.arange(piece.shape[0], dtype=jnp.int32)
    keep = jnp.any(
        ((rows // SEG_LEN)[:, None] == seg_ids_all[None, :])[None] & used[:, None, :], axis=2
    )
    summed = total
    acc = accum
    scores = jnp.einsum("lqhc,kc->lhqk", query, piece, preferred_element_type=jnp.float32) * scale
    scores = jnp.where(keep[:, None, None, :], scores, NEG)
    new_high = jnp.maximum(top, jnp.max(scores, axis=3))
    factor = jnp.exp(top - new_high)
    probs = jnp.exp(scores - new_high[..., None])
    summed = summed * factor + jnp.sum(probs, axis=3)
    acc = acc * factor[..., None] + jnp.einsum(
        "lhqk,kc->lhqc",
        probs.astype(jnp.bfloat16),
        piece[:, :LATENT],
        preferred_element_type=jnp.float32,
    )
    latent_out = (acc / summed[..., None]).astype(jnp.bfloat16)
    head_out = jnp.einsum(
        "lhqc,hcv->lqhv", latent_out, value_up, preferred_element_type=jnp.float32
    )
    head_out = jnp.where((pos[None, :] < leaf_length[:, None])[:, :, None, None], head_out, 0.0)
    head_out = head_out.astype(jnp.bfloat16).reshape(leaves * SEG_LEN, heads_dev, head_out.shape[3])
    partial_value = jnp.einsum(
        "thc,hcd->td",
        head_out,
        lax.all_gather(out_weight, "seg", axis=1, tiled=True),
        preferred_element_type=jnp.float32,
    )
    mixed = lax.psum_scatter(
        partial_value.astype(jnp.bfloat16), "head", scatter_dimension=1, tiled=True
    )
    return mixed


def solution(mesh):
    return jax.shard_map(
        per_device,
        mesh=mesh,
        in_specs=(
            P("seg", "head"),
            P("seg", None),
            P("seg", None),
            P(),
            P("seg"),
            P("seg"),
            P("head", None, None),
            P("head", "seg", None),
        ),
        out_specs=P("seg", "head"),
        check_vma=False,
    )
```

profile of v0, /device:TPU:68, one launch (start us, length us, event | category | flops | bytes accessed | tf_op | source)
XLA Modules:
  0.0 362.2 jit_solution(18240852740075958897)
XLA Ops:
  6.5 0.0 copy-start
  6.5 0.0 copy-start.1
  6.5 0.0 copy-start.3
  6.5 0.0 all-gather.3.cloned.1.call-start
  6.5 0.7 all-gather.3.cloned.1.call-update
  7.3 0.0 all-gather.5.cloned.1.call-start
  7.3 0.7 all-gather.5.cloned.1.call-update
  8.0 0.0 reduce-scatter.2.cloned.1.call-start
  8.1 1.7 copy.12
  11.1 0.0 copy-done.1
  11.1 0.2 copy.13
  11.3 0.0 copy-done.3
  11.3 22.6 %while.13 = (s32[]{:T(128)}, pred[1,16]{1,0:T(4,128)(4,1)S(1)}, s32[1]{0:T(128)}, s32[16]{0:T(128)S(1)}, s32[]{:T(128)}, /*index=5*/s32[]{:T(128)}, s32[1]{0:T(128)}, s32[1]{0:T(128)}) while((s32[]{:T(128)}, pred[1,16]{1,0:T(4,128)(4,1)S(1)}, s32[1]{0:T(128)}, s32[16]{0:T(128)S(1)}, s32[]{:T(128)}, /*index=5*/s32[]{:T(128)}, ...), condition=%wide.region_3.4_spmd.clone, body=%wide.region_1.3_spmd.clone.sunk | while | flops 100 | bytes 233 | solution.py:28
  11.3 0.7 fusion.44
  12.7 0.7 fusion.44
  14.1 0.7 fusion.44
  15.5 0.7 fusion.44
  16.9 0.7 fusion.44
  18.4 0.7 fusion.44
  19.8 0.7 fusion.44
  21.2 0.7 fusion.44
  22.6 0.7 fusion.44
  24.0 0.7 fusion.44
  25.4 0.7 fusion.44
  26.8 0.7 fusion.44
  28.3 0.7 fusion.44
  29.7 0.7 fusion.44
  31.1 0.7 fusion.44
  32.5 0.7 fusion.44
  33.9 0.1 fusion.30
  34.0 0.1 fusion.31
  34.1 0.4 fusion.37
  34.5 0.1 fusion.21
  34.6 17.3 %all-gather.3.cloned.1.call-done = bf16[2048,576]{0,1:T(8,128)(2,1)} async-done(((bf16[128,576]{0,1:T(8,128)(2,1)}), bf16[2048,576]{0,1:T(8,128)(2,1)}) %all-gather.3.cloned.1.call-update) | async-done | bytes 2359312 | tf_op jit(solution)/shard_map/all_gather | solution.py:65
  51.9 5.7 %bitcast_reduce_fusion = (f32[8,128]{1,0:T(8,128)S(1)}, f32[2048,128,8]{1,0,2:T(8,128)S(1)}) fusion(pred[2048]{0:T(1024)(128)(4,1)S(1)} %fusion.30, bf16[128,8,576]{0,2,1:T(8,128)(2,1)S(1)} %bitcast.95, bf16[2048,576]{0,1:T(8,128)(2,1)} %all-gather.3.cloned.1.call-done), kind=kOutput, calls=%fused_computation.7 | convolution fusion | flops 2422209536 | bytes 11933696 | tf_op jit(solution)/shard_map/lqhc,kc->lhqk/dot_general | solution.py:72
  57.6 0.0 copy-start.2
  57.6 2.0 fusion.5
  59.7 0.0 copy-done.2
  59.7 4.4 %fusion.8 = f32[8,128,512]{2,1,0:T(8,128)} fusion(f32[2048,128,8]{1,0,2:T(8,128)S(1)} %get-tuple-element.63, f32[8,128]{1,0:T(8,128)S(1)} %max.17, pred[2048]{0:T(1024)(128)(4,1)S(1)} %fusion.30, bf16[2048,576]{0,1:T(8,128)(2,1)S(1)} %copy-done.2), kind=kOutput, calls=%fused_computation.13 | convolution fusion | flops 2155872256 | bytes 12589056 | tf_op jit(solution)/shard_map/lhqk,kc->lhqc/dot_general | solution.py:78
  64.2 0.0 copy-done
  64.2 2.4 fusion.20
  66.5 71.9 %all-gather.5.cloned.1.call-done = bf16[8,128,7168]{2,1,0:T(8,128)(2,1)} async-done(((bf16[8,8,7168]{2,1,0:T(8,128)(2,1)}), bf16[8,128,7168]{2,1,0:T(8,128)(2,1)}) %all-gather.5.cloned.1.call-update) | async-done | bytes 14680080 | tf_op jit(solution)/shard_map/all_gather | solution.py:93
  138.4 12.2 %fusion.3 = bf16[128,7168]{0,1:T(8,128)(2,1)} fusion(bf16[128,8,128]{2,0,1:T(8,128)(2,1)S(1)} %fusion.20, bf16[8,128,7168]{2,1,0:T(8,128)(2,1)} %all-gather.5.cloned.1.call-done), kind=kOutput, calls=%fused_computation.5 | convolution fusion | flops 1879965696 | bytes 16777216 | tf_op jit(solution)/shard_map/thc,hcd->td/dot_general | solution.py:90
  150.7 0.0 reduce-scatter.2.cloned.1.call-update
  150.7 204.9 %reduce-scatter.2.cloned.1.call-done = bf16[128,448]{0,1:T(8,128)(2,1)} async-done(((bf16[128,7168]{0,1:T(8,128)(2,1)}), bf16[128,448]{0,1:T(8,128)(2,1)}) %reduce-scatter.2.cloned.1.call-update) | async-done | bytes 114704 | tf_op jit(solution)/shard_map/reduce_scatter | solution.py:96
  (21 shorter events, 0.3 us)
Async XLA Ops:
  6.5 57.6 %copy-start = (bf16[8,512,128]{2,1,0:T(8,128)(2,1)S(1)}, bf16[8,512,128]{2,1,0:T(8,128)(2,1)}, u32[]{:S(2)}) copy-start(bf16[8,512,128]{2,1,0:T(8,128)(2,1)} %param.16) | copy-start | bytes 3145732
  6.5 4.5 %copy-start.1 = (bf16[128,576]{0,1:T(8,128)(2,1)S(1)}, bf16[128,576]{0,1:T(8,128)(2,1)}, u32[]{:S(2)}) copy-start(bf16[128,576]{0,1:T(8,128)(2,1)} %param.11) | copy-start | bytes 442372
  6.5 4.7 %copy-start.3 = (s32[16]{0:T(128)S(1)}, s32[16]{0:T(128)}, u32[]{:S(2)}) copy-start(s32[16]{0:T(128)} %param.13) | copy-start | bytes 196
  6.5 45.4 %all-gather.3.cloned.1.call-start = ((), (), s32[]{:S(2)}) async-start(), calls=%async_computation.1 | async-start | bytes 2506752 | tf_op jit(solution)/shard_map/all_gather | solution.py:65
  7.3 131.2 %all-gather.5.cloned.1.call-start = ((), (), s32[]{:S(2)}) async-start(), calls=%async_computation.2 | async-start | bytes 15597568 | tf_op jit(solution)/shard_map/all_gather | solution.py:93
  8.0 347.6 %reduce-scatter.2.cloned.1.call-start = ((), (), s32[]{:S(2)}) async-start(), calls=%async_computation.3 | async-start | bytes 1949696 | tf_op jit(solution)/shard_map/reduce_scatter | solution.py:96
  57.6 2.1 copy-start.2
Sparse Core Ops, SparseCore 0:
  9.1 42.7 all-gather.2
  53.7 84.6 all-gather.4
  150.8 204.7 reduce-scatter.1
where the time goes:
time: 366 us; the launch traced here: 362 us
  waiting for transfers between devices  296 us (81%)
  matrix products  25.1 us (7%)
  between operations  14.5 us (4%)
  other arithmetic  13.7 us (4%)
  loops' own time  11.2 us (3%)
    reduce_scatter x1, waiting for transfers between devices, per_device(): lax.psum_scatter(partial_value.astype(jnp.bfloat16), 'head', scatter_dime...  205 us
    all_gather x1, waiting for transfers between devices, per_device(): lax.all_gather(out_weight, 'seg', axis=1, tiled=True)  71.9 us
    all_gather x1, waiting for transfers between devices, per_device(): piece = lax.all_gather(ancestor_latent, 'seg', axis=0, tiled=True)  17.3 us
    dot_general x1, matrix products, per_device(): jnp.einsum('thc,hcd->td', head_out, lax.all_gather(out_weight, 'seg', axi...  12.2 us
    another operation x1, loops' own time, chains(): marked, current = lax.fori_loop(0, count, advance, (marked, start))  11.2 us
    reduce_sum x16, other arithmetic, advance(): nxt = jnp.sum(jnp.where(match, parents[None, :], 0), axis=1)  11.2 us
  transfers between devices with their start and end apart: 3, of which 3 were waited for; matrix products, arithmetic and copies ran while one was open for 8% of the time, Pallas kernels for 0%

commit v1 on v0

v1 whole, which is shorter than its diff:
```python
import itertools

import jax
import jax.numpy as jnp
from jax import lax
from jax.experimental import pallas as pl
from jax.experimental.pallas import tpu as pltpu
from jax.sharding import PartitionSpec as P

LATENT = 512
ROPE = 64
WIDTH = LATENT + ROPE
NOPE = 128
SEG_LEN = 128
VHEAD = 128
HEADS_DEV = 8
ROWS = HEADS_DEV * SEG_LEN
ANC_SEGS = 16
COLS = 448

NEG = -1e30
LOG2E = 1.4426950408889634
SCALE = (NOPE + ROPE) ** -0.5


def seg_of(y, xl, c):
    return y * 4 + xl * 2 + c


def move(x, to):
    pairs = []
    for y, xl, c, z, xh in itertools.product(range(4), range(2), range(2), range(8), range(2)):
        ty, txl, tc, tz, txh = to(y, xl, c, z, xh)
        pairs.append((seg_of(y, xl, c) * 16 + z * 2 + xh, seg_of(ty, txl, tc) * 16 + tz * 2 + txh))
    return lax.ppermute(x, ("seg", "head"), pairs)


def swap_core(x):
    return move(x, lambda y, xl, c, z, xh: (y, xl, 1 - c, z, xh))


def swap_x(x, a, b):
    return move(x, lambda y, xl, c, z, xh: (y, xl ^ a, c, z, xh ^ b))


def from_y(x, r):
    return move(x, lambda y, xl, c, z, xh: ((y - r) % 4, xl, c, z, xh))


def to_z(x, k):
    return move(x, lambda y, xl, c, z, xh: (y, xl, c, (z + k) % 8, xh))


def to_owner(x):
    return move(x, lambda y, xl, c, z, xh: (y, z >> 2, (z >> 1) & 1, xl * 4 + c * 2 + xh, z & 1))


def attention_kernel(meta, q_ref, own_ref, *refs):
    anc_refs = refs[:8]
    up_ref, out_ref, keys, scores, top, total, accum, where_ref = refs[8:]
    y, xl, c = meta[18], meta[19], meta[20]
    length = meta[17]

    for slot in range(ANC_SEGS):
        where_ref[slot] = -1

    def walk(step, state):
        count, current = state
        valid = current >= 0

        @pl.when(valid)
        def _():
            rel_y = lax.bitwise_and((current >> 2) - y + 4, 3)
            rel_x = lax.bitwise_xor(lax.bitwise_and(current >> 1, 1), xl)
            rel_c = lax.bitwise_xor(lax.bitwise_and(current, 1), c)
            where_ref[rel_c * 8 + rel_y * 2 + rel_x] = count

        following = meta[jnp.maximum(current, 0)]
        return (jnp.where(valid, count + 1, count), jnp.where(valid, following, -1))

    end, _ = lax.fori_loop(0, ANC_SEGS, walk, (jnp.int32(1), meta[16]))

    keys[0] = own_ref[...]
    keys[end] = own_ref[...]
    for slot in range(ANC_SEGS):
        place = where_ref[slot]

        @pl.when(place >= 0)
        def _(slot=slot, place=place):
            keys[place] = anc_refs[slot // 2][slot % 2]

    pairs = (end + 1) // 2

    def score(j):
        pair = jnp.concatenate([keys[2 * j], keys[2 * j + 1]], axis=1)
        s = jnp.dot(q_ref[...], pair, preferred_element_type=jnp.float32)
        return s[:, :SEG_LEN], s[:, SEG_LEN:]

    row = lax.broadcasted_iota(jnp.int32, (ROWS, SEG_LEN), 0) & (SEG_LEN - 1)
    col = lax.broadcasted_iota(jnp.int32, (ROWS, SEG_LEN), 1)
    left, right = score(0)
    left = jnp.where((col <= row) & (col < length), left, NEG)
    scores[0, :, :SEG_LEN] = left
    scores[0, :, SEG_LEN:] = right
    top[...] = jnp.maximum(left, right)

    def first(j, carry):
        left, right = score(j)
        right = jnp.where(2 * j + 1 < end, right, NEG)
        scores[j, :, :SEG_LEN] = left
        scores[j, :, SEG_LEN:] = right
        top[...] = jnp.maximum(top[...], jnp.maximum(left, right))
        return carry

    lax.fori_loop(1, pairs, first, 0)
    factor = SCALE * LOG2E
    high = jnp.max(top[...], axis=1, keepdims=True)
    top[...] = jnp.broadcast_to(high, (ROWS, SEG_LEN))
    total[...] = jnp.zeros_like(total)
    accum[...] = jnp.zeros_like(accum)

    def second(j, carry):
        high = top[...]
        left = jnp.exp2((scores[j, :, :SEG_LEN] - high) * factor)
        right = jnp.exp2((scores[j, :, SEG_LEN:] - high) * factor)
        total[...] += left + right
        weight = jnp.concatenate([left, right], axis=1).astype(jnp.bfloat16)
        pair = jnp.concatenate([keys[2 * j, :LATENT], keys[2 * j + 1, :LATENT]], axis=1)
        accum[...] += lax.dot_general(
            weight, pair, (((1,), (1,)), ((), ())), preferred_element_type=jnp.float32
        )
        return carry

    lax.fori_loop(0, pairs, second, 0)
    pos = lax.broadcasted_iota(jnp.int32, (SEG_LEN, VHEAD), 0)
    for h in range(HEADS_DEV):
        rows = slice(h * SEG_LEN, (h + 1) * SEG_LEN)
        denominator = jnp.sum(total[rows], axis=1, keepdims=True)
        latent_out = (accum[rows] / denominator).astype(jnp.bfloat16)
        head_out = jnp.dot(latent_out, up_ref[h], preferred_element_type=jnp.float32)
        head_out = jnp.where(pos < length, head_out, 0.0).astype(jnp.bfloat16)
        for block in range(4):
            rel = lax.bitwise_and(block - y + 4, 3)
            out_ref[rel, :, h * 32 : (h + 1) * 32] = head_out[:, block * 32 : (block + 1) * 32]


def attention(meta, q, own, anc, up):
    vmem = pl.BlockSpec(memory_space=pltpu.VMEM)
    return pl.pallas_call(
        attention_kernel,
        out_shape=jax.ShapeDtypeStruct((4, SEG_LEN, 256), jnp.bfloat16),
        in_specs=[pl.BlockSpec(memory_space=pltpu.SMEM)] + [vmem] * 11,
        out_specs=vmem,
        scratch_shapes=[
            pltpu.VMEM((ANC_SEGS + 2, WIDTH, SEG_LEN), jnp.bfloat16),
            pltpu.VMEM((9, ROWS, 2 * SEG_LEN), jnp.float32),
            pltpu.VMEM((ROWS, SEG_LEN), jnp.float32),
            pltpu.VMEM((ROWS, SEG_LEN), jnp.float32),
            pltpu.VMEM((ROWS, LATENT), jnp.float32),
            pltpu.SMEM((ANC_SEGS,), jnp.int32),
        ],
        compiler_params=pltpu.CompilerParams(vmem_limit_bytes=48 * 2**20),
        cost_estimate=pl.CostEstimate(
            flops=4 * 10**9, bytes_accessed=6 * 2**20, transcendentals=2 * 10**6
        ),
        name="attention",
    )(meta, q, own, *anc, up)


def project_kernel(meta, *refs):
    heads = refs[:8]
    w0, w1, w3, w2a, w2b = refs[8:13]
    outs = refs[13:21]
    left, partial = refs[21:]
    xl, c, z = meta[19], meta[20], meta[21]
    weights = [[w0.at[0], w1.at[0], w2a, w3.at[0]], [w0.at[1], w1.at[1], w2b, w3.at[1]]]
    for b in range(2):
        for t in range(4):
            for r in range(4):
                left[t * SEG_LEN : (t + 1) * SEG_LEN, b * 1024 + r * 256 : b * 1024 + r * 256 + 256] = heads[t * 2 + b][r]
    for n in range(7):
        cols = slice(n * 128, (n + 1) * 128)
        value = None
        for b in range(2):
            for r in range(4):
                term = jnp.dot(
                    left[:, b * 1024 + r * 256 : b * 1024 + r * 256 + 256],
                    weights[b][r][:, cols],
                    preferred_element_type=jnp.float32,
                )
                value = term if value is None else value + term
        for t in range(4):
            partial[t, cols] = value[t * SEG_LEN : (t + 1) * SEG_LEN].T.astype(jnp.bfloat16)
    for k in range(8):
        target = lax.bitwise_and(z + k, 7)
        t = lax.bitwise_xor(target >> 2, xl) * 2 + lax.bitwise_xor(lax.bitwise_and(target >> 1, 1), c)
        half = lax.bitwise_and(target, 1)

        @pl.when(half == 0)
        def _(k=k, t=t):
            outs[k][...] = partial[t, :COLS]

        @pl.when(half == 1)
        def _(k=k, t=t):
            outs[k][...] = partial[t, COLS:]


def project(meta, heads, weights):
    vmem = pl.BlockSpec(memory_space=pltpu.VMEM)
    return pl.pallas_call(
        project_kernel,
        out_shape=[jax.ShapeDtypeStruct((COLS, SEG_LEN), jnp.bfloat16)] * 8,
        in_specs=[pl.BlockSpec(memory_space=pltpu.SMEM)] + [vmem] * 13,
        out_specs=[vmem] * 8,
        scratch_shapes=[
            pltpu.VMEM((4 * SEG_LEN, 2048), jnp.bfloat16),
            pltpu.VMEM((4, 2 * COLS, SEG_LEN), jnp.bfloat16),
        ],
        compiler_params=pltpu.CompilerParams(vmem_limit_bytes=48 * 2**20),
        cost_estimate=pl.CostEstimate(
            flops=2 * 10**9, bytes_accessed=8 * 2**20, transcendentals=0
        ),
        name="project",
    )(meta, *heads, *weights)


def per_device(
    queries,
    leaf_latent,
    ancestor_latent,
    ancestor_parent,
    leaf_parent,
    leaf_length,
    value_up,
    out_weight,
):
    seg, head = lax.axis_index("seg"), lax.axis_index("head")
    y, xl, c = seg // 4, (seg // 2) % 2, seg % 2
    z, xh = head // 2, head % 2
    place = jnp.stack([y, xl, c, z, xh]).astype(jnp.int32)
    meta = jnp.concatenate([ancestor_parent, leaf_parent, leaf_length, place])

    mine = ancestor_latent.T
    column = jnp.stack([mine, swap_x(mine, 1, 0)])
    anc = [column] + [from_y(column, r) for r in (1, 2, 3)]
    anc = anc + [swap_core(x) for x in anc]

    blocks = out_weight.reshape(HEADS_DEV, 8, 2, 2, 2, 2 * COLS).transpose(3, 2, 4, 0, 1, 5)
    keep = lax.dynamic_index_in_dim(blocks, c, 0, keepdims=False)
    other = swap_core(lax.dynamic_index_in_dim(blocks, 1 - c, 0, keepdims=False))
    cores = jnp.where(c == 0, jnp.stack([keep, other], 3), jnp.stack([other, keep], 3))

    def for_x(a, b):
        part = lax.dynamic_index_in_dim(cores, xl ^ a, 0, keepdims=False)
        part = lax.dynamic_index_in_dim(part, xh ^ b, 0, keepdims=False)
        return swap_x(part, a, b) if a or b else part

    rows = []
    for b in range(2):
        near, far = for_x(0, b), for_x(1, b)
        rows.append(jnp.where(xl == 0, jnp.stack([near, far], 1), jnp.stack([far, near], 1)))
    w0 = jnp.stack(rows).reshape(2, 256, 2 * COLS)
    w1, w3 = from_y(w0, 1), from_y(w0, 3)
    w2a, w2b = from_y(w1[0], 1), from_y(w3[1], 3)

    q = queries.reshape(SEG_LEN, HEADS_DEV, WIDTH).transpose(1, 0, 2).reshape(ROWS, WIDTH)
    head_out = attention(meta, q, leaf_latent.T, anc, value_up)

    heads = []
    for a in range(2):
        row = [head_out if not (a or b) else swap_x(head_out, a, b) for b in range(2)]
        heads += row + [swap_core(x) for x in row]
    parts = project(meta, heads, (w0, w1, w3, w2a, w2b))
    summed = parts[0].astype(jnp.float32)
    for k in range(1, 8):
        summed = summed + to_z(parts[k], k).astype(jnp.float32)
    return to_owner(summed.astype(jnp.bfloat16)).T


def solution(mesh):
    return jax.shard_map(
        per_device,
        mesh=mesh,
        in_specs=(
            P("seg", "head"),
            P("seg", None),
            P("seg", None),
            P(),
            P("seg"),
            P("seg"),
            P("head", None, None),
            P("head", "seg", None),
        ),
        out_specs=P("seg", "head"),
        check_vma=False,
    )
```

time: 366 us -> 121 us (0.33)
  the two profiles are of different devices: /device:TPU:68 before, /device:TPU:34 now
where the time goes in v1:
time: 121 us; the launch traced here: 119 us
  waiting for transfers between devices  49.6 us (41%)
  starting transfers between devices  42.3 us (35%)
  Pallas kernels  15.1 us (12%)
  local copies, waits for them, and re-layouts  10.3 us (9%)
  between operations  1.52 us (1%)
    ppermute x31, waiting for transfers between devices, move(): return lax.ppermute(x, ('seg', 'head'), pairs)  49.6 us
    ppermute x31, starting transfers between devices, move(): return lax.ppermute(x, ('seg', 'head'), pairs)  42.3 us
    pallas_call x1, Pallas kernels, attention(): pl.pallas_call(attention_kernel, out_shape=jax.ShapeDtypeStruct((4, SEG_L...  9.73 us
    unnamed x16, local copies, waits for them, and re-layouts  5.92 us
    pallas_call x1, Pallas kernels, project(): pl.pallas_call(project_kernel, out_shape=[jax.ShapeDtypeStruct((COLS, SEG...  5.38 us
  transfers between devices with their start and end apart: 31, of which 19 were waited for; matrix products, arithmetic and copies ran while one was open for 4% of the time, Pallas kernels for 8%

profile of v1, /device:TPU:34, one launch (start us, length us, event | category | flops | bytes accessed | tf_op | source)
XLA Modules:
  0.0 119.4 jit_solution(18391319895280861264)
XLA Ops:
  0.0 1.3 %dynamic-slice_bitcast_fusion.1 = (bf16[2,2,8,1,8,896]{5,4,1,0,2,3:T(8,128)(2,1)S(1)}, bf16[2,2,8,8,896]{4,3,1,0,2:T(8,128)(2,1)S(1)}) fusion(bf16[8,8,2,2,2,896]{5,1,4,3,2,0:T(8,128)(2,1)} %bitcast.53, s32[]{:T(128)S(6)} %select_n.108, s32[]{:T(128)S(6)} %select_n.109), kind=kLoop, calls=%fused_computation.7 | loop fusion | bytes 1835016 | tf_op jit(solution)/shard_map/stack | solution.py:251
  1.4 0.6 collective-permute-start
  2.0 1.2 collective-permute-done.15
  3.5 1.6 %collective-permute-start.18 = (bf16[8,2,8,896]{3,2,1,0:T(8,128)(2,1)S(1)}, bf16[8,2,8,896]{3,2,1,0:T(8,128)(2,1)S(1)}, u32[]{:S(2)}, u32[]{:S(2)}) collective-permute-start(bf16[8,2,8,896]{3,2,1,0:T(8,128)(2,1)S(1)} %bitcast.58), channel_id=1, source_target_pairs={{0,33},{1,32},{2,35},{3,34},{4,37},{5,36},{6,39},{7,38},{8,41},{9,... | collective-permute-start | bytes 688136 | tf_op jit(solution)/shard_map/ppermute | solution.py:35
  5.1 1.2 %collective-permute-start.17 = (bf16[8,2,8,896]{3,2,1,0:T(8,128)(2,1)S(1)}, bf16[8,2,8,896]{3,2,1,0:T(8,128)(2,1)S(1)}, u32[]{:S(2)}, u32[]{:S(2)}) collective-permute-start(bf16[8,2,8,896]{3,2,1,0:T(8,128)(2,1)S(1)} %bitcast.57), channel_id=1, source_target_pairs={{0,1},{1,0},{2,3},{3,2},{4,5},{5,4},{6,7},{7,6},{8,9},{9,8},{10,11... | collective-permute-start | bytes 688136 | tf_op jit(solution)/shard_map/ppermute | solution.py:35
  6.3 1.6 %collective-permute-start.16 = (bf16[8,2,8,896]{3,2,1,0:T(8,128)(2,1)S(1)}, bf16[8,2,8,896]{3,2,1,0:T(8,128)(2,1)S(1)}, u32[]{:S(2)}, u32[]{:S(2)}) collective-permute-start(bf16[8,2,8,896]{3,2,1,0:T(8,128)(2,1)S(1)} %bitcast.56), channel_id=1, source_target_pairs={{0,32},{1,33},{2,34},{3,35},{4,36},{5,37},{6,38},{7,39},{8,40},{9,... | collective-permute-start | bytes 688136 | tf_op jit(solution)/shard_map/ppermute | solution.py:35
  7.9 3.1 %collective-permute-start.1 = (bf16[2,576,128]{2,1,0:T(8,128)(2,1)S(1)}, bf16[2,576,128]{2,1,0:T(8,128)(2,1)}, u32[]{:S(2)}, u32[]{:S(2)}) collective-permute-start(bf16[2,576,128]{2,1,0:T(8,128)(2,1)S(1)} %pad_maximum_fusion.1.refs_0_), channel_id=1, source_target_pairs={{0,192},{1,193},{2,194},{3,195},{4,196},{5,197},{6,198},{7,199},{8... | collective-permute-start | bytes 884744 | tf_op jit(solution)/shard_map/ppermute | solution.py:35
  11.0 0.6 collective-permute-start.2
  11.7 4.5 %collective-permute-done.18 = bf16[8,2,8,896]{3,2,1,0:T(8,128)(2,1)S(1)} collective-permute-done((bf16[8,2,8,896]{3,2,1,0:T(8,128)(2,1)S(1)}, bf16[8,2,8,896]{3,2,1,0:T(8,128)(2,1)S(1)}, u32[]{:S(2)}, u32[]{:S(2)}) %collective-permute-start.18) | collective-permute-done | bytes 229408 | tf_op jit(solution)/shard_map/ppermute | solution.py:35
  16.1 1.6 %collective-permute-start.3 = (bf16[2,576,128]{2,1,0:T(8,128)(2,1)S(1)}, bf16[2,576,128]{2,1,0:T(8,128)(2,1)}, u32[]{:S(2)}, u32[]{:S(2)}) collective-permute-start(bf16[2,576,128]{2,1,0:T(8,128)(2,1)S(1)} %pad_maximum_fusion.1.refs_0_), channel_id=1, source_target_pairs={{0,64},{1,65},{2,66},{3,67},{4,68},{5,69},{6,70},{7,71},{8,72},{9,... | collective-permute-start | bytes 884744 | tf_op jit(solution)/shard_map/ppermute | solution.py:35
  18.3 3.1 %collective-permute-start.19 = (bf16[2,256,896]{2,1,0:T(8,128)(2,1)S(1)}, bf16[2,256,896]{2,1,0:T(8,128)(2,1)S(1)}, u32[]{:S(2)}, u32[]{:S(2)}) collective-permute-start(bf16[2,256,896]{2,1,0:T(8,128)(2,1)S(1)} %pad_maximum_fusion.refs_8_), channel_id=1, source_target_pairs={{0,192},{1,193},{2,194},{3,195},{4,196},{5,197},{6,198},{7,199},{8... | collective-permute-start | bytes 2752520 | tf_op jit(solution)/shard_map/ppermute | solution.py:35
  21.4 2.9 %collective-permute-done.1.refs_1_ = bf16[2,576,128]{2,1,0:T(8,128)(2,1)} collective-permute-done((bf16[2,576,128]{2,1,0:T(8,128)(2,1)S(1)}, bf16[2,576,128]{2,1,0:T(8,128)(2,1)}, u32[]{:S(2)}, u32[]{:S(2)}) %collective-permute-start.1) | collective-permute-done | bytes 294944 | tf_op jit(solution)/shard_map/ppermute | solution.py:35
  24.3 0.5 collective-permute-start.6
  24.8 2.2 %collective-permute-done.3.refs_3_ = bf16[2,576,128]{2,1,0:T(8,128)(2,1)} collective-permute-done((bf16[2,576,128]{2,1,0:T(8,128)(2,1)S(1)}, bf16[2,576,128]{2,1,0:T(8,128)(2,1)}, u32[]{:S(2)}, u32[]{:S(2)}) %collective-permute-start.3) | collective-permute-done | bytes 294944 | tf_op jit(solution)/shard_map/ppermute | solution.py:35
  27.0 0.7 copy-done.1
  27.7 0.5 collective-permute-start.20
  29.5 1.4 %copy.15 = bf16[128,4608]{0,1:T(8,128)(2,1)} copy(bf16[128,4608]{1,0:T(8,128)(2,1)S(1)} %copy-done.4) | data formatting | bytes 2359296 | tf_op args[0]
  31.0 1.7 %copy.16 = bf16[8,128,576]{2,1,0:T(8,128)(2,1)S(1)} copy(bf16[8,128,576]{1,2,0:T(8,128)(2,1)} %bitcast.50) | data formatting | bytes 2359296 | tf_op jit(solution)/shard_map/transpose | solution.py:266
  32.8 1.2 %copy-done = bf16[8,512,128]{2,1,0:T(8,128)(2,1)S(1)} copy-done((bf16[8,512,128]{2,1,0:T(8,128)(2,1)S(1)}, bf16[8,512,128]{2,1,0:T(8,128)(2,1)}, u32[]{:S(2)}) %copy-start) | copy-done | bytes 1048600
  34.1 1.0 copy-done.2
  35.0 0.9 copy-done.3
  35.9 9.7 %attention.1.refs_0_ = bf16[4,128,256]{2,1,0:T(8,128)(2,1)S(1)} custom-call(s32[23]{0:T(128)S(1)} %concatenate.8.meta, bf16[1024,576]{1,0:T(8,128)(2,1)S(1)} %bitcast.48, bf16[576,128]{1,0:T(8,128)(2,1)S(1)} %bitcast.49, bf16[2,576,128]{2,1,0:T(8,128)(2,1)S(1)} %pad_maximum_fusion.1.refs_0_, bf16[2,576,128]{2,1,0:T(8,128)(2,1)} %collective-permute-done.1.refs_1_, ...), custom_call_target="tpu_custom_call" | custom-call | flops 4000000000 | bytes 6291456 | tf_op jit(solution)/shard_map/attention/pallas_call | solution.py:149
  45.7 2.1 %collective-permute-start.8 = (bf16[4,128,256]{2,1,0:T(8,128)(2,1)S(1)}, bf16[4,128,256]{2,1,0:T(8,128)(2,1)S(1)}, u32[]{:S(2)}, u32[]{:S(2)}) collective-permute-start(bf16[4,128,256]{2,1,0:T(8,128)(2,1)S(1)} %attention.1.refs_0_), channel_id=1, source_target_pairs={{0,1},{1,0},{2,3},{3,2},{4,5},{5,4},{6,7},{7,6},{8,9},{9,8},{10,11... | collective-permute-start | bytes 786440 | tf_op jit(solution)/shard_map/ppermute | solution.py:35
  47.9 1.5 %collective-permute-start.11 = (bf16[4,128,256]{2,1,0:T(8,128)(2,1)S(1)}, bf16[4,128,256]{2,1,0:T(8,128)(2,1)S(1)}, u32[]{:S(2)}, u32[]{:S(2)}) collective-permute-start(bf16[4,128,256]{2,1,0:T(8,128)(2,1)S(1)} %attention.1.refs_0_), channel_id=1, source_target_pairs={{0,32},{1,33},{2,34},{3,35},{4,36},{5,37},{6,38},{7,39},{8,40},{9,... | collective-permute-start | bytes 786440 | tf_op jit(solution)/shard_map/ppermute | solution.py:35
  49.3 0.5 collective-permute-start.12
  49.9 1.9 %collective-permute-done.20.refs_10_ = bf16[2,256,896]{2,1,0:T(8,128)(2,1)} collective-permute-done((bf16[2,256,896]{2,1,0:T(8,128)(2,1)S(1)}, bf16[2,256,896]{2,1,0:T(8,128)(2,1)}, u32[]{:S(2)}, u32[]{:S(2)}) %collective-permute-start.20) | collective-permute-done | bytes 917536 | tf_op jit(solution)/shard_map/ppermute | solution.py:35
  51.8 0.9 collective-permute-start.21
  52.7 1.1 slice_bitcast_fusion
  53.8 2.7 %collective-permute-done.8.refs_1_ = bf16[4,128,256]{2,1,0:T(8,128)(2,1)S(1)} collective-permute-done((bf16[4,128,256]{2,1,0:T(8,128)(2,1)S(1)}, bf16[4,128,256]{2,1,0:T(8,128)(2,1)S(1)}, u32[]{:S(2)}, u32[]{:S(2)}) %collective-permute-start.8) | collective-permute-done | bytes 262176 | tf_op jit(solution)/shard_map/ppermute | solution.py:35
  56.5 3.5 %collective-permute-done.11.refs_4_ = bf16[4,128,256]{2,1,0:T(8,128)(2,1)S(1)} collective-permute-done((bf16[4,128,256]{2,1,0:T(8,128)(2,1)S(1)}, bf16[4,128,256]{2,1,0:T(8,128)(2,1)S(1)}, u32[]{:S(2)}, u32[]{:S(2)}) %collective-permute-start.11) | collective-permute-done | bytes 262176 | tf_op jit(solution)/shard_map/ppermute | solution.py:35
  60.0 1.1 collective-permute-done.12.refs_5_
  61.6 1.1 collective-permute-done.14.refs_7_
  62.7 1.3 %collective-permute-done.21.refs_11_ = bf16[256,896]{1,0:T(8,128)(2,1)S(1)} collective-permute-done((bf16[256,896]{1,0:T(8,128)(2,1)S(1)}, bf16[256,896]{1,0:T(8,128)(2,1)S(1)}, u32[]{:S(2)}, u32[]{:S(2)}) %collective-permute-start.21) | collective-permute-done | bytes 458784 | tf_op jit(solution)/shard_map/ppermute | solution.py:35
  63.9 4.6 %collective-permute-done.22.refs_12_ = bf16[256,896]{1,0:T(8,128)(2,1)S(1)} collective-permute-done((bf16[256,896]{1,0:T(8,128)(2,1)S(1)}, bf16[256,896]{1,0:T(8,128)(2,1)S(1)}, u32[]{:S(2)}, u32[]{:S(2)}) %collective-permute-start.22) | collective-permute-done | bytes 458784 | tf_op jit(solution)/shard_map/ppermute | solution.py:35
  68.6 5.4 %project.1 = (bf16[448,128]{1,0:T(8,128)(2,1)S(1)}, bf16[448,128]{1,0:T(8,128)(2,1)S(1)}, bf16[448,128]{1,0:T(8,128)(2,1)S(1)}, bf16[448,128]{1,0:T(8,128)(2,1)S...) custom-call(s32[23]{0:T(128)S(1)} %concatenate.8.meta, ...), custom_call_target="tpu_custom_call" | custom-call | flops 2000000000 | bytes 8388608 | tf_op jit(solution)/shard_map/project/pallas_call | solution.py:210
  74.2 6.3 %collective-permute-start.28 = (bf16[448,128]{1,0:T(8,128)(2,1)S(1)}, bf16[448,128]{1,0:T(8,128)(2,1)S(1)}, u32[]{:S(2)}, u32[]{:S(2)}) collective-permute-start(bf16[448,128]{1,0:T(8,128)(2,1)S(1)} %get-tuple-element.19), channel_id=1, source_target_pairs={{0,12},{1,13},{2,14},{3,15},{4,0},{5,1},{6,2},{7,3},{8,4},{9,5},{1... | collective-permute-start | bytes 344072 | tf_op jit(solution)/shard_map/ppermute | solution.py:35
  80.5 1.0 collective-permute-start.27
  81.4 4.5 %collective-permute-start.26 = (bf16[448,128]{1,0:T(8,128)(2,1)S(1)}, bf16[448,128]{1,0:T(8,128)(2,1)S(1)}, u32[]{:S(2)}, u32[]{:S(2)}) collective-permute-start(bf16[448,128]{1,0:T(8,128)(2,1)S(1)} %get-tuple-element.17), channel_id=1, source_target_pairs={{0,8},{1,9},{2,10},{3,11},{4,12},{5,13},{6,14},{7,15},{8,0},{9,1},... | collective-permute-start | bytes 344072 | tf_op jit(solution)/shard_map/ppermute | solution.py:35
  86.4 2.9 %collective-permute-start.24 = (bf16[448,128]{1,0:T(8,128)(2,1)S(1)}, bf16[448,128]{1,0:T(8,128)(2,1)S(1)}, u32[]{:S(2)}, u32[]{:S(2)}) collective-permute-start(bf16[448,128]{1,0:T(8,128)(2,1)S(1)} %get-tuple-element.15), channel_id=1, source_target_pairs={{0,4},{1,5},{2,6},{3,7},{4,8},{5,9},{6,10},{7,11},{8,12},{9,13},{1... | collective-permute-start | bytes 344072 | tf_op jit(solution)/shard_map/ppermute | solution.py:35
  89.3 1.0 collective-permute-start.23
  90.3 3.5 %collective-permute-done.27 = bf16[448,128]{1,0:T(8,128)(2,1)S(1)} collective-permute-done((bf16[448,128]{1,0:T(8,128)(2,1)S(1)}, bf16[448,128]{1,0:T(8,128)(2,1)S(1)}, u32[]{:S(2)}, u32[]{:S(2)}) %collective-permute-start.27) | collective-permute-done | bytes 114720 | tf_op jit(solution)/shard_map/ppermute | solution.py:35
  93.8 5.6 %collective-permute-done.26 = bf16[448,128]{1,0:T(8,128)(2,1)S(1)} collective-permute-done((bf16[448,128]{1,0:T(8,128)(2,1)S(1)}, bf16[448,128]{1,0:T(8,128)(2,1)S(1)}, u32[]{:S(2)}, u32[]{:S(2)}) %collective-permute-start.26) | collective-permute-done | bytes 114720 | tf_op jit(solution)/shard_map/ppermute | solution.py:35
  99.5 0.5 collective-permute-done.25
  100.0 2.6 %collective-permute-done.24 = bf16[448,128]{1,0:T(8,128)(2,1)S(1)} collective-permute-done((bf16[448,128]{1,0:T(8,128)(2,1)S(1)}, bf16[448,128]{1,0:T(8,128)(2,1)S(1)}, u32[]{:S(2)}, u32[]{:S(2)}) %collective-permute-start.24) | collective-permute-done | bytes 114720 | tf_op jit(solution)/shard_map/ppermute | solution.py:35
  102.6 1.4 %collective-permute-done.23 = bf16[448,128]{1,0:T(8,128)(2,1)S(1)} collective-permute-done((bf16[448,128]{1,0:T(8,128)(2,1)S(1)}, bf16[448,128]{1,0:T(8,128)(2,1)S(1)}, u32[]{:S(2)}, u32[]{:S(2)}) %collective-permute-start.23) | collective-permute-done | bytes 114720 | tf_op jit(solution)/shard_map/ppermute | solution.py:35
  104.1 6.3 %collective-permute-start.30 = (bf16[448,128]{1,0:T(8,128)(2,1)S(1)}, bf16[448,128]{1,0:T(8,128)(2,1)S(1)}, u32[]{:S(2)}, u32[]{:S(2)}) collective-permute-start(bf16[448,128]{1,0:T(8,128)(2,1)S(1)} %add_convert_fusion), channel_id=1, source_target_pairs={{0,0},{1,2},{2,1},{3,3},{4,16},{5,18},{6,17},{7,19},{8,32},{9,34},... | collective-permute-start | bytes 344072 | tf_op jit(solution)/shard_map/ppermute | solution.py:35
  110.5 8.2 %collective-permute-done.30 = bf16[448,128]{1,0:T(8,128)(2,1)S(1)} collective-permute-done((bf16[448,128]{1,0:T(8,128)(2,1)S(1)}, bf16[448,128]{1,0:T(8,128)(2,1)S(1)}, u32[]{:S(2)}, u32[]{:S(2)}) %collective-permute-start.30) | collective-permute-done | bytes 114720 | tf_op jit(solution)/shard_map/ppermute | solution.py:35
  118.7 0.6 copy.34
  (48 shorter events, 2.4 us)
Async XLA Ops:
  0.0 1.4 %copy-start.5 = (bf16[128,576]{0,1:T(8,128)(2,1)S(1)}, bf16[128,576]{0,1:T(8,128)(2,1)}, u32[]{:S(2)}) copy-start(bf16[128,576]{0,1:T(8,128)(2,1)} %param.10) | copy-start | bytes 442372
  1.3 1.9 %collective-permute-start.15 = (bf16[2,2,8,8,896]{4,3,1,0,2:T(8,128)(2,1)S(1)}, bf16[2,2,8,8,896]{4,3,1,0,2:T(8,128)(2,1)S(1)}, u32[]{:S(2)}, u32[]{:S(2)}) collective-permute-start(bf16[2,2,8,8,896]{4,3,1,0,2:T(8,128)(2,1)S(1)} %get-tuple-element.26), channel_id=1, source_target_pairs={{0,16},{1,17},{2,18},{3,19},{4,20},{5,21},{6,22},{7,23},{8,24},{9,... | collective-permute-start | bytes 1376264 | tf_op jit(solution)/shard_map/ppermute | solution.py:35
  1.4 6.5 %collective-permute-start = (bf16[576,128]{1,0:T(8,128)(2,1)S(1)}, bf16[576,128]{1,0:T(8,128)(2,1)S(1)}, u32[]{:S(2)}, u32[]{:S(2)}) collective-permute-start(bf16[576,128]{1,0:T(8,128)(2,1)S(1)} %bitcast.62), channel_id=1, source_target_pairs={{0,32},{1,33},{2,34},{3,35},{4,36},{5,37},{6,38},{7,39},{8,40},{9,... | collective-permute-start | bytes 442376 | tf_op jit(solution)/shard_map/ppermute | solution.py:35
  3.5 12.6 %collective-permute-start.18 = (bf16[8,2,8,896]{3,2,1,0:T(8,128)(2,1)S(1)}, bf16[8,2,8,896]{3,2,1,0:T(8,128)(2,1)S(1)}, u32[]{:S(2)}, u32[]{:S(2)}) collective-permute-start(bf16[8,2,8,896]{3,2,1,0:T(8,128)(2,1)S(1)} %bitcast.58), channel_id=1, source_target_pairs={{0,33},{1,32},{2,35},{3,34},{4,37},{5,36},{6,39},{7,38},{8,41},{9,... | collective-permute-start | bytes 688136 | tf_op jit(solution)/shard_map/ppermute | solution.py:35
  5.1 12.6 %collective-permute-start.17 = (bf16[8,2,8,896]{3,2,1,0:T(8,128)(2,1)S(1)}, bf16[8,2,8,896]{3,2,1,0:T(8,128)(2,1)S(1)}, u32[]{:S(2)}, u32[]{:S(2)}) collective-permute-start(bf16[8,2,8,896]{3,2,1,0:T(8,128)(2,1)S(1)} %bitcast.57), channel_id=1, source_target_pairs={{0,1},{1,0},{2,3},{3,2},{4,5},{5,4},{6,7},{7,6},{8,9},{9,8},{10,11... | collective-permute-start | bytes 688136 | tf_op jit(solution)/shard_map/ppermute | solution.py:35
  6.3 11.8 %collective-permute-start.16 = (bf16[8,2,8,896]{3,2,1,0:T(8,128)(2,1)S(1)}, bf16[8,2,8,896]{3,2,1,0:T(8,128)(2,1)S(1)}, u32[]{:S(2)}, u32[]{:S(2)}) collective-permute-start(bf16[8,2,8,896]{3,2,1,0:T(8,128)(2,1)S(1)} %bitcast.56), channel_id=1, source_target_pairs={{0,32},{1,33},{2,34},{3,35},{4,36},{5,37},{6,38},{7,39},{8,40},{9,... | collective-permute-start | bytes 688136 | tf_op jit(solution)/shard_map/ppermute | solution.py:35
  7.9 16.3 %collective-permute-start.1 = (bf16[2,576,128]{2,1,0:T(8,128)(2,1)S(1)}, bf16[2,576,128]{2,1,0:T(8,128)(2,1)}, u32[]{:S(2)}, u32[]{:S(2)}) collective-permute-start(bf16[2,576,128]{2,1,0:T(8,128)(2,1)S(1)} %pad_maximum_fusion.1.refs_0_), channel_id=1, source_target_pairs={{0,192},{1,193},{2,194},{3,195},{4,196},{5,197},{6,198},{7,199},{8... | collective-permute-start | bytes 884744 | tf_op jit(solution)/shard_map/ppermute | solution.py:35
  11.0 13.3 %collective-permute-start.2 = (bf16[2,576,128]{2,1,0:T(8,128)(2,1)S(1)}, bf16[2,576,128]{2,1,0:T(8,128)(2,1)}, u32[]{:S(2)}, u32[]{:S(2)}) collective-permute-start(bf16[2,576,128]{2,1,0:T(8,128)(2,1)S(1)} %pad_maximum_fusion.1.refs_0_), channel_id=1, source_target_pairs={{0,128},{1,129},{2,130},{3,131},{4,132},{5,133},{6,134},{7,135},{8... | collective-permute-start | bytes 884744 | tf_op jit(solution)/shard_map/ppermute | solution.py:35
  16.1 10.8 %collective-permute-start.3 = (bf16[2,576,128]{2,1,0:T(8,128)(2,1)S(1)}, bf16[2,576,128]{2,1,0:T(8,128)(2,1)}, u32[]{:S(2)}, u32[]{:S(2)}) collective-permute-start(bf16[2,576,128]{2,1,0:T(8,128)(2,1)S(1)} %pad_maximum_fusion.1.refs_0_), channel_id=1, source_target_pairs={{0,64},{1,65},{2,66},{3,67},{4,68},{5,69},{6,70},{7,71},{8,72},{9,... | collective-permute-start | bytes 884744 | tf_op jit(solution)/shard_map/ppermute | solution.py:35
  17.7 9.3 %collective-permute-start.4 = (bf16[2,576,128]{2,1,0:T(8,128)(2,1)S(1)}, bf16[2,576,128]{2,1,0:T(8,128)(2,1)S(1)}, u32[]{:S(2)}, u32[]{:S(2)}) collective-permute-start(bf16[2,576,128]{2,1,0:T(8,128)(2,1)S(1)} %pad_maximum_fusion.1.refs_0_), channel_id=1, source_target_pairs={{0,16},{1,17},{2,18},{3,19},{4,20},{5,21},{6,22},{7,23},{8,24},{9,... | collective-permute-start | bytes 884744 | tf_op jit(solution)/shard_map/ppermute | solution.py:35
  18.1 11.4 %copy-start.4 = (bf16[128,4608]{1,0:T(8,128)(2,1)S(1)}, bf16[128,4608]{1,0:T(8,128)(2,1)}, u32[]{:S(2)}) copy-start(bf16[128,4608]{1,0:T(8,128)(2,1)} %param.8) | copy-start | bytes 3538948
  18.3 31.1 %collective-permute-start.19 = (bf16[2,256,896]{2,1,0:T(8,128)(2,1)S(1)}, bf16[2,256,896]{2,1,0:T(8,128)(2,1)S(1)}, u32[]{:S(2)}, u32[]{:S(2)}) collective-permute-start(bf16[2,256,896]{2,1,0:T(8,128)(2,1)S(1)} %pad_maximum_fusion.refs_8_), channel_id=1, source_target_pairs={{0,192},{1,193},{2,194},{3,195},{4,196},{5,197},{6,198},{7,199},{8... | collective-permute-start | bytes 2752520 | tf_op jit(solution)/shard_map/ppermute | solution.py:35
  24.3 8.5 %collective-permute-start.5 = (bf16[2,576,128]{2,1,0:T(8,128)(2,1)}, bf16[2,576,128]{2,1,0:T(8,128)(2,1)}, u32[]{:S(2)}, u32[]{:S(2)}) collective-permute-start(bf16[2,576,128]{2,1,0:T(8,128)(2,1)} %collective-permute-done.1.refs_1_), channel_id=1, source_target_pairs={{0,16},{1,17},{2,18},{3,19},{4,20},{5,21},{6,22},{7,23},{8,24},{9,... | collective-permute-start | bytes 884744 | tf_op jit(solution)/shard_map/ppermute | solution.py:35
  24.3 8.5 %collective-permute-start.6 = (bf16[2,576,128]{2,1,0:T(8,128)(2,1)}, bf16[2,576,128]{2,1,0:T(8,128)(2,1)}, u32[]{:S(2)}, u32[]{:S(2)}) collective-permute-start(bf16[2,576,128]{2,1,0:T(8,128)(2,1)} %collective-permute-done.2.refs_2_), channel_id=1, source_target_pairs={{0,16},{1,17},{2,18},{3,19},{4,20},{5,21},{6,22},{7,23},{8,24},{9,... | collective-permute-start | bytes 884744 | tf_op jit(solution)/shard_map/ppermute | solution.py:35
  27.0 5.8 %collective-permute-start.7 = (bf16[2,576,128]{2,1,0:T(8,128)(2,1)}, bf16[2,576,128]{2,1,0:T(8,128)(2,1)}, u32[]{:S(2)}, u32[]{:S(2)}) collective-permute-start(bf16[2,576,128]{2,1,0:T(8,128)(2,1)} %collective-permute-done.3.refs_3_), channel_id=1, source_target_pairs={{0,16},{1,17},{2,18},{3,19},{4,20},{5,21},{6,22},{7,23},{8,24},{9,... | collective-permute-start | bytes 884744 | tf_op jit(solution)/shard_map/ppermute | solution.py:35
  27.0 0.7 copy-start.1
  27.7 24.1 %collective-permute-start.20 = (bf16[2,256,896]{2,1,0:T(8,128)(2,1)S(1)}, bf16[2,256,896]{2,1,0:T(8,128)(2,1)}, u32[]{:S(2)}, u32[]{:S(2)}) collective-permute-start(bf16[2,256,896]{2,1,0:T(8,128)(2,1)S(1)} %pad_maximum_fusion.refs_8_), channel_id=1, source_target_pairs={{0,64},{1,65},{2,66},{3,67},{4,68},{5,69},{6,70},{7,71},{8,72},{9,... | collective-permute-start | bytes 2752520 | tf_op jit(solution)/shard_map/ppermute | solution.py:35
  31.0 1.7 %copy-start.6 = (s32[16]{0:T(128)S(1)}, s32[16]{0:T(128)}, u32[]{:S(2)}) copy-start(s32[16]{0:T(128)} %param.11) | copy-start | bytes 196
  32.8 1.2 %copy-start = (bf16[8,512,128]{2,1,0:T(8,128)(2,1)S(1)}, bf16[8,512,128]{2,1,0:T(8,128)(2,1)}, u32[]{:S(2)}) copy-start(bf16[8,512,128]{2,1,0:T(8,128)(2,1)} %refs_8_.1) | copy-start | bytes 3145732
  34.1 1.0 copy-start.2
  35.0 0.9 copy-start.3
  45.7 10.8 %collective-permute-start.8 = (bf16[4,128,256]{2,1,0:T(8,128)(2,1)S(1)}, bf16[4,128,256]{2,1,0:T(8,128)(2,1)S(1)}, u32[]{:S(2)}, u32[]{:S(2)}) collective-permute-start(bf16[4,128,256]{2,1,0:T(8,128)(2,1)S(1)} %attention.1.refs_0_), channel_id=1, source_target_pairs={{0,1},{1,0},{2,3},{3,2},{4,5},{5,4},{6,7},{7,6},{8,9},{9,8},{10,11... | collective-permute-start | bytes 786440 | tf_op jit(solution)/shard_map/ppermute | solution.py:35
  47.8 8.7 %collective-permute-start.9 = (bf16[4,128,256]{2,1,0:T(8,128)(2,1)S(1)}, bf16[4,128,256]{2,1,0:T(8,128)(2,1)S(1)}, u32[]{:S(2)}, u32[]{:S(2)}) collective-permute-start(bf16[4,128,256]{2,1,0:T(8,128)(2,1)S(1)} %attention.1.refs_0_), channel_id=1, source_target_pairs={{0,16},{1,17},{2,18},{3,19},{4,20},{5,21},{6,22},{7,23},{8,24},{9,... | collective-permute-start | bytes 786440 | tf_op jit(solution)/shard_map/ppermute | solution.py:35
  47.9 12.2 %collective-permute-start.11 = (bf16[4,128,256]{2,1,0:T(8,128)(2,1)S(1)}, bf16[4,128,256]{2,1,0:T(8,128)(2,1)S(1)}, u32[]{:S(2)}, u32[]{:S(2)}) collective-permute-start(bf16[4,128,256]{2,1,0:T(8,128)(2,1)S(1)} %attention.1.refs_0_), channel_id=1, source_target_pairs={{0,32},{1,33},{2,34},{3,35},{4,36},{5,37},{6,38},{7,39},{8,40},{9,... | collective-permute-start | bytes 786440 | tf_op jit(solution)/shard_map/ppermute | solution.py:35
  49.3 11.8 %collective-permute-start.12 = (bf16[4,128,256]{2,1,0:T(8,128)(2,1)S(1)}, bf16[4,128,256]{2,1,0:T(8,128)(2,1)S(1)}, u32[]{:S(2)}, u32[]{:S(2)}) collective-permute-start(bf16[4,128,256]{2,1,0:T(8,128)(2,1)S(1)} %attention.1.refs_0_), channel_id=1, source_target_pairs={{0,33},{1,32},{2,35},{3,34},{4,37},{5,36},{6,39},{7,38},{8,41},{9,... | collective-permute-start | bytes 786440 | tf_op jit(solution)/shard_map/ppermute | solution.py:35
  51.8 12.2 %collective-permute-start.21 = (bf16[256,896]{1,0:T(8,128)(2,1)S(1)}, bf16[256,896]{1,0:T(8,128)(2,1)S(1)}, u32[]{:S(2)}, u32[]{:S(2)}) collective-permute-start(bf16[256,896]{1,0:T(8,128)(2,1)S(1)} %slice_bitcast_fusion.1), channel_id=1, source_target_pairs={{0,192},{1,193},{2,194},{3,195},{4,196},{5,197},{6,198},{7,199},{8... | collective-permute-start | bytes 1376264 | tf_op jit(solution)/shard_map/ppermute | solution.py:35
  56.5 12.1 %collective-permute-start.22 = (bf16[256,896]{1,0:T(8,128)(2,1)S(1)}, bf16[256,896]{1,0:T(8,128)(2,1)S(1)}, u32[]{:S(2)}, u32[]{:S(2)}) collective-permute-start(bf16[256,896]{1,0:T(8,128)(2,1)S(1)} %slice_bitcast_fusion), channel_id=1, source_target_pairs={{0,64},{1,65},{2,66},{3,67},{4,68},{5,69},{6,70},{7,71},{8,72},{9,... | collective-permute-start | bytes 1376264 | tf_op jit(solution)/shard_map/ppermute | solution.py:35
  56.5 4.7 %collective-permute-start.10 = (bf16[4,128,256]{2,1,0:T(8,128)(2,1)S(1)}, bf16[4,128,256]{2,1,0:T(8,128)(2,1)S(1)}, u32[]{:S(2)}, u32[]{:S(2)}) collective-permute-start(bf16[4,128,256]{2,1,0:T(8,128)(2,1)S(1)} %collective-permute-done.8.refs_1_), channel_id=1, source_target_pairs={{0,16},{1,17},{2,18},{3,19},{4,20},{5,21},{6,22},{7,23},{8,24},{9,... | collective-permute-start | bytes 786440 | tf_op jit(solution)/shard_map/ppermute | solution.py:35
  60.0 1.5 %collective-permute-start.13 = (bf16[4,128,256]{2,1,0:T(8,128)(2,1)S(1)}, bf16[4,128,256]{2,1,0:T(8,128)(2,1)S(1)}, u32[]{:S(2)}, u32[]{:S(2)}) collective-permute-start(bf16[4,128,256]{2,1,0:T(8,128)(2,1)S(1)} %collective-permute-done.11.refs_4_), channel_id=1, source_target_pairs={{0,16},{1,17},{2,18},{3,19},{4,20},{5,21},{6,22},{7,23},{8,24},{9,... | collective-permute-start | bytes 786440 | tf_op jit(solution)/shard_map/ppermute | solution.py:35
  61.1 1.5 %collective-permute-start.14 = (bf16[4,128,256]{2,1,0:T(8,128)(2,1)S(1)}, bf16[4,128,256]{2,1,0:T(8,128)(2,1)S(1)}, u32[]{:S(2)}, u32[]{:S(2)}) collective-permute-start(bf16[4,128,256]{2,1,0:T(8,128)(2,1)S(1)} %collective-permute-done.12.refs_5_), channel_id=1, source_target_pairs={{0,16},{1,17},{2,18},{3,19},{4,20},{5,21},{6,22},{7,23},{8,24},{9,... | collective-permute-start | bytes 786440 | tf_op jit(solution)/shard_map/ppermute | solution.py:35
  74.0 12.4 %collective-permute-start.29 = (bf16[448,128]{1,0:T(8,128)(2,1)S(1)}, bf16[448,128]{1,0:T(8,128)(2,1)S(1)}, u32[]{:S(2)}, u32[]{:S(2)}) collective-permute-start(bf16[448,128]{1,0:T(8,128)(2,1)S(1)} %get-tuple-element.20), channel_id=1, source_target_pairs={{0,14},{1,15},{2,0},{3,1},{4,2},{5,3},{6,4},{7,5},{8,6},{9,7},{10,... | collective-permute-start | bytes 344072 | tf_op jit(solution)/shard_map/ppermute | solution.py:35
  74.2 15.2 %collective-permute-start.28 = (bf16[448,128]{1,0:T(8,128)(2,1)S(1)}, bf16[448,128]{1,0:T(8,128)(2,1)S(1)}, u32[]{:S(2)}, u32[]{:S(2)}) collective-permute-start(bf16[448,128]{1,0:T(8,128)(2,1)S(1)} %get-tuple-element.19), channel_id=1, source_target_pairs={{0,12},{1,13},{2,14},{3,15},{4,0},{5,1},{6,2},{7,3},{8,4},{9,5},{1... | collective-permute-start | bytes 344072 | tf_op jit(solution)/shard_map/ppermute | solution.py:35
  80.5 13.4 %collective-permute-start.27 = (bf16[448,128]{1,0:T(8,128)(2,1)S(1)}, bf16[448,128]{1,0:T(8,128)(2,1)S(1)}, u32[]{:S(2)}, u32[]{:S(2)}) collective-permute-start(bf16[448,128]{1,0:T(8,128)(2,1)S(1)} %get-tuple-element.18), channel_id=1, source_target_pairs={{0,10},{1,11},{2,12},{3,13},{4,14},{5,15},{6,0},{7,1},{8,2},{9,3},... | collective-permute-start | bytes 344072 | tf_op jit(solution)/shard_map/ppermute | solution.py:35
  81.4 18.0 %collective-permute-start.26 = (bf16[448,128]{1,0:T(8,128)(2,1)S(1)}, bf16[448,128]{1,0:T(8,128)(2,1)S(1)}, u32[]{:S(2)}, u32[]{:S(2)}) collective-permute-start(bf16[448,128]{1,0:T(8,128)(2,1)S(1)} %get-tuple-element.17), channel_id=1, source_target_pairs={{0,8},{1,9},{2,10},{3,11},{4,12},{5,13},{6,14},{7,15},{8,0},{9,1},... | collective-permute-start | bytes 344072 | tf_op jit(solution)/shard_map/ppermute | solution.py:35
  85.9 14.1 %collective-permute-start.25 = (bf16[448,128]{1,0:T(8,128)(2,1)S(1)}, bf16[448,128]{1,0:T(8,128)(2,1)S(1)}, u32[]{:S(2)}, u32[]{:S(2)}) collective-permute-start(bf16[448,128]{1,0:T(8,128)(2,1)S(1)} %get-tuple-element.16), channel_id=1, source_target_pairs={{0,6},{1,7},{2,8},{3,9},{4,10},{5,11},{6,12},{7,13},{8,14},{9,15},... | collective-permute-start | bytes 344072 | tf_op jit(solution)/shard_map/ppermute | solution.py:35
  86.4 16.2 %collective-permute-start.24 = (bf16[448,128]{1,0:T(8,128)(2,1)S(1)}, bf16[448,128]{1,0:T(8,128)(2,1)S(1)}, u32[]{:S(2)}, u32[]{:S(2)}) collective-permute-start(bf16[448,128]{1,0:T(8,128)(2,1)S(1)} %get-tuple-element.15), channel_id=1, source_target_pairs={{0,4},{1,5},{2,6},{3,7},{4,8},{5,9},{6,10},{7,11},{8,12},{9,13},{1... | collective-permute-start | bytes 344072 | tf_op jit(solution)/shard_map/ppermute | solution.py:35
  89.3 14.7 %collective-permute-start.23 = (bf16[448,128]{1,0:T(8,128)(2,1)S(1)}, bf16[448,128]{1,0:T(8,128)(2,1)S(1)}, u32[]{:S(2)}, u32[]{:S(2)}) collective-permute-start(bf16[448,128]{1,0:T(8,128)(2,1)S(1)} %get-tuple-element.14), channel_id=1, source_target_pairs={{0,2},{1,3},{2,4},{3,5},{4,6},{5,7},{6,8},{7,9},{8,10},{9,11},{10,... | collective-permute-start | bytes 344072 | tf_op jit(solution)/shard_map/ppermute | solution.py:35
  104.1 14.6 %collective-permute-start.30 = (bf16[448,128]{1,0:T(8,128)(2,1)S(1)}, bf16[448,128]{1,0:T(8,128)(2,1)S(1)}, u32[]{:S(2)}, u32[]{:S(2)}) collective-permute-start(bf16[448,128]{1,0:T(8,128)(2,1)S(1)} %add_convert_fusion), channel_id=1, source_target_pairs={{0,0},{1,2},{2,1},{3,3},{4,16},{5,18},{6,17},{7,19},{8,32},{9,34},... | collective-permute-start | bytes 344072 | tf_op jit(solution)/shard_map/ppermute | solution.py:35

commit v2 on v1

--- a/solution.py
+++ b/solution.py
@@ -17,6 +17,7 @@
 ROWS = HEADS_DEV * SEG_LEN
 ANC_SEGS = 16
 COLS = 448
+PAD = 64
 
 NEG = -1e30
 LOG2E = 1.4426950408889634
@@ -52,12 +53,14 @@
 
 
 def to_owner(x):
-    return move(x, lambda y, xl, c, z, xh: (y, z >> 2, (z >> 1) & 1, xl * 4 + c * 2 + xh, z & 1))
+    return move(
+        x, lambda y, xl, c, z, xh: (y, xl ^ (z >> 2), c ^ ((z >> 1) & 1), xl * 4 + c * 2 + xh, z & 1)
+    )
 
 
 def attention_kernel(meta, q_ref, own_ref, *refs):
     anc_refs = refs[:8]
-    up_ref, out_ref, keys, scores, top, total, accum, where_ref = refs[8:]
+    up_hbm, out_ref, keys, scores, top, total, accum, up_ref, where_ref, sems = refs[8:]
     y, xl, c = meta[18], meta[19], meta[20]
     length = meta[17]
 
@@ -80,20 +83,42 @@
 
     end, _ = lax.fori_loop(0, ANC_SEGS, walk, (jnp.int32(1), meta[16]))
 
-    keys[0] = own_ref[...]
-    keys[end] = own_ref[...]
+    body = pl.ds(PAD, WIDTH)
+    copies = [
+        (None, pltpu.make_async_copy(own_ref, keys.at[0, body], sems.at[ANC_SEGS])),
+        (None, pltpu.make_async_copy(own_ref, keys.at[end, body], sems.at[ANC_SEGS + 1])),
+    ]
     for slot in range(ANC_SEGS):
         place = where_ref[slot]
-
-        @pl.when(place >= 0)
-        def _(slot=slot, place=place):
-            keys[place] = anc_refs[slot // 2][slot % 2]
+        target = keys.at[jnp.maximum(place, 0), body]
+        source = anc_refs[slot // 2].at[slot % 2]
+        copies.append((place >= 0, pltpu.make_async_copy(source, target, sems.at[slot])))
+    for used, copy in copies:
+        if used is None:
+            copy.start()
+        else:
+            pl.when(used)(copy.start)
+    up_copy = pltpu.make_async_copy(up_hbm, up_ref, sems.at[ANC_SEGS + 2])
+    up_copy.start()
+    keys[:, :PAD] = jnp.zeros((ANC_SEGS + 2, PAD, SEG_LEN), jnp.bfloat16)
+    keys[:, PAD + WIDTH :] = jnp.zeros((ANC_SEGS + 2, PAD, SEG_LEN), jnp.bfloat16)
+    for used, copy in copies:
+        if used is None:
+            copy.wait()
+        else:
+            pl.when(used)(copy.wait)
 
     pairs = (end + 1) // 2
+
+    def queries(odd):
+        starts = [h * WIDTH - PAD * odd for h in range(odd, HEADS_DEV, 2)]
+        return jnp.concatenate([q_ref[:, s : s + WIDTH + PAD] for s in starts], axis=0)
 
     def score(j):
         pair = jnp.concatenate([keys[2 * j], keys[2 * j + 1]], axis=1)
-        s = jnp.dot(q_ref[...], pair, preferred_element_type=jnp.float32)
+        even = jnp.dot(queries(0), pair[PAD:], preferred_element_type=jnp.float32)
+        odd = jnp.dot(queries(1), pair[: WIDTH + PAD], preferred_element_type=jnp.float32)
+        s = jnp.concatenate([even, odd], axis=0)
         return s[:, :SEG_LEN], s[:, SEG_LEN:]
 
     row = lax.broadcasted_iota(jnp.int32, (ROWS, SEG_LEN), 0) & (SEG_LEN - 1)
@@ -125,16 +150,19 @@
         right = jnp.exp2((scores[j, :, SEG_LEN:] - high) * factor)
         total[...] += left + right
         weight = jnp.concatenate([left, right], axis=1).astype(jnp.bfloat16)
-        pair = jnp.concatenate([keys[2 * j, :LATENT], keys[2 * j + 1, :LATENT]], axis=1)
+        values = pl.ds(PAD, LATENT)
+        pair = jnp.concatenate([keys[2 * j, values], keys[2 * j + 1, values]], axis=1)
         accum[...] += lax.dot_general(
             weight, pair, (((1,), (1,)), ((), ())), preferred_element_type=jnp.float32
         )
         return carry
 
     lax.fori_loop(0, pairs, second, 0)
+    up_copy.wait()
     pos = lax.broadcasted_iota(jnp.int32, (SEG_LEN, VHEAD), 0)
     for h in range(HEADS_DEV):
-        rows = slice(h * SEG_LEN, (h + 1) * SEG_LEN)
+        at = (h % 2) * (HEADS_DEV // 2) + h // 2
+        rows = slice(at * SEG_LEN, (at + 1) * SEG_LEN)
         denominator = jnp.sum(total[rows], axis=1, keepdims=True)
         latent_out = (accum[rows] / denominator).astype(jnp.bfloat16)
         head_out = jnp.dot(latent_out, up_ref[h], preferred_element_type=jnp.float32)
@@ -146,20 +174,23 @@
 
 def attention(meta, q, own, anc, up):
     vmem = pl.BlockSpec(memory_space=pltpu.VMEM)
+    anywhere = pl.BlockSpec(memory_space=pl.ANY)
     return pl.pallas_call(
         attention_kernel,
         out_shape=jax.ShapeDtypeStruct((4, SEG_LEN, 256), jnp.bfloat16),
-        in_specs=[pl.BlockSpec(memory_space=pltpu.SMEM)] + [vmem] * 11,
+        in_specs=[pl.BlockSpec(memory_space=pltpu.SMEM), vmem] + [anywhere] * 10,
         out_specs=vmem,
         scratch_shapes=[
-            pltpu.VMEM((ANC_SEGS + 2, WIDTH, SEG_LEN), jnp.bfloat16),
+            pltpu.VMEM((ANC_SEGS + 2, WIDTH + 2 * PAD, SEG_LEN), jnp.bfloat16),
             pltpu.VMEM((9, ROWS, 2 * SEG_LEN), jnp.float32),
             pltpu.VMEM((ROWS, SEG_LEN), jnp.float32),
             pltpu.VMEM((ROWS, SEG_LEN), jnp.float32),
             pltpu.VMEM((ROWS, LATENT), jnp.float32),
+            pltpu.VMEM((HEADS_DEV, LATENT, VHEAD), jnp.bfloat16),
             pltpu.SMEM((ANC_SEGS,), jnp.int32),
+            pltpu.SemaphoreType.DMA((ANC_SEGS + 3,)),
         ],
-        compiler_params=pltpu.CompilerParams(vmem_limit_bytes=48 * 2**20),
+        compiler_params=pltpu.CompilerParams(vmem_limit_bytes=30 * 2**20),
         cost_estimate=pl.CostEstimate(
             flops=4 * 10**9, bytes_accessed=6 * 2**20, transcendentals=2 * 10**6
         ),
@@ -172,7 +203,7 @@
     w0, w1, w3, w2a, w2b = refs[8:13]
     outs = refs[13:21]
     left, partial = refs[21:]
-    xl, c, z = meta[19], meta[20], meta[21]
+    z = meta[21]
     weights = [[w0.at[0], w1.at[0], w2a, w3.at[0]], [w0.at[1], w1.at[1], w2b, w3.at[1]]]
     for b in range(2):
         for t in range(4):
@@ -193,7 +224,7 @@
             partial[t, cols] = value[t * SEG_LEN : (t + 1) * SEG_LEN].T.astype(jnp.bfloat16)
     for k in range(8):
         target = lax.bitwise_and(z + k, 7)
-        t = lax.bitwise_xor(target >> 2, xl) * 2 + lax.bitwise_xor(lax.bitwise_and(target >> 1, 1), c)
+        t = target >> 1
         half = lax.bitwise_and(target, 1)
 
         @pl.when(half == 0)
@@ -216,7 +247,7 @@
             pltpu.VMEM((4 * SEG_LEN, 2048), jnp.bfloat16),
             pltpu.VMEM((4, 2 * COLS, SEG_LEN), jnp.bfloat16),
         ],
-        compiler_params=pltpu.CompilerParams(vmem_limit_bytes=48 * 2**20),
+        compiler_params=pltpu.CompilerParams(vmem_limit_bytes=20 * 2**20),
         cost_estimate=pl.CostEstimate(
             flops=2 * 10**9, bytes_accessed=8 * 2**20, transcendentals=0
         ),
@@ -242,29 +273,32 @@
 
     mine = ancestor_latent.T
     column = jnp.stack([mine, swap_x(mine, 1, 0)])
-    anc = [column] + [from_y(column, r) for r in (1, 2, 3)]
-    anc = anc + [swap_core(x) for x in anc]
+    column, out_weight = lax.optimization_barrier((column, out_weight))
 
     blocks = out_weight.reshape(HEADS_DEV, 8, 2, 2, 2, 2 * COLS).transpose(3, 2, 4, 0, 1, 5)
     keep = lax.dynamic_index_in_dim(blocks, c, 0, keepdims=False)
     other = swap_core(lax.dynamic_index_in_dim(blocks, 1 - c, 0, keepdims=False))
     cores = jnp.where(c == 0, jnp.stack([keep, other], 3), jnp.stack([other, keep], 3))
+    near, far = from_y(column, 1), from_y(column, 3)
+    opposite = jnp.stack([from_y(near[0], 1), from_y(far[1], 3)])
+    anc = [column, near, opposite, far]
 
     def for_x(a, b):
         part = lax.dynamic_index_in_dim(cores, xl ^ a, 0, keepdims=False)
         part = lax.dynamic_index_in_dim(part, xh ^ b, 0, keepdims=False)
         return swap_x(part, a, b) if a or b else part
 
-    rows = []
+    w0 = []
     for b in range(2):
         near, far = for_x(0, b), for_x(1, b)
-        rows.append(jnp.where(xl == 0, jnp.stack([near, far], 1), jnp.stack([far, near], 1)))
-    w0 = jnp.stack(rows).reshape(2, 256, 2 * COLS)
+        w0.append(jnp.where(xl == 0, jnp.stack([near, far], 1), jnp.stack([far, near], 1)))
+    w0 = jnp.stack(w0).reshape(2, 256, 2 * COLS)
+    w0, anc = lax.optimization_barrier((w0, anc))
+    anc = anc + [swap_core(x) for x in anc]
     w1, w3 = from_y(w0, 1), from_y(w0, 3)
     w2a, w2b = from_y(w1[0], 1), from_y(w3[1], 3)
 
-    q = queries.reshape(SEG_LEN, HEADS_DEV, WIDTH).transpose(1, 0, 2).reshape(ROWS, WIDTH)
-    head_out = attention(meta, q, leaf_latent.T, anc, value_up)
+    head_out = attention(meta, queries, leaf_latent.T, anc, value_up)
 
     heads = []
     for a in range(2):

time: 121 us -> 129 us (1.066)
  the two profiles are of different devices: /device:TPU:34 before, /device:TPU:42 now
where the time goes in v2:
time: 129 us; the launch traced here: 127 us
  waiting for transfers between devices  51.8 us (40%)
  starting transfers between devices  49.4 us (38%)
  Pallas kernels  14.7 us (11%)
  local copies, waits for them, and re-layouts  8.28 us (6%)
  between operations  1.51 us (1%)
  other arithmetic  1.47 us (1%)
    ppermute x32, waiting for transfers between devices, move(): return lax.ppermute(x, ('seg', 'head'), pairs)  51.8 us
    ppermute x32, starting transfers between devices, move(): return lax.ppermute(x, ('seg', 'head'), pairs)  49.4 us
    pallas_call x1, Pallas kernels, attention(): pl.pallas_call(attention_kernel, out_shape=jax.ShapeDtypeStruct((4, SEG_L...  10 us
    unnamed x13, local copies, waits for them, and re-layouts  4.84 us
    pallas_call x1, Pallas kernels, project(): pl.pallas_call(project_kernel, out_shape=[jax.ShapeDtypeStruct((COLS, SEG...  4.73 us
  transfers between devices with their start and end apart: 32, of which 16 were waited for; matrix products, arithmetic and copies ran while one was open for 3% of the time, Pallas kernels for 8%

profile of v2, /device:TPU:42, one launch (start us, length us, event | category | flops | bytes accessed | tf_op | source)
XLA Modules:
  0.0 127.2 jit_solution(9829328623335486164)
XLA Ops:
  0.0 0.5 collective-permute-start
  0.5 5.3 %collective-permute-done = bf16[576,128]{1,0:T(8,128)(2,1)S(1)} collective-permute-done((bf16[576,128]{1,0:T(8,128)(2,1)}, bf16[576,128]{1,0:T(8,128)(2,1)S(1)}, u32[]{:S(2)}, u32[]{:S(2)}) %collective-permute-start) | collective-permute-done | bytes 147488 | tf_op jit(solution)/shard_map/ppermute | solution.py:36
  5.8 0.9 pad_maximum_fusion.1.refs_0_
  6.7 1.7 %collective-permute-start.7 = (bf16[2,576,128]{2,1,0:T(8,128)(2,1)S(1)}, bf16[2,576,128]{2,1,0:T(8,128)(2,1)}, u32[]{:S(2)}, u32[]{:S(2)}) collective-permute-start(bf16[2,576,128]{2,1,0:T(8,128)(2,1)S(1)} %pad_maximum_fusion.1.refs_0_), channel_id=1, source_target_pairs={{0,64},{1,65},{2,66},{3,67},{4,68},{5,69},{6,70},{7,71},{8,72},{9,... | collective-permute-start | bytes 884744 | tf_op jit(solution)/shard_map/ppermute | solution.py:36
  8.8 1.2 dynamic-slice_bitcast_fusion.1
  10.2 4.6 %collective-permute-done.7.refs_3_ = bf16[2,576,128]{2,1,0:T(8,128)(2,1)} collective-permute-done((bf16[2,576,128]{2,1,0:T(8,128)(2,1)S(1)}, bf16[2,576,128]{2,1,0:T(8,128)(2,1)}, u32[]{:S(2)}, u32[]{:S(2)}) %collective-permute-start.7) | collective-permute-done | bytes 294944 | tf_op jit(solution)/shard_map/ppermute | solution.py:36
  14.8 0.9 slice_bitcast_fusion.2
  15.7 1.7 %collective-permute-start.8 = (bf16[576,128]{1,0:T(8,128)(2,1)S(1)}, bf16[576,128]{1,0:T(8,128)(2,1)S(1)}, u32[]{:S(2)}, u32[]{:S(2)}) collective-permute-start(bf16[576,128]{1,0:T(8,128)(2,1)S(1)} %slice_bitcast_fusion.2), channel_id=1, source_target_pairs={{0,64},{1,65},{2,66},{3,67},{4,68},{5,69},{6,70},{7,71},{8,72},{9,... | collective-permute-start | bytes 442376 | tf_op jit(solution)/shard_map/ppermute | solution.py:36
  17.4 0.9 slice_bitcast_fusion.3
  19.2 0.6 collective-permute-start.2
  19.8 2.5 %collective-permute-start.3 = (bf16[8,2,8,896]{3,2,1,0:T(8,128)(2,1)S(1)}, bf16[8,2,8,896]{3,2,1,0:T(8,128)(2,1)S(1)}, u32[]{:S(2)}, u32[]{:S(2)}) collective-permute-start(bf16[8,2,8,896]{3,2,1,0:T(8,128)(2,1)S(1)} %bitcast.58), channel_id=1, source_target_pairs={{0,1},{1,0},{2,3},{3,2},{4,5},{5,4},{6,7},{7,6},{8,9},{9,8},{10,11... | collective-permute-start | bytes 688136 | tf_op jit(solution)/shard_map/ppermute | solution.py:36
  22.3 0.5 collective-permute-start.4
  22.9 0.7 collective-permute-done.6
  23.6 3.3 %collective-permute-done.2 = bf16[8,2,8,896]{3,2,1,0:T(8,128)(2,1)S(1)} collective-permute-done((bf16[8,2,8,896]{3,2,1,0:T(8,128)(2,1)S(1)}, bf16[8,2,8,896]{3,2,1,0:T(8,128)(2,1)S(1)}, u32[]{:S(2)}, u32[]{:S(2)}) %collective-permute-start.2) | collective-permute-done | bytes 229408 | tf_op jit(solution)/shard_map/ppermute | solution.py:36
  26.9 3.3 %collective-permute-done.3 = bf16[8,2,8,896]{3,2,1,0:T(8,128)(2,1)S(1)} collective-permute-done((bf16[8,2,8,896]{3,2,1,0:T(8,128)(2,1)S(1)}, bf16[8,2,8,896]{3,2,1,0:T(8,128)(2,1)S(1)}, u32[]{:S(2)}, u32[]{:S(2)}) %collective-permute-start.3) | collective-permute-done | bytes 229408 | tf_op jit(solution)/shard_map/ppermute | solution.py:36
  30.3 1.5 %collective-permute-done.4 = bf16[8,2,8,896]{3,2,1,0:T(8,128)(2,1)S(1)} collective-permute-done((bf16[8,2,8,896]{3,2,1,0:T(8,128)(2,1)S(1)}, bf16[8,2,8,896]{3,2,1,0:T(8,128)(2,1)S(1)}, u32[]{:S(2)}, u32[]{:S(2)}) %collective-permute-start.4) | collective-permute-done | bytes 229408 | tf_op jit(solution)/shard_map/ppermute | solution.py:36
  32.0 1.6 %collective-permute-start.21 = (bf16[2,256,896]{2,1,0:T(8,128)(2,1)S(1)}, bf16[2,256,896]{2,1,0:T(8,128)(2,1)S(1)}, u32[]{:S(2)}, u32[]{:S(2)}) collective-permute-start(bf16[2,256,896]{2,1,0:T(8,128)(2,1)S(1)} %pad_maximum_fusion.refs_8_), channel_id=1, source_target_pairs={{0,64},{1,65},{2,66},{3,67},{4,68},{5,69},{6,70},{7,71},{8,72},{9,... | collective-permute-start | bytes 2752520 | tf_op jit(solution)/shard_map/ppermute | solution.py:36
  34.3 0.7 copy-done.2
  35.0 2.2 %collective-permute-start.20 = (bf16[2,256,896]{2,1,0:T(8,128)(2,1)S(1)}, bf16[2,256,896]{2,1,0:T(8,128)(2,1)S(1)}, u32[]{:S(2)}, u32[]{:S(2)}) collective-permute-start(bf16[2,256,896]{2,1,0:T(8,128)(2,1)S(1)} %pad_maximum_fusion.refs_8_), channel_id=1, source_target_pairs={{0,192},{1,193},{2,194},{3,195},{4,196},{5,197},{6,198},{7,199},{8... | collective-permute-start | bytes 2752520 | tf_op jit(solution)/shard_map/ppermute | solution.py:36
  38.7 1.3 copy-done
  40.0 1.2 copy-done.1
  41.2 1.0 copy-done.3
  42.2 10.0 %attention.1.refs_0_ = bf16[4,128,256]{2,1,0:T(8,128)(2,1)S(1)} custom-call(s32[23]{0:T(128)S(1)} %concatenate.8.meta, bf16[128,4608]{1,0:T(8,128)(2,1)S(1)} %copy-done, bf16[576,128]{1,0:T(8,128)(2,1)S(1)} %bitcast.50, bf16[2,576,128]{2,1,0:T(8,128)(2,1)S(1)} %pad_maximum_fusion.1.refs_0_, bf16[2,576,128]{2,1,0:T(8,128)(2,1)} %collective-permute-done.5.refs_1_, ...), custom_call_target="tpu_custom_call" | custom-call | flops 4000000000 | bytes 6291456 | tf_op jit(solution)/shard_map/attention/pallas_call | solution.py:178
  52.2 0.6 collective-permute-start.17
  52.7 2.6 %collective-permute-start.16 = (bf16[4,128,256]{2,1,0:T(8,128)(2,1)S(1)}, bf16[4,128,256]{2,1,0:T(8,128)(2,1)S(1)}, u32[]{:S(2)}, u32[]{:S(2)}) collective-permute-start(bf16[4,128,256]{2,1,0:T(8,128)(2,1)S(1)} %attention.1.refs_0_), channel_id=1, source_target_pairs={{0,32},{1,33},{2,34},{3,35},{4,36},{5,37},{6,38},{7,39},{8,40},{9,... | collective-permute-start | bytes 786440 | tf_op jit(solution)/shard_map/ppermute | solution.py:36
  55.4 0.6 collective-permute-start.14
  56.0 2.0 %collective-permute-start.13 = (bf16[4,128,256]{2,1,0:T(8,128)(2,1)S(1)}, bf16[4,128,256]{2,1,0:T(8,128)(2,1)S(1)}, u32[]{:S(2)}, u32[]{:S(2)}) collective-permute-start(bf16[4,128,256]{2,1,0:T(8,128)(2,1)S(1)} %attention.1.refs_0_), channel_id=1, source_target_pairs={{0,1},{1,0},{2,3},{3,2},{4,5},{5,4},{6,7},{7,6},{8,9},{9,8},{10,11... | collective-permute-start | bytes 786440 | tf_op jit(solution)/shard_map/ppermute | solution.py:36
  58.0 2.0 %collective-permute-start.23 = (bf16[256,896]{1,0:T(8,128)(2,1)S(1)}, bf16[256,896]{1,0:T(8,128)(2,1)S(1)}, u32[]{:S(2)}, u32[]{:S(2)}) collective-permute-start(bf16[256,896]{1,0:T(8,128)(2,1)S(1)} %slice_bitcast_fusion), channel_id=1, source_target_pairs={{0,64},{1,65},{2,66},{3,67},{4,68},{5,69},{6,70},{7,71},{8,72},{9,... | collective-permute-start | bytes 1376264 | tf_op jit(solution)/shard_map/ppermute | solution.py:36
  60.0 1.3 %collective-permute-done.17.refs_5_ = bf16[4,128,256]{2,1,0:T(8,128)(2,1)S(1)} collective-permute-done((bf16[4,128,256]{2,1,0:T(8,128)(2,1)S(1)}, bf16[4,128,256]{2,1,0:T(8,128)(2,1)S(1)}, u32[]{:S(2)}, u32[]{:S(2)}) %collective-permute-start.17) | collective-permute-done | bytes 262176 | tf_op jit(solution)/shard_map/ppermute | solution.py:36
  61.3 3.0 %collective-permute-start.22 = (bf16[256,896]{1,0:T(8,128)(2,1)S(1)}, bf16[256,896]{1,0:T(8,128)(2,1)S(1)}, u32[]{:S(2)}, u32[]{:S(2)}) collective-permute-start(bf16[256,896]{1,0:T(8,128)(2,1)S(1)} %slice_bitcast_fusion.1), channel_id=1, source_target_pairs={{0,192},{1,193},{2,194},{3,195},{4,196},{5,197},{6,198},{7,199},{8... | collective-permute-start | bytes 1376264 | tf_op jit(solution)/shard_map/ppermute | solution.py:36
  64.8 4.9 %collective-permute-done.13.refs_1_ = bf16[4,128,256]{2,1,0:T(8,128)(2,1)S(1)} collective-permute-done((bf16[4,128,256]{2,1,0:T(8,128)(2,1)S(1)}, bf16[4,128,256]{2,1,0:T(8,128)(2,1)S(1)}, u32[]{:S(2)}, u32[]{:S(2)}) %collective-permute-start.13) | collective-permute-done | bytes 262176 | tf_op jit(solution)/shard_map/ppermute | solution.py:36
  69.8 1.4 %collective-permute-done.15.refs_3_ = bf16[4,128,256]{2,1,0:T(8,128)(2,1)S(1)} collective-permute-done((bf16[4,128,256]{2,1,0:T(8,128)(2,1)S(1)}, bf16[4,128,256]{2,1,0:T(8,128)(2,1)S(1)}, u32[]{:S(2)}, u32[]{:S(2)}) %collective-permute-start.15) | collective-permute-done | bytes 262176 | tf_op jit(solution)/shard_map/ppermute | solution.py:36
  71.5 2.5 %collective-permute-done.22.refs_11_ = bf16[256,896]{1,0:T(8,128)(2,1)S(1)} collective-permute-done((bf16[256,896]{1,0:T(8,128)(2,1)S(1)}, bf16[256,896]{1,0:T(8,128)(2,1)S(1)}, u32[]{:S(2)}, u32[]{:S(2)}) %collective-permute-start.22) | collective-permute-done | bytes 458784 | tf_op jit(solution)/shard_map/ppermute | solution.py:36
  74.0 4.7 %project.1 = (bf16[448,128]{1,0:T(8,128)(2,1)S(1)}, bf16[448,128]{1,0:T(8,128)(2,1)S(1)}, bf16[448,128]{1,0:T(8,128)(2,1)S(1)}, bf16[448,128]{1,0:T(8,128)(2,1)S...) custom-call(s32[23]{0:T(128)S(1)} %concatenate.8.meta, ...), custom_call_target="tpu_custom_call" | custom-call | flops 2000000000 | bytes 8388608 | tf_op jit(solution)/shard_map/project/pallas_call | solution.py:241
  78.7 2.0 %collective-permute-start.24 = (bf16[448,128]{1,0:T(8,128)(2,1)S(1)}, bf16[448,128]{1,0:T(8,128)(2,1)S(1)}, u32[]{:S(2)}, u32[]{:S(2)}) collective-permute-start(bf16[448,128]{1,0:T(8,128)(2,1)S(1)} %get-tuple-element.28), channel_id=1, source_target_pairs={{0,2},{1,3},{2,4},{3,5},{4,6},{5,7},{6,8},{7,9},{8,10},{9,11},{10,... | collective-permute-start | bytes 344072 | tf_op jit(solution)/shard_map/ppermute | solution.py:36
  80.7 4.5 %collective-permute-start.25 = (bf16[448,128]{1,0:T(8,128)(2,1)S(1)}, bf16[448,128]{1,0:T(8,128)(2,1)S(1)}, u32[]{:S(2)}, u32[]{:S(2)}) collective-permute-start(bf16[448,128]{1,0:T(8,128)(2,1)S(1)} %get-tuple-element.29), channel_id=1, source_target_pairs={{0,4},{1,5},{2,6},{3,7},{4,8},{5,9},{6,10},{7,11},{8,12},{9,13},{1... | collective-permute-start | bytes 344072 | tf_op jit(solution)/shard_map/ppermute | solution.py:36
  85.2 1.9 %collective-permute-start.26 = (bf16[448,128]{1,0:T(8,128)(2,1)S(1)}, bf16[448,128]{1,0:T(8,128)(2,1)S(1)}, u32[]{:S(2)}, u32[]{:S(2)}) collective-permute-start(bf16[448,128]{1,0:T(8,128)(2,1)S(1)} %get-tuple-element.30), channel_id=1, source_target_pairs={{0,6},{1,7},{2,8},{3,9},{4,10},{5,11},{6,12},{7,13},{8,14},{9,15},... | collective-permute-start | bytes 344072 | tf_op jit(solution)/shard_map/ppermute | solution.py:36
  87.1 1.4 %collective-permute-start.27 = (bf16[448,128]{1,0:T(8,128)(2,1)S(1)}, bf16[448,128]{1,0:T(8,128)(2,1)S(1)}, u32[]{:S(2)}, u32[]{:S(2)}) collective-permute-start(bf16[448,128]{1,0:T(8,128)(2,1)S(1)} %get-tuple-element.31), channel_id=1, source_target_pairs={{0,8},{1,9},{2,10},{3,11},{4,12},{5,13},{6,14},{7,15},{8,0},{9,1},... | collective-permute-start | bytes 344072 | tf_op jit(solution)/shard_map/ppermute | solution.py:36
  88.6 3.1 %collective-permute-start.28 = (bf16[448,128]{1,0:T(8,128)(2,1)S(1)}, bf16[448,128]{1,0:T(8,128)(2,1)S(1)}, u32[]{:S(2)}, u32[]{:S(2)}) collective-permute-start(bf16[448,128]{1,0:T(8,128)(2,1)S(1)} %get-tuple-element.32), channel_id=1, source_target_pairs={{0,10},{1,11},{2,12},{3,13},{4,14},{5,15},{6,0},{7,1},{8,2},{9,3},... | collective-permute-start | bytes 344072 | tf_op jit(solution)/shard_map/ppermute | solution.py:36
  91.7 2.4 %collective-permute-start.29 = (bf16[448,128]{1,0:T(8,128)(2,1)S(1)}, bf16[448,128]{1,0:T(8,128)(2,1)S(1)}, u32[]{:S(2)}, u32[]{:S(2)}) collective-permute-start(bf16[448,128]{1,0:T(8,128)(2,1)S(1)} %get-tuple-element.33), channel_id=1, source_target_pairs={{0,12},{1,13},{2,14},{3,15},{4,0},{5,1},{6,2},{7,3},{8,4},{9,5},{1... | collective-permute-start | bytes 344072 | tf_op jit(solution)/shard_map/ppermute | solution.py:36
  94.1 4.3 %collective-permute-start.30 = (bf16[448,128]{1,0:T(8,128)(2,1)S(1)}, bf16[448,128]{1,0:T(8,128)(2,1)S(1)}, u32[]{:S(2)}, u32[]{:S(2)}) collective-permute-start(bf16[448,128]{1,0:T(8,128)(2,1)S(1)} %get-tuple-element.34), channel_id=1, source_target_pairs={{0,14},{1,15},{2,0},{3,1},{4,2},{5,3},{6,4},{7,5},{8,6},{9,7},{10,... | collective-permute-start | bytes 344072 | tf_op jit(solution)/shard_map/ppermute | solution.py:36
  98.3 5.8 %collective-permute-done.26 = bf16[448,128]{1,0:T(8,128)(2,1)S(1)} collective-permute-done((bf16[448,128]{1,0:T(8,128)(2,1)S(1)}, bf16[448,128]{1,0:T(8,128)(2,1)S(1)}, u32[]{:S(2)}, u32[]{:S(2)}) %collective-permute-start.26) | collective-permute-done | bytes 114720 | tf_op jit(solution)/shard_map/ppermute | solution.py:36
  104.1 0.8 collective-permute-done.28
  104.9 4.9 %collective-permute-done.29 = bf16[448,128]{1,0:T(8,128)(2,1)S(1)} collective-permute-done((bf16[448,128]{1,0:T(8,128)(2,1)S(1)}, bf16[448,128]{1,0:T(8,128)(2,1)S(1)}, u32[]{:S(2)}, u32[]{:S(2)}) %collective-permute-start.29) | collective-permute-done | bytes 114720 | tf_op jit(solution)/shard_map/ppermute | solution.py:36
  109.8 1.2 collective-permute-done.30
  111.1 5.4 %collective-permute-start.31 = (bf16[448,128]{1,0:T(8,128)(2,1)S(1)}, bf16[448,128]{1,0:T(8,128)(2,1)S(1)}, u32[]{:S(2)}, u32[]{:S(2)}) collective-permute-start(bf16[448,128]{1,0:T(8,128)(2,1)S(1)} %add_convert_fusion), channel_id=1, source_target_pairs={{0,0},{1,2},{2,1},{3,3},{4,16},{5,18},{6,17},{7,19},{8,32},{9,34},... | collective-permute-start | bytes 344072 | tf_op jit(solution)/shard_map/ppermute | solution.py:36
  116.5 10.0 %collective-permute-done.31 = bf16[448,128]{1,0:T(8,128)(2,1)S(1)} collective-permute-done((bf16[448,128]{1,0:T(8,128)(2,1)S(1)}, bf16[448,128]{1,0:T(8,128)(2,1)S(1)}, u32[]{:S(2)}, u32[]{:S(2)}) %collective-permute-start.31) | collective-permute-done | bytes 114720 | tf_op jit(solution)/shard_map/ppermute | solution.py:36
  126.6 0.6 copy.26
  (49 shorter events, 3.7 us)
Async XLA Ops:
  0.0 5.8 %collective-permute-start = (bf16[576,128]{1,0:T(8,128)(2,1)}, bf16[576,128]{1,0:T(8,128)(2,1)S(1)}, u32[]{:S(2)}, u32[]{:S(2)}) collective-permute-start(bf16[576,128]{1,0:T(8,128)(2,1)} %bitcast.62), channel_id=1, source_target_pairs={{0,32},{1,33},{2,34},{3,35},{4,36},{5,37},{6,38},{7,39},{8,40},{9,... | collective-permute-start | bytes 442376 | tf_op jit(solution)/shard_map/ppermute | solution.py:36
  6.7 8.1 %collective-permute-start.7 = (bf16[2,576,128]{2,1,0:T(8,128)(2,1)S(1)}, bf16[2,576,128]{2,1,0:T(8,128)(2,1)}, u32[]{:S(2)}, u32[]{:S(2)}) collective-permute-start(bf16[2,576,128]{2,1,0:T(8,128)(2,1)S(1)} %pad_maximum_fusion.1.refs_0_), channel_id=1, source_target_pairs={{0,64},{1,65},{2,66},{3,67},{4,68},{5,69},{6,70},{7,71},{8,72},{9,... | collective-permute-start | bytes 884744 | tf_op jit(solution)/shard_map/ppermute | solution.py:36
  8.4 9.0 %collective-permute-start.5 = (bf16[2,576,128]{2,1,0:T(8,128)(2,1)S(1)}, bf16[2,576,128]{2,1,0:T(8,128)(2,1)}, u32[]{:S(2)}, u32[]{:S(2)}) collective-permute-start(bf16[2,576,128]{2,1,0:T(8,128)(2,1)S(1)} %pad_maximum_fusion.1.refs_0_), channel_id=1, source_target_pairs={{0,192},{1,193},{2,194},{3,195},{4,196},{5,197},{6,198},{7,199},{8... | collective-permute-start | bytes 884744 | tf_op jit(solution)/shard_map/ppermute | solution.py:36
  10.1 8.8 %collective-permute-start.1 = (bf16[2,2,8,8,896]{4,3,1,0,2:T(8,128)(2,1)S(1)}, bf16[2,2,8,8,896]{4,3,1,0,2:T(8,128)(2,1)S(1)}, u32[]{:S(2)}, u32[]{:S(2)}) collective-permute-start(bf16[2,2,8,8,896]{4,3,1,0,2:T(8,128)(2,1)S(1)} %get-tuple-element.40), channel_id=1, source_target_pairs={{0,16},{1,17},{2,18},{3,19},{4,20},{5,21},{6,22},{7,23},{8,24},{9,... | collective-permute-start | bytes 1376264 | tf_op jit(solution)/shard_map/ppermute | solution.py:36
  15.7 7.1 %collective-permute-start.8 = (bf16[576,128]{1,0:T(8,128)(2,1)S(1)}, bf16[576,128]{1,0:T(8,128)(2,1)S(1)}, u32[]{:S(2)}, u32[]{:S(2)}) collective-permute-start(bf16[576,128]{1,0:T(8,128)(2,1)S(1)} %slice_bitcast_fusion.2), channel_id=1, source_target_pairs={{0,64},{1,65},{2,66},{3,67},{4,68},{5,69},{6,70},{7,71},{8,72},{9,... | collective-permute-start | bytes 442376 | tf_op jit(solution)/shard_map/ppermute | solution.py:36
  18.3 5.2 %collective-permute-start.6 = (bf16[576,128]{1,0:T(8,128)(2,1)S(1)}, bf16[576,128]{1,0:T(8,128)(2,1)S(1)}, u32[]{:S(2)}, u32[]{:S(2)}) collective-permute-start(bf16[576,128]{1,0:T(8,128)(2,1)S(1)} %slice_bitcast_fusion.3), channel_id=1, source_target_pairs={{0,192},{1,193},{2,194},{3,195},{4,196},{5,197},{6,198},{7,199},{8... | collective-permute-start | bytes 442376 | tf_op jit(solution)/shard_map/ppermute | solution.py:36
  19.2 7.7 %collective-permute-start.2 = (bf16[8,2,8,896]{3,2,1,0:T(8,128)(2,1)S(1)}, bf16[8,2,8,896]{3,2,1,0:T(8,128)(2,1)S(1)}, u32[]{:S(2)}, u32[]{:S(2)}) collective-permute-start(bf16[8,2,8,896]{3,2,1,0:T(8,128)(2,1)S(1)} %bitcast.57), channel_id=1, source_target_pairs={{0,32},{1,33},{2,34},{3,35},{4,36},{5,37},{6,38},{7,39},{8,40},{9,... | collective-permute-start | bytes 688136 | tf_op jit(solution)/shard_map/ppermute | solution.py:36
  19.8 10.5 %collective-permute-start.3 = (bf16[8,2,8,896]{3,2,1,0:T(8,128)(2,1)S(1)}, bf16[8,2,8,896]{3,2,1,0:T(8,128)(2,1)S(1)}, u32[]{:S(2)}, u32[]{:S(2)}) collective-permute-start(bf16[8,2,8,896]{3,2,1,0:T(8,128)(2,1)S(1)} %bitcast.58), channel_id=1, source_target_pairs={{0,1},{1,0},{2,3},{3,2},{4,5},{5,4},{6,7},{7,6},{8,9},{9,8},{10,11... | collective-permute-start | bytes 688136 | tf_op jit(solution)/shard_map/ppermute | solution.py:36
  22.3 9.4 %collective-permute-start.4 = (bf16[8,2,8,896]{3,2,1,0:T(8,128)(2,1)S(1)}, bf16[8,2,8,896]{3,2,1,0:T(8,128)(2,1)S(1)}, u32[]{:S(2)}, u32[]{:S(2)}) collective-permute-start(bf16[8,2,8,896]{3,2,1,0:T(8,128)(2,1)S(1)} %bitcast.56), channel_id=1, source_target_pairs={{0,33},{1,32},{2,35},{3,34},{4,37},{5,36},{6,39},{7,38},{8,41},{9,... | collective-permute-start | bytes 688136 | tf_op jit(solution)/shard_map/ppermute | solution.py:36
  31.7 6.8 %copy-start.5 = (s32[16]{0:T(128)S(1)}, s32[16]{0:T(128)}, u32[]{:S(2)}) copy-start(s32[16]{0:T(128)} %param.11) | copy-start | bytes 196
  31.7 6.9 %copy-start.4 = (bf16[128,576]{0,1:T(8,128)(2,1)S(1)}, bf16[128,576]{0,1:T(8,128)(2,1)}, u32[]{:S(2)}) copy-start(bf16[128,576]{0,1:T(8,128)(2,1)} %param.9) | copy-start | bytes 442372
  31.9 2.4 %collective-permute-start.9 = (bf16[2,576,128]{2,1,0:T(8,128)(2,1)S(1)}, bf16[2,576,128]{2,1,0:T(8,128)(2,1)S(1)}, u32[]{:S(2)}, u32[]{:S(2)}) collective-permute-start(bf16[2,576,128]{2,1,0:T(8,128)(2,1)S(1)} %pad_maximum_fusion.1.refs_0_), channel_id=1, source_target_pairs={{0,16},{1,17},{2,18},{3,19},{4,20},{5,21},{6,22},{7,23},{8,24},{9,... | collective-permute-start | bytes 884744 | tf_op jit(solution)/shard_map/ppermute | solution.py:36
  32.0 23.9 %collective-permute-start.21 = (bf16[2,256,896]{2,1,0:T(8,128)(2,1)S(1)}, bf16[2,256,896]{2,1,0:T(8,128)(2,1)S(1)}, u32[]{:S(2)}, u32[]{:S(2)}) collective-permute-start(bf16[2,256,896]{2,1,0:T(8,128)(2,1)S(1)} %pad_maximum_fusion.refs_8_), channel_id=1, source_target_pairs={{0,64},{1,65},{2,66},{3,67},{4,68},{5,69},{6,70},{7,71},{8,72},{9,... | collective-permute-start | bytes 2752520 | tf_op jit(solution)/shard_map/ppermute | solution.py:36
  33.6 5.1 %collective-permute-start.10 = (bf16[2,576,128]{2,1,0:T(8,128)(2,1)}, bf16[2,576,128]{2,1,0:T(8,128)(2,1)}, u32[]{:S(2)}, u32[]{:S(2)}) collective-permute-start(bf16[2,576,128]{2,1,0:T(8,128)(2,1)} %collective-permute-done.5.refs_1_), channel_id=1, source_target_pairs={{0,16},{1,17},{2,18},{3,19},{4,20},{5,21},{6,22},{7,23},{8,24},{9,... | collective-permute-start | bytes 884744 | tf_op jit(solution)/shard_map/ppermute | solution.py:36
  33.8 4.9 %collective-permute-start.11 = (bf16[2,576,128]{2,1,0:T(8,128)(2,1)S(1)}, bf16[2,576,128]{2,1,0:T(8,128)(2,1)}, u32[]{:S(2)}, u32[]{:S(2)}) collective-permute-start(bf16[2,576,128]{2,1,0:T(8,128)(2,1)S(1)} %pad_maximum_fusion.2.refs_2_), channel_id=1, source_target_pairs={{0,16},{1,17},{2,18},{3,19},{4,20},{5,21},{6,22},{7,23},{8,24},{9,... | collective-permute-start | bytes 884744 | tf_op jit(solution)/shard_map/ppermute | solution.py:36
  34.1 4.6 %collective-permute-start.12 = (bf16[2,576,128]{2,1,0:T(8,128)(2,1)}, bf16[2,576,128]{2,1,0:T(8,128)(2,1)}, u32[]{:S(2)}, u32[]{:S(2)}) collective-permute-start(bf16[2,576,128]{2,1,0:T(8,128)(2,1)} %collective-permute-done.7.refs_3_), channel_id=1, source_target_pairs={{0,16},{1,17},{2,18},{3,19},{4,20},{5,21},{6,22},{7,23},{8,24},{9,... | collective-permute-start | bytes 884744 | tf_op jit(solution)/shard_map/ppermute | solution.py:36
  34.3 0.7 copy-start.2
  35.0 23.0 %collective-permute-start.20 = (bf16[2,256,896]{2,1,0:T(8,128)(2,1)S(1)}, bf16[2,256,896]{2,1,0:T(8,128)(2,1)S(1)}, u32[]{:S(2)}, u32[]{:S(2)}) collective-permute-start(bf16[2,256,896]{2,1,0:T(8,128)(2,1)S(1)} %pad_maximum_fusion.refs_8_), channel_id=1, source_target_pairs={{0,192},{1,193},{2,194},{3,195},{4,196},{5,197},{6,198},{7,199},{8... | collective-permute-start | bytes 2752520 | tf_op jit(solution)/shard_map/ppermute | solution.py:36
  38.7 1.3 %copy-start = (bf16[128,4608]{1,0:T(8,128)(2,1)S(1)}, bf16[128,4608]{1,0:T(8,128)(2,1)}, u32[]{:S(2)}) copy-start(bf16[128,4608]{1,0:T(8,128)(2,1)} %q_ref.1) | copy-start | bytes 3538948
  40.0 1.2 copy-start.1
  41.2 1.0 copy-start.3
  52.2 9.1 %collective-permute-start.17 = (bf16[4,128,256]{2,1,0:T(8,128)(2,1)S(1)}, bf16[4,128,256]{2,1,0:T(8,128)(2,1)S(1)}, u32[]{:S(2)}, u32[]{:S(2)}) collective-permute-start(bf16[4,128,256]{2,1,0:T(8,128)(2,1)S(1)} %attention.1.refs_0_), channel_id=1, source_target_pairs={{0,33},{1,32},{2,35},{3,34},{4,37},{5,36},{6,39},{7,38},{8,41},{9,... | collective-permute-start | bytes 786440 | tf_op jit(solution)/shard_map/ppermute | solution.py:36
  52.7 11.5 %collective-permute-start.16 = (bf16[4,128,256]{2,1,0:T(8,128)(2,1)S(1)}, bf16[4,128,256]{2,1,0:T(8,128)(2,1)S(1)}, u32[]{:S(2)}, u32[]{:S(2)}) collective-permute-start(bf16[4,128,256]{2,1,0:T(8,128)(2,1)S(1)} %attention.1.refs_0_), channel_id=1, source_target_pairs={{0,32},{1,33},{2,34},{3,35},{4,36},{5,37},{6,38},{7,39},{8,40},{9,... | collective-permute-start | bytes 786440 | tf_op jit(solution)/shard_map/ppermute | solution.py:36
  55.4 8.9 %collective-permute-start.14 = (bf16[4,128,256]{2,1,0:T(8,128)(2,1)S(1)}, bf16[4,128,256]{2,1,0:T(8,128)(2,1)S(1)}, u32[]{:S(2)}, u32[]{:S(2)}) collective-permute-start(bf16[4,128,256]{2,1,0:T(8,128)(2,1)S(1)} %attention.1.refs_0_), channel_id=1, source_target_pairs={{0,16},{1,17},{2,18},{3,19},{4,20},{5,21},{6,22},{7,23},{8,24},{9,... | collective-permute-start | bytes 786440 | tf_op jit(solution)/shard_map/ppermute | solution.py:36
  56.0 13.7 %collective-permute-start.13 = (bf16[4,128,256]{2,1,0:T(8,128)(2,1)S(1)}, bf16[4,128,256]{2,1,0:T(8,128)(2,1)S(1)}, u32[]{:S(2)}, u32[]{:S(2)}) collective-permute-start(bf16[4,128,256]{2,1,0:T(8,128)(2,1)S(1)} %attention.1.refs_0_), channel_id=1, source_target_pairs={{0,1},{1,0},{2,3},{3,2},{4,5},{5,4},{6,7},{7,6},{8,9},{9,8},{10,11... | collective-permute-start | bytes 786440 | tf_op jit(solution)/shard_map/ppermute | solution.py:36
  58.0 13.5 %collective-permute-start.23 = (bf16[256,896]{1,0:T(8,128)(2,1)S(1)}, bf16[256,896]{1,0:T(8,128)(2,1)S(1)}, u32[]{:S(2)}, u32[]{:S(2)}) collective-permute-start(bf16[256,896]{1,0:T(8,128)(2,1)S(1)} %slice_bitcast_fusion), channel_id=1, source_target_pairs={{0,64},{1,65},{2,66},{3,67},{4,68},{5,69},{6,70},{7,71},{8,72},{9,... | collective-permute-start | bytes 1376264 | tf_op jit(solution)/shard_map/ppermute | solution.py:36
  61.3 12.7 %collective-permute-start.22 = (bf16[256,896]{1,0:T(8,128)(2,1)S(1)}, bf16[256,896]{1,0:T(8,128)(2,1)S(1)}, u32[]{:S(2)}, u32[]{:S(2)}) collective-permute-start(bf16[256,896]{1,0:T(8,128)(2,1)S(1)} %slice_bitcast_fusion.1), channel_id=1, source_target_pairs={{0,192},{1,193},{2,194},{3,195},{4,196},{5,197},{6,198},{7,199},{8... | collective-permute-start | bytes 1376264 | tf_op jit(solution)/shard_map/ppermute | solution.py:36
  64.3 5.5 %collective-permute-start.19 = (bf16[4,128,256]{2,1,0:T(8,128)(2,1)S(1)}, bf16[4,128,256]{2,1,0:T(8,128)(2,1)S(1)}, u32[]{:S(2)}, u32[]{:S(2)}) collective-permute-start(bf16[4,128,256]{2,1,0:T(8,128)(2,1)S(1)} %collective-permute-done.17.refs_5_), channel_id=1, source_target_pairs={{0,16},{1,17},{2,18},{3,19},{4,20},{5,21},{6,22},{7,23},{8,24},{9,... | collective-permute-start | bytes 786440 | tf_op jit(solution)/shard_map/ppermute | solution.py:36
  64.3 5.5 %collective-permute-start.18 = (bf16[4,128,256]{2,1,0:T(8,128)(2,1)S(1)}, bf16[4,128,256]{2,1,0:T(8,128)(2,1)S(1)}, u32[]{:S(2)}, u32[]{:S(2)}) collective-permute-start(bf16[4,128,256]{2,1,0:T(8,128)(2,1)S(1)} %collective-permute-done.16.refs_4_), channel_id=1, source_target_pairs={{0,16},{1,17},{2,18},{3,19},{4,20},{5,21},{6,22},{7,23},{8,24},{9,... | collective-permute-start | bytes 786440 | tf_op jit(solution)/shard_map/ppermute | solution.py:36
  69.7 1.5 %collective-permute-start.15 = (bf16[4,128,256]{2,1,0:T(8,128)(2,1)S(1)}, bf16[4,128,256]{2,1,0:T(8,128)(2,1)S(1)}, u32[]{:S(2)}, u32[]{:S(2)}) collective-permute-start(bf16[4,128,256]{2,1,0:T(8,128)(2,1)S(1)} %collective-permute-done.13.refs_1_), channel_id=1, source_target_pairs={{0,16},{1,17},{2,18},{3,19},{4,20},{5,21},{6,22},{7,23},{8,24},{9,... | collective-permute-start | bytes 786440 | tf_op jit(solution)/shard_map/ppermute | solution.py:36
  78.7 13.0 %collective-permute-start.24 = (bf16[448,128]{1,0:T(8,128)(2,1)S(1)}, bf16[448,128]{1,0:T(8,128)(2,1)S(1)}, u32[]{:S(2)}, u32[]{:S(2)}) collective-permute-start(bf16[448,128]{1,0:T(8,128)(2,1)S(1)} %get-tuple-element.28), channel_id=1, source_target_pairs={{0,2},{1,3},{2,4},{3,5},{4,6},{5,7},{6,8},{7,9},{8,10},{9,11},{10,... | collective-permute-start | bytes 344072 | tf_op jit(solution)/shard_map/ppermute | solution.py:36
  80.7 13.4 %collective-permute-start.25 = (bf16[448,128]{1,0:T(8,128)(2,1)S(1)}, bf16[448,128]{1,0:T(8,128)(2,1)S(1)}, u32[]{:S(2)}, u32[]{:S(2)}) collective-permute-start(bf16[448,128]{1,0:T(8,128)(2,1)S(1)} %get-tuple-element.29), channel_id=1, source_target_pairs={{0,4},{1,5},{2,6},{3,7},{4,8},{5,9},{6,10},{7,11},{8,12},{9,13},{1... | collective-permute-start | bytes 344072 | tf_op jit(solution)/shard_map/ppermute | solution.py:36
  85.2 18.9 %collective-permute-start.26 = (bf16[448,128]{1,0:T(8,128)(2,1)S(1)}, bf16[448,128]{1,0:T(8,128)(2,1)S(1)}, u32[]{:S(2)}, u32[]{:S(2)}) collective-permute-start(bf16[448,128]{1,0:T(8,128)(2,1)S(1)} %get-tuple-element.30), channel_id=1, source_target_pairs={{0,6},{1,7},{2,8},{3,9},{4,10},{5,11},{6,12},{7,13},{8,14},{9,15},... | collective-permute-start | bytes 344072 | tf_op jit(solution)/shard_map/ppermute | solution.py:36
  87.1 17.0 %collective-permute-start.27 = (bf16[448,128]{1,0:T(8,128)(2,1)S(1)}, bf16[448,128]{1,0:T(8,128)(2,1)S(1)}, u32[]{:S(2)}, u32[]{:S(2)}) collective-permute-start(bf16[448,128]{1,0:T(8,128)(2,1)S(1)} %get-tuple-element.31), channel_id=1, source_target_pairs={{0,8},{1,9},{2,10},{3,11},{4,12},{5,13},{6,14},{7,15},{8,0},{9,1},... | collective-permute-start | bytes 344072 | tf_op jit(solution)/shard_map/ppermute | solution.py:36
  88.6 16.3 %collective-permute-start.28 = (bf16[448,128]{1,0:T(8,128)(2,1)S(1)}, bf16[448,128]{1,0:T(8,128)(2,1)S(1)}, u32[]{:S(2)}, u32[]{:S(2)}) collective-permute-start(bf16[448,128]{1,0:T(8,128)(2,1)S(1)} %get-tuple-element.32), channel_id=1, source_target_pairs={{0,10},{1,11},{2,12},{3,13},{4,14},{5,15},{6,0},{7,1},{8,2},{9,3},... | collective-permute-start | bytes 344072 | tf_op jit(solution)/shard_map/ppermute | solution.py:36
  91.7 18.1 %collective-permute-start.29 = (bf16[448,128]{1,0:T(8,128)(2,1)S(1)}, bf16[448,128]{1,0:T(8,128)(2,1)S(1)}, u32[]{:S(2)}, u32[]{:S(2)}) collective-permute-start(bf16[448,128]{1,0:T(8,128)(2,1)S(1)} %get-tuple-element.33), channel_id=1, source_target_pairs={{0,12},{1,13},{2,14},{3,15},{4,0},{5,1},{6,2},{7,3},{8,4},{9,5},{1... | collective-permute-start | bytes 344072 | tf_op jit(solution)/shard_map/ppermute | solution.py:36
  94.1 16.9 %collective-permute-start.30 = (bf16[448,128]{1,0:T(8,128)(2,1)S(1)}, bf16[448,128]{1,0:T(8,128)(2,1)S(1)}, u32[]{:S(2)}, u32[]{:S(2)}) collective-permute-start(bf16[448,128]{1,0:T(8,128)(2,1)S(1)} %get-tuple-element.34), channel_id=1, source_target_pairs={{0,14},{1,15},{2,0},{3,1},{4,2},{5,3},{6,4},{7,5},{8,6},{9,7},{10,... | collective-permute-start | bytes 344072 | tf_op jit(solution)/shard_map/ppermute | solution.py:36
  111.1 15.4 %collective-permute-start.31 = (bf16[448,128]{1,0:T(8,128)(2,1)S(1)}, bf16[448,128]{1,0:T(8,128)(2,1)S(1)}, u32[]{:S(2)}, u32[]{:S(2)}) collective-permute-start(bf16[448,128]{1,0:T(8,128)(2,1)S(1)} %add_convert_fusion), channel_id=1, source_target_pairs={{0,0},{1,2},{2,1},{3,3},{4,16},{5,18},{6,17},{7,19},{8,32},{9,34},... | collective-permute-start | bytes 344072 | tf_op jit(solution)/shard_map/ppermute | solution.py:36

commit v3 on v2

v3 whole, which is shorter than its diff:
```python
import itertools

import jax
import jax.numpy as jnp
from jax import lax
from jax.experimental import pallas as pl
from jax.experimental.pallas import tpu as pltpu
from jax.sharding import Mesh
from jax.sharding import PartitionSpec as P

LATENT = 512
ROPE = 64
WIDTH = LATENT + ROPE
NOPE = 128
SEG_LEN = 128
VHEAD = 128
HEADS_DEV = 8
ROWS = HEADS_DEV * SEG_LEN
ANC_SEGS = 16
COLS = 448
PAD = 64

NEAR = {0: (1, 0), 1: (1, 1), 7: (0, 0), 2: (0, 1)}

NEG = -1e30
LOG2E = 1.4426950408889634
SCALE = (NOPE + ROPE) ** -0.5


AXES = ("y", "xl", "c", "z", "xh")
SEG, HEAD = AXES[:3], AXES[3:]


def seg_of(y, xl, c):
    return y * 4 + xl * 2 + c


def move(x, to):
    pairs = []
    for y, xl, c, z, xh in itertools.product(range(4), range(2), range(2), range(8), range(2)):
        ty, txl, tc, tz, txh = to(y, xl, c, z, xh)
        pairs.append((seg_of(y, xl, c) * 16 + z * 2 + xh, seg_of(ty, txl, tc) * 16 + tz * 2 + txh))
    return lax.ppermute(x, AXES, pairs)


def swap_core(x):
    return move(x, lambda y, xl, c, z, xh: (y, xl, 1 - c, z, xh))


def swap_x(x, a, b):
    return move(x, lambda y, xl, c, z, xh: (y, xl ^ a, c, z, xh ^ b))


def from_y(x, r):
    return move(x, lambda y, xl, c, z, xh: ((y - r) % 4, xl, c, z, xh))


def to_z(x, k):
    return move(x, lambda y, xl, c, z, xh: (y, xl, c, (z + k) % 8, xh))


def to_owner(x, k):
    def to(y, xl, c, z, xh):
        for half in range(2):
            owner = xl * 2 + c + 4 * half
            step = (z + k - owner) % 8
            if step in NEAR:
                return (y, xl ^ NEAR[step][0], c ^ NEAR[step][1], owner, xh)

    return move(x, to)


def cut_kernel(meta, w_ref, keep_ref, other_ref):
    for c in range(2):

        @pl.when(meta[2] == c)
        def _(c=c):
            for core, ref in ((c, keep_ref), (1 - c, other_ref)):
                for xl in range(2):
                    for xh in range(2):
                        for half in range(2):
                            start = ((xl * 2 + core + 4 * half) * 2 + xh) * COLS
                            cols = slice(half * COLS, (half + 1) * COLS)
                            ref[xl, xh, :, :, cols] = w_ref[:, :, start : start + COLS]


def small_call(kernel, name, shapes, *args):
    vmem = pl.BlockSpec(memory_space=pltpu.VMEM)
    return pl.pallas_call(
        kernel,
        out_shape=[jax.ShapeDtypeStruct(x, jnp.bfloat16) for x in shapes],
        in_specs=[pl.BlockSpec(memory_space=pltpu.SMEM)] + [vmem] * (len(args) - 1),
        out_specs=[vmem] * len(shapes),
        cost_estimate=pl.CostEstimate(flops=0, bytes_accessed=2 * 2**20, transcendentals=0),
        name=name,
    )(*args)


def attention_kernel(meta, q_hbm, own_ref, *refs):
    anc_refs = refs[:8]
    up_hbm, out_ref, keys, scores, top, total, accum, up_ref, q_ref, mixed, where_ref, sems = refs[8:]
    y, xl, c = meta[18], meta[19], meta[20]
    length = meta[17]
    q_copy = pltpu.make_async_copy(q_hbm, q_ref, sems.at[0])
    q_copy.start()

    for slot in range(ANC_SEGS):
        where_ref[slot] = 0

    def walk(step, current):
        @pl.when(current >= 0)
        def _():
            rel_y = lax.bitwise_and((current >> 2) - y + 4, 3)
            rel_x = lax.bitwise_xor(lax.bitwise_and(current >> 1, 1), xl)
            rel_c = lax.bitwise_xor(lax.bitwise_and(current, 1), c)
            where_ref[rel_c * 8 + rel_y * 2 + rel_x] = 1

        return jnp.where(current >= 0, meta[jnp.maximum(current, 0)], -1)

    lax.fori_loop(0, ANC_SEGS, walk, meta[16])

    keys[0, PAD : PAD + WIDTH] = own_ref[...]
    end = jnp.int32(1)
    for slot in range(ANC_SEGS):
        used = where_ref[slot]

        @pl.when(used == 1)
        def _(slot=slot, place=end):
            keys[place, PAD : PAD + WIDTH] = anc_refs[slot // 2][slot % 2]

        end = end + used
    keys[end, PAD : PAD + WIDTH] = own_ref[...]

    up_copy = pltpu.make_async_copy(up_hbm, up_ref, sems.at[1])
    up_copy.start()
    keys[:, :PAD] = jnp.zeros((ANC_SEGS + 2, PAD, SEG_LEN), jnp.bfloat16)
    keys[:, PAD + WIDTH :] = jnp.zeros((ANC_SEGS + 2, PAD, SEG_LEN), jnp.bfloat16)
    q_copy.wait()
    pairs = (end + 1) // 2

    def queries(odd):
        starts = [h * WIDTH - PAD * odd for h in range(odd, HEADS_DEV, 2)]
        return jnp.concatenate([q_ref[:, s : s + WIDTH + PAD] for s in starts], axis=0)

    def score(j):
        pair = jnp.concatenate([keys[2 * j], keys[2 * j + 1]], axis=1)
        even = jnp.dot(queries(0), pair[PAD:], preferred_element_type=jnp.float32)
        odd = jnp.dot(queries(1), pair[: WIDTH + PAD], preferred_element_type=jnp.float32)
        s = jnp.concatenate([even, odd], axis=0)
        return s[:, :SEG_LEN], s[:, SEG_LEN:]

    row = lax.broadcasted_iota(jnp.int32, (ROWS, SEG_LEN), 0) & (SEG_LEN - 1)
    col = lax.broadcasted_iota(jnp.int32, (ROWS, SEG_LEN), 1)
    left, right = score(0)
    left = jnp.where((col <= row) & (col < length), left, NEG)
    scores[0, :, :SEG_LEN] = left
    scores[0, :, SEG_LEN:] = right
    top[...] = jnp.maximum(left, right)

    def first(j, carry):
        left, right = score(j)
        right = jnp.where(2 * j + 1 < end, right, NEG)
        scores[j, :, :SEG_LEN] = left
        scores[j, :, SEG_LEN:] = right
        top[...] = jnp.maximum(top[...], jnp.maximum(left, right))
        return carry

    lax.fori_loop(1, pairs, first, 0)
    factor = SCALE * LOG2E
    high = jnp.max(top[...], axis=1, keepdims=True)
    top[...] = jnp.broadcast_to(high, (ROWS, SEG_LEN))
    total[...] = jnp.zeros_like(total)
    accum[...] = jnp.zeros_like(accum)

    def second(j, carry):
        high = top[...]
        left = jnp.exp2((scores[j, :, :SEG_LEN] - high) * factor)
        right = jnp.exp2((scores[j, :, SEG_LEN:] - high) * factor)
        total[...] += left + right
        weight = jnp.concatenate([left, right], axis=1).astype(jnp.bfloat16)
        values = pl.ds(PAD, LATENT)
        pair = jnp.concatenate([keys[2 * j, values], keys[2 * j + 1, values]], axis=1)
        accum[...] += lax.dot_general(
            weight, pair, (((1,), (1,)), ((), ())), preferred_element_type=jnp.float32
        )
        return carry

    lax.fori_loop(0, pairs, second, 0)
    up_copy.wait()
    pos = lax.broadcasted_iota(jnp.int32, (SEG_LEN, VHEAD), 0)
    for h in range(HEADS_DEV):
        at = (h % 2) * (HEADS_DEV // 2) + h // 2
        rows = slice(at * SEG_LEN, (at + 1) * SEG_LEN)
        denominator = jnp.sum(total[rows], axis=1, keepdims=True)
        latent_out = (accum[rows] / denominator).astype(jnp.bfloat16)
        head_out = jnp.dot(latent_out, up_ref[h], preferred_element_type=jnp.float32)
        head_out = jnp.where(pos < length, head_out, 0.0).astype(jnp.bfloat16)
        for block in range(4):
            rel = lax.bitwise_and(block - y + 4, 3)
            mixed[rel, :, h * 32 : (h + 1) * 32] = head_out[:, block * 32 : (block + 1) * 32]
    for copy in range(4):
        out_ref[copy] = mixed[...]


def attention(meta, q, own, anc, up):
    vmem = pl.BlockSpec(memory_space=pltpu.VMEM)
    hbm = pl.BlockSpec(memory_space=pltpu.HBM)
    return pl.pallas_call(
        attention_kernel,
        out_shape=jax.ShapeDtypeStruct((4, 4, SEG_LEN, 256), jnp.bfloat16),
        in_specs=[pl.BlockSpec(memory_space=pltpu.SMEM), hbm] + [vmem] * 9 + [hbm],
        out_specs=vmem,
        scratch_shapes=[
            pltpu.VMEM((ANC_SEGS + 2, WIDTH + 2 * PAD, SEG_LEN), jnp.bfloat16),
            pltpu.VMEM((9, ROWS, 2 * SEG_LEN), jnp.float32),
            pltpu.VMEM((ROWS, SEG_LEN), jnp.float32),
            pltpu.VMEM((ROWS, SEG_LEN), jnp.float32),
            pltpu.VMEM((ROWS, LATENT), jnp.float32),
            pltpu.VMEM((HEADS_DEV, LATENT, VHEAD), jnp.bfloat16),
            pltpu.VMEM((SEG_LEN, HEADS_DEV * WIDTH), jnp.bfloat16),
            pltpu.VMEM((4, SEG_LEN, 256), jnp.bfloat16),
            pltpu.SMEM((ANC_SEGS,), jnp.int32),
            pltpu.SemaphoreType.DMA((2,)),
        ],
        compiler_params=pltpu.CompilerParams(vmem_limit_bytes=51 * 2**20),
        cost_estimate=pl.CostEstimate(
            flops=10**6, bytes_accessed=2**16, transcendentals=0
        ),
        name="attention",
    )(meta, q, own, *anc, up)


def project_kernel(meta, *refs):
    heads = refs[:2]
    w0, w1, w3, w2a, w2b = refs[2:7]
    outs = refs[7:13]
    left, partial = refs[13:]
    xl, c, z, xh = meta[19], meta[20], meta[21], meta[22]
    weights = [[w0.at[0], w1.at[0], w2a, w3.at[0]], [w0.at[1], w1.at[1], w2b, w3.at[1]]]
    for b in range(2):
        for t in range(4):
            source = lax.bitwise_xor(xl, t // 2) * 2 + lax.bitwise_xor(xh, b)
            for r in range(4):
                cols = slice(b * 1024 + r * 256, b * 1024 + r * 256 + 256)
                left[t * SEG_LEN : (t + 1) * SEG_LEN, cols] = heads[t % 2][source, r]
    for n in range(7):
        cols = slice(n * 128, (n + 1) * 128)
        value = None
        for b in range(2):
            for r in range(4):
                term = jnp.dot(
                    left[:, b * 1024 + r * 256 : b * 1024 + r * 256 + 256],
                    weights[b][r][:, cols],
                    preferred_element_type=jnp.float32,
                )
                value = term if value is None else value + term
        for t in range(4):
            partial[t, cols] = value[t * SEG_LEN : (t + 1) * SEG_LEN].T.astype(jnp.bfloat16)
    places = {0: (0, None), 1: (1, 0), 3: (1, 1), 7: (2, 0), 5: (2, 1), 4: (3, None), 2: (4, None), 6: (5, None)}
    for k, (out, part) in places.items():
        step = lax.bitwise_and(z + k - xl * 2 - c, 7)
        upper = (step >= 3) & (step <= 6)
        near = lax.bitwise_and(jnp.where(upper, step - 4, step), 7)
        t = sum(jnp.where(near == n, a * 2 + d, 0) for n, (a, d) in NEAR.items())
        ref = outs[out] if part is None else outs[out].at[part]

        @pl.when(jnp.logical_not(upper))
        def _(ref=ref, t=t):
            ref[...] = partial[t, :COLS]

        @pl.when(upper)
        def _(ref=ref, t=t):
            ref[...] = partial[t, COLS:]


def project(meta, heads, weights):
    vmem = pl.BlockSpec(memory_space=pltpu.VMEM)
    one = jax.ShapeDtypeStruct((COLS, SEG_LEN), jnp.bfloat16)
    two = jax.ShapeDtypeStruct((2, COLS, SEG_LEN), jnp.bfloat16)
    return pl.pallas_call(
        project_kernel,
        out_shape=[one, two, two, one, one, one],
        in_specs=[pl.BlockSpec(memory_space=pltpu.SMEM)] + [vmem] * 7,
        out_specs=[vmem] * 6,
        scratch_shapes=[
            pltpu.VMEM((4 * SEG_LEN, 2048), jnp.bfloat16),
            pltpu.VMEM((4, 2 * COLS, SEG_LEN), jnp.bfloat16),
        ],
        compiler_params=pltpu.CompilerParams(vmem_limit_bytes=20 * 2**20),
        cost_estimate=pl.CostEstimate(
            flops=10**6, bytes_accessed=2**16, transcendentals=0
        ),
        name="project",
    )(meta, *heads, *weights)


def per_device(
    queries,
    leaf_latent,
    ancestor_latent,
    ancestor_parent,
    leaf_parent,
    leaf_length,
    value_up,
    out_weight,
):
    y, xl, c, z, xh = [lax.axis_index(name) for name in AXES]
    place = jnp.stack([y, xl, c, z, xh]).astype(jnp.int32)
    meta = jnp.concatenate([ancestor_parent, leaf_parent, leaf_length, place])

    mine = ancestor_latent.T
    column = jnp.stack([mine, swap_x(mine, 1, 0)])

    keep, other = small_call(cut_kernel, "cut", [(2, 2, HEADS_DEV, 8, 2 * COLS)] * 2, place, out_weight)
    other = swap_core(other)
    cores = jnp.where(c == 0, jnp.stack([keep, other], 3), jnp.stack([other, keep], 3))

    def for_x(a, b):
        part = lax.dynamic_index_in_dim(cores, xl ^ a, 0, keepdims=False)
        return lax.dynamic_index_in_dim(part, xh ^ b, 0, keepdims=False)

    w00, w10, w11 = for_x(0, 0), swap_x(for_x(1, 0), 1, 0), swap_x(for_x(1, 1), 1, 1)
    w01, _ = lax.optimization_barrier((for_x(0, 1), w10))
    w01 = swap_x(w01, 0, 1)
    anc = [column] + [from_y(column, r) for r in (1, 2, 3)]
    w0, _ = lax.optimization_barrier(([[w00, w01], [w10, w11]], anc))
    anc = anc + [swap_core(x) for x in anc]

    w0 = [jnp.stack(x) for x in w0]
    w0 = jnp.where(xl == 0, jnp.stack(w0, 2), jnp.stack(w0[::-1], 2)).reshape(2, 256, 2 * COLS)
    w1, w3 = from_y(w0, 1), from_y(w0, 3)
    w2a, w2b = w1[0], w3[1]

    head_out = attention(meta, queries, leaf_latent.T, anc, value_up)

    w2a, w2b, _ = lax.optimization_barrier((w2a, w2b, head_out))
    w2a, w2b = from_y(w2a, 1), from_y(w2b, 3)
    heads = lax.all_to_all(head_out, ("xl", "xh"), 0, 0)
    heads, w2a, w2b = lax.optimization_barrier((heads, w2a, w2b))
    heads = (heads, swap_core(heads))
    mine, right, left, far, right2, left2 = project(meta, heads, (w0, w1, w3, w2a, w2b))
    right, left = to_z(right, 1), to_z(left, -1)
    far = move(far, lambda y, xl, c, z, xh: (y, xl, c, (z + 2 - 4 * c) % 8, xh))

    def f32(x):
        return x.astype(jnp.float32)

    mine = f32(mine) + f32(right[0]) + f32(left[0])
    right2 = f32(right2) + f32(right[1]) + jnp.where(c == 0, f32(far), 0.0)
    left2 = f32(left2) + f32(left[1]) + jnp.where(c == 1, f32(far), 0.0)
    terms = [to_owner(x.astype(jnp.bfloat16), k) for x, k in ((mine, 0), (right2, 2), (left2, -2))]
    return (f32(terms[0]) + f32(terms[1]) + f32(terms[2])).astype(jnp.bfloat16).T


def solution(mesh):
    mesh = Mesh(mesh.devices.reshape(4, 2, 2, 8, 2), AXES)
    return jax.shard_map(
        per_device,
        mesh=mesh,
        in_specs=(
            P(SEG, HEAD),
            P(SEG, None),
            P(SEG, None),
            P(),
            P(SEG),
            P(SEG),
            P(HEAD, None, None),
            P(HEAD, SEG, None),
        ),
        out_specs=P(SEG, HEAD),
        check_vma=False,
    )
```

time: 129 us -> 112 us (0.87)
  the two profiles are of different devices: /device:TPU:42 before, /device:TPU:68 now
where the time goes in v3:
time: 112 us; the launch traced here: 111 us
  waiting for transfers between devices  42 us (38%)
  starting transfers between devices  39.6 us (35%)
  Pallas kernels  20 us (18%)
  local copies, waits for them, and re-layouts  4.9 us (4%)
  other arithmetic  3.4 us (3%)
  between operations  1.44 us (1%)
    ppermute x23, starting transfers between devices, move(): return lax.ppermute(x, AXES, pairs)  34.5 us
    ppermute x23, waiting for transfers between devices, move(): return lax.ppermute(x, AXES, pairs)  34 us
    pallas_call x1, Pallas kernels, attention(): pl.pallas_call(attention_kernel, out_shape=jax.ShapeDtypeStruct((4, 4, SE...  11.4 us
    all_to_all x1, waiting for transfers between devices, per_device(): heads = lax.all_to_all(head_out, ('xl', 'xh'), 0, 0)  7.96 us
    pallas_call x1, Pallas kernels, project(): pl.pallas_call(project_kernel, out_shape=[one, two, two, one, one, one],...  6.31 us
    all_to_all x1, starting transfers between devices, per_device(): heads = lax.all_to_all(head_out, ('xl', 'xh'), 0, 0)  5.07 us
    squeeze x2, local copies, waits for them, and re-layouts, per_device(): w2a, w2b = (w1[0], w3[1])  2.66 us
    pallas_call x1, Pallas kernels, small_call(): pl.pallas_call(kernel, out_shape=[jax.ShapeDtypeStruct(x, jnp.bfloat16) f...  2.34 us
  transfers between devices with their start and end apart: 24, of which 14 were waited for; matrix products, arithmetic and copies ran while one was open for 4% of the time, Pallas kernels for 10%

profile of v3, /device:TPU:68, one launch (start us, length us, event | category | flops | bytes accessed | tf_op | source)
XLA Modules:
  0.0 111.4 jit_solution(17447465502773445203)
XLA Ops:
  0.0 0.6 stack.81.meta
  0.6 2.3 %cut.1 = (bf16[2,2,8,8,896]{4,3,2,1,0:T(8,128)(2,1)}, bf16[2,2,8,8,896]{4,3,2,1,0:T(8,128)(2,1)}) custom-call(s32[5]{0:T(128)} %stack.81.meta, bf16[8,8,7168]{2,1,0:T(8,128)(2,1)} %w_ref.1), custom_call_target="tpu_custom_call" | custom-call | bytes 2097152 | tf_op jit(solution)/shard_map/cut/pallas_call | solution.py:89
  2.9 1.2 %collective-permute-start = (bf16[576,128]{1,0:T(8,128)(2,1)}, bf16[576,128]{1,0:T(8,128)(2,1)S(1)}, u32[]{:S(2)}, u32[]{:S(2)}) collective-permute-start(bf16[576,128]{1,0:T(8,128)(2,1)} %bitcast.72), channel_id=1, source_target_pairs={{0,32},{1,33},{2,34},{3,35},{4,36},{5,37},{6,38},{7,39},{8,40},{9,... | collective-permute-start | bytes 442376 | tf_op jit(solution)/shard_map/ppermute | solution.py:43
  4.1 0.8 collective-permute-done.8
  5.0 1.3 %maximum_select_fusion = bf16[2,2,8,2,8,896]{5,4,2,1,0,3:T(8,128)(2,1)S(1)} fusion(bf16[2,2,8,1,8,896]{5,4,2,1,0,3:T(8,128)(2,1)S(1)} %bitcast.65, bf16[2,2,8,1,8,896]{5,4,2,1,0,3:T(8,128)(2,1)} %bitcast.64, pred[]{:T(512)S(6)} %eq.11), kind=kLoop, calls=%fused_computation | loop fusion | flops 1376256 | bytes 1835009 | tf_op jit(solution)/shard_map/jit(_where)/select_n | solution.py:316
  6.3 0.1 constant_dynamic-slice_fusion
  6.4 1.3 %collective-permute-start.9 = (bf16[8,2,8,896]{3,2,1,0:T(8,128)(2,1)S(1)}, bf16[8,2,8,896]{3,2,1,0:T(8,128)(2,1)S(1)}, u32[]{:S(2)}, u32[]{:S(2)}) collective-permute-start(bf16[8,2,8,896]{3,2,1,0:T(8,128)(2,1)S(1)} %bitcast.70), channel_id=1, source_target_pairs={{0,32},{1,33},{2,34},{3,35},{4,36},{5,37},{6,38},{7,39},{8,40},{9,... | collective-permute-start | bytes 688136 | tf_op jit(solution)/shard_map/ppermute | solution.py:43
  7.7 1.8 %collective-permute-done = bf16[576,128]{1,0:T(8,128)(2,1)S(1)} collective-permute-done((bf16[576,128]{1,0:T(8,128)(2,1)}, bf16[576,128]{1,0:T(8,128)(2,1)S(1)}, u32[]{:S(2)}, u32[]{:S(2)}) %collective-permute-start) | collective-permute-done | bytes 147488 | tf_op jit(solution)/shard_map/ppermute | solution.py:43
  9.6 1.7 %collective-permute-start.3 = (bf16[2,576,128]{2,1,0:T(8,128)(2,1)S(1)}, bf16[2,576,128]{2,1,0:T(8,128)(2,1)S(1)}, u32[]{:S(2)}, u32[]{:S(2)}) collective-permute-start(bf16[2,576,128]{2,1,0:T(8,128)(2,1)S(1)} %pad_maximum_fusion.refs_0_), channel_id=1, source_target_pairs={{0,64},{1,65},{2,66},{3,67},{4,68},{5,69},{6,70},{7,71},{8,72},{9,... | collective-permute-start | bytes 884744 | tf_op jit(solution)/shard_map/ppermute | solution.py:43
  11.2 2.9 %collective-permute-start.2 = (bf16[2,576,128]{2,1,0:T(8,128)(2,1)S(1)}, bf16[2,576,128]{2,1,0:T(8,128)(2,1)S(1)}, u32[]{:S(2)}, u32[]{:S(2)}) collective-permute-start(bf16[2,576,128]{2,1,0:T(8,128)(2,1)S(1)} %pad_maximum_fusion.refs_0_), channel_id=1, source_target_pairs={{0,128},{1,129},{2,130},{3,131},{4,132},{5,133},{6,134},{7,135},{8... | collective-permute-start | bytes 884744 | tf_op jit(solution)/shard_map/ppermute | solution.py:43
  14.1 1.3 %collective-permute-start.1 = (bf16[2,576,128]{2,1,0:T(8,128)(2,1)S(1)}, bf16[2,576,128]{2,1,0:T(8,128)(2,1)S(1)}, u32[]{:S(2)}, u32[]{:S(2)}) collective-permute-start(bf16[2,576,128]{2,1,0:T(8,128)(2,1)S(1)} %pad_maximum_fusion.refs_0_), channel_id=1, source_target_pairs={{0,192},{1,193},{2,194},{3,195},{4,196},{5,197},{6,198},{7,199},{8... | collective-permute-start | bytes 884744 | tf_op jit(solution)/shard_map/ppermute | solution.py:43
  15.5 0.6 collective-permute-start.11
  16.1 2.7 %collective-permute-start.10 = (bf16[8,2,8,896]{3,2,1,0:T(8,128)(2,1)S(1)}, bf16[8,2,8,896]{3,2,1,0:T(8,128)(2,1)S(1)}, u32[]{:S(2)}, u32[]{:S(2)}) collective-permute-start(bf16[8,2,8,896]{3,2,1,0:T(8,128)(2,1)S(1)} %bitcast.69), channel_id=1, source_target_pairs={{0,1},{1,0},{2,3},{3,2},{4,5},{5,4},{6,7},{7,6},{8,9},{9,8},{10,11... | collective-permute-start | bytes 688136 | tf_op jit(solution)/shard_map/ppermute | solution.py:43
  18.9 0.8 collective-permute-done.3.refs_3_
  19.6 7.3 %collective-permute-done.2.refs_2_ = bf16[2,576,128]{2,1,0:T(8,128)(2,1)S(1)} collective-permute-done((bf16[2,576,128]{2,1,0:T(8,128)(2,1)S(1)}, bf16[2,576,128]{2,1,0:T(8,128)(2,1)S(1)}, u32[]{:S(2)}, u32[]{:S(2)}) %collective-permute-start.2) | collective-permute-done | bytes 294944 | tf_op jit(solution)/shard_map/ppermute | solution.py:43
  27.0 0.1 maximum_bitcast_fusion
  27.1 0.2 maximum_select_fusion.1
  27.3 1.3 %collective-permute-start.13 = (bf16[2,256,896]{2,1,0:T(8,128)(2,1)S(1)}, bf16[2,256,896]{2,1,0:T(8,128)(2,1)S(1)}, u32[]{:S(2)}, u32[]{:S(2)}) collective-permute-start(bf16[2,256,896]{2,1,0:T(8,128)(2,1)S(1)} %bitcast.59), channel_id=1, source_target_pairs={{0,64},{1,65},{2,66},{3,67},{4,68},{5,69},{6,70},{7,71},{8,72},{9,... | collective-permute-start | bytes 2752520 | tf_op jit(solution)/shard_map/ppermute | solution.py:43
  28.6 2.0 %collective-permute-start.12 = (bf16[2,256,896]{2,1,0:T(8,128)(2,1)S(1)}, bf16[2,256,896]{2,1,0:T(8,128)(2,1)}, u32[]{:S(2)}, u32[]{:S(2)}) collective-permute-start(bf16[2,256,896]{2,1,0:T(8,128)(2,1)S(1)} %bitcast.60), channel_id=1, source_target_pairs={{0,192},{1,193},{2,194},{3,195},{4,196},{5,197},{6,198},{7,199},{8... | collective-permute-start | bytes 2752520 | tf_op jit(solution)/shard_map/ppermute | solution.py:43
  30.7 0.5 collective-permute-start.7
  31.2 1.5 %collective-permute-done.4.refs_4_ = bf16[2,576,128]{2,1,0:T(8,128)(2,1)S(1)} collective-permute-done((bf16[2,576,128]{2,1,0:T(8,128)(2,1)S(1)}, bf16[2,576,128]{2,1,0:T(8,128)(2,1)S(1)}, u32[]{:S(2)}, u32[]{:S(2)}) %collective-permute-start.4) | collective-permute-done | bytes 294944 | tf_op jit(solution)/shard_map/ppermute | solution.py:43
  32.6 0.1 collective-permute-start.5
  34.1 0.1 concatenate.4.meta
  34.2 0.2 collective-permute-done.5.refs_5_
  34.3 11.4 %attention.1 = bf16[4,4,128,256]{3,2,1,0:T(8,128)(2,1)} custom-call(s32[23]{0:T(128)S(1)} %concatenate.4.meta, bf16[128,4608]{1,0:T(8,128)(2,1)} %q_hbm.1, bf16[576,128]{1,0:T(8,128)(2,1)S(1)} %bitcast.62, bf16[2,576,128]{2,1,0:T(8,128)(2,1)S(1)} %pad_maximum_fusion.refs_0_, bf16[2,576,128]{2,1,0:T(8,128)(2,1)S(1)} %collective-permute-done.1.refs_1_, ...), custom_call_target="tpu_custom_call" | custom-call | flops 1000000 | bytes 65536 | tf_op jit(solution)/shard_map/attention/pallas_call | solution.py:208
  45.7 5.1 %all-to-all-start = ((bf16[4,4,128,256]{3,2,1,0:T(8,128)(2,1)}), bf16[4,4,128,256]{3,2,1,0:T(8,128)(2,1)S(1)}, u32[]{:S(2)}, u32[]{:S(2)}) async-start(bf16[4,4,128,256]{3,2,1,0:T(8,128)(2,1)} %attention.1), calls=%async_computation | async-start | bytes 2097152 | tf_op jit(solution)/shard_map/all_to_all | solution.py:338
  50.8 0.8 slice_bitcast_fusion
  51.6 1.8 %slice_bitcast_fusion.1 = bf16[256,896]{1,0:T(8,128)(2,1)} fusion(bf16[2,256,896]{2,1,0:T(8,128)(2,1)} %collective-permute-done.12.refs_3_), kind=kLoop, calls=%fused_computation.3 | loop fusion | bytes 917504 | tf_op jit(solution)/shard_map/squeeze | solution.py:332
  53.5 1.6 %collective-permute-start.14 = (bf16[256,896]{1,0:T(8,128)(2,1)}, bf16[256,896]{1,0:T(8,128)(2,1)S(1)}, u32[]{:S(2)}, u32[]{:S(2)}) collective-permute-start(bf16[256,896]{1,0:T(8,128)(2,1)} %slice_bitcast_fusion.1), channel_id=1, source_target_pairs={{0,192},{1,193},{2,194},{3,195},{4,196},{5,197},{6,198},{7,199},{8... | collective-permute-start | bytes 1376264 | tf_op jit(solution)/shard_map/ppermute | solution.py:43
  55.1 0.4 collective-permute-start.15
  55.5 8.0 %all-to-all-done.refs_0_ = bf16[4,4,128,256]{3,2,1,0:T(8,128)(2,1)S(1)} async-done(((bf16[4,4,128,256]{3,2,1,0:T(8,128)(2,1)}), bf16[4,4,128,256]{3,2,1,0:T(8,128)(2,1)S(1)}, u32[]{:S(2)}, u32[]{:S(2)}) %all-to-all-start) | async-done | bytes 1048608 | tf_op jit(solution)/shard_map/all_to_all | solution.py:338
  63.4 1.8 %collective-permute-done.14.refs_5_ = bf16[256,896]{1,0:T(8,128)(2,1)S(1)} collective-permute-done((bf16[256,896]{1,0:T(8,128)(2,1)}, bf16[256,896]{1,0:T(8,128)(2,1)S(1)}, u32[]{:S(2)}, u32[]{:S(2)}) %collective-permute-start.14) | collective-permute-done | bytes 458784 | tf_op jit(solution)/shard_map/ppermute | solution.py:43
  65.2 2.2 %collective-permute-done.15.refs_6_ = bf16[256,896]{1,0:T(8,128)(2,1)} collective-permute-done((bf16[256,896]{1,0:T(8,128)(2,1)}, bf16[256,896]{1,0:T(8,128)(2,1)}, u32[]{:S(2)}, u32[]{:S(2)}) %collective-permute-start.15) | collective-permute-done | bytes 458784 | tf_op jit(solution)/shard_map/ppermute | solution.py:43
  67.5 2.7 %collective-permute-done.16.refs_1_ = bf16[4,4,128,256]{3,2,1,0:T(8,128)(2,1)S(1)} collective-permute-done((bf16[4,4,128,256]{3,2,1,0:T(8,128)(2,1)S(1)}, bf16[4,4,128,256]{3,2,1,0:T(8,128)(2,1)S(1)}, u32[]{:S(2)}, u32[]{:S(2)}) %collective-permute-start.16) | collective-permute-done | bytes 1048608 | tf_op jit(solution)/shard_map/ppermute | solution.py:43
  70.1 6.3 %project.1 = (bf16[448,128]{1,0:T(8,128)(2,1)S(1)}, bf16[2,448,128]{2,1,0:T(8,128)(2,1)}, bf16[2,448,128]{2,1,0:T(8,128)(2,1)}, bf16[448,128]{1,0:T(8,128)(2,1)}...) custom-call(s32[23]{0:T(128)S(1)} %concatenate.4.meta, bf16[4,4,128,256]{3,2,1,0:T(8,128)(2,1)S(1)} %all-to-all-done.refs_0_, ...), custom_call_target="tpu_custom_call" | custom-call | flops 1000000 | bytes 65536 | tf_op jit(solution)/shard_map/project/pallas_call | solution.py:280
  76.4 0.6 copy-done.1
  77.1 0.6 copy-done.2
  77.7 1.9 %collective-permute-start.17 = (bf16[2,448,128]{2,1,0:T(8,128)(2,1)}, bf16[2,448,128]{2,1,0:T(8,128)(2,1)S(1)}, u32[]{:S(2)}, u32[]{:S(2)}) collective-permute-start(bf16[2,448,128]{2,1,0:T(8,128)(2,1)} %get-tuple-element.36), channel_id=1, source_target_pairs={{0,2},{1,3},{2,4},{3,5},{4,6},{5,7},{6,8},{7,9},{8,10},{9,11},{10,... | collective-permute-start | bytes 688136 | tf_op jit(solution)/shard_map/ppermute | solution.py:43
  79.6 0.1 collective-permute-start.18
  79.8 5.7 %collective-permute-start.20 = (bf16[448,128]{1,0:T(8,128)(2,1)}, bf16[448,128]{1,0:T(8,128)(2,1)S(1)}, u32[]{:S(2)}, u32[]{:S(2)}) collective-permute-start(bf16[448,128]{1,0:T(8,128)(2,1)} %get-tuple-element.39), channel_id=1, source_target_pairs={{0,4},{1,5},{2,6},{3,7},{4,8},{5,9},{6,10},{7,11},{8,12},{9,13},{1... | collective-permute-start | bytes 344072 | tf_op jit(solution)/shard_map/ppermute | solution.py:43
  85.4 3.0 %collective-permute-done.20 = bf16[448,128]{1,0:T(8,128)(2,1)S(1)} collective-permute-done((bf16[448,128]{1,0:T(8,128)(2,1)}, bf16[448,128]{1,0:T(8,128)(2,1)S(1)}, u32[]{:S(2)}, u32[]{:S(2)}) %collective-permute-start.20) | collective-permute-done | bytes 114720 | tf_op jit(solution)/shard_map/ppermute | solution.py:43
  88.4 1.0 collective-permute-done.18
  89.4 1.1 fusion.4
  90.5 1.6 %collective-permute-start.19 = (bf16[448,128]{1,0:T(8,128)(2,1)S(1)}, bf16[448,128]{1,0:T(8,128)(2,1)S(1)}, u32[]{:S(2)}, u32[]{:S(2)}) collective-permute-start(bf16[448,128]{1,0:T(8,128)(2,1)S(1)} %get-tuple-element.45), channel_id=1, source_target_pairs={{0,32},{1,33},{2,48},{3,49},{4,16},{5,17},{6,8},{7,9},{8,40},{9,41... | collective-permute-start | bytes 344072 | tf_op jit(solution)/shard_map/ppermute | solution.py:43
  92.1 7.5 %collective-permute-start.21 = (bf16[448,128]{1,0:T(8,128)(2,1)S(1)}, bf16[448,128]{1,0:T(8,128)(2,1)S(1)}, u32[]{:S(2)}, u32[]{:S(2)}) collective-permute-start(bf16[448,128]{1,0:T(8,128)(2,1)S(1)} %get-tuple-element.46), channel_id=1, source_target_pairs={{0,16},{1,17},{2,8},{3,9},{4,40},{5,41},{6,56},{7,57},{8,24},{9,25... | collective-permute-start | bytes 344072 | tf_op jit(solution)/shard_map/ppermute | solution.py:43
  99.6 3.4 %collective-permute-done.21 = bf16[448,128]{1,0:T(8,128)(2,1)S(1)} collective-permute-done((bf16[448,128]{1,0:T(8,128)(2,1)S(1)}, bf16[448,128]{1,0:T(8,128)(2,1)S(1)}, u32[]{:S(2)}, u32[]{:S(2)}) %collective-permute-start.21) | collective-permute-done | bytes 114720 | tf_op jit(solution)/shard_map/ppermute | solution.py:43
  103.0 7.7 %collective-permute-done.22 = bf16[448,128]{1,0:T(8,128)(2,1)S(1)} collective-permute-done((bf16[448,128]{1,0:T(8,128)(2,1)S(1)}, bf16[448,128]{1,0:T(8,128)(2,1)S(1)}, u32[]{:S(2)}, u32[]{:S(2)}) %collective-permute-start.22) | collective-permute-done | bytes 114720 | tf_op jit(solution)/shard_map/ppermute | solution.py:43
  110.7 0.7 fusion.5
  (29 shorter events, 0.2 us)
Async XLA Ops:
  2.9 2.0 %collective-permute-start.8 = (bf16[2,2,8,8,896]{4,3,2,1,0:T(8,128)(2,1)}, bf16[2,2,8,8,896]{4,3,2,1,0:T(8,128)(2,1)S(1)}, u32[]{:S(2)}, u32[]{:S(2)}) collective-permute-start(bf16[2,2,8,8,896]{4,3,2,1,0:T(8,128)(2,1)} %get-tuple-element.24), channel_id=1, source_target_pairs={{0,16},{1,17},{2,18},{3,19},{4,20},{5,21},{6,22},{7,23},{8,24},{9,... | collective-permute-start | bytes 1376264 | tf_op jit(solution)/shard_map/ppermute | solution.py:43
  2.9 6.6 %collective-permute-start = (bf16[576,128]{1,0:T(8,128)(2,1)}, bf16[576,128]{1,0:T(8,128)(2,1)S(1)}, u32[]{:S(2)}, u32[]{:S(2)}) collective-permute-start(bf16[576,128]{1,0:T(8,128)(2,1)} %bitcast.72), channel_id=1, source_target_pairs={{0,32},{1,33},{2,34},{3,35},{4,36},{5,37},{6,38},{7,39},{8,40},{9,... | collective-permute-start | bytes 442376 | tf_op jit(solution)/shard_map/ppermute | solution.py:43
  6.3 3.2 %copy-start.3 = (bf16[128,576]{0,1:T(8,128)(2,1)S(1)}, bf16[128,576]{0,1:T(8,128)(2,1)}, u32[]{:S(2)}) copy-start(bf16[128,576]{0,1:T(8,128)(2,1)} %param.10) | copy-start | bytes 442372
  6.4 9.7 %collective-permute-start.9 = (bf16[8,2,8,896]{3,2,1,0:T(8,128)(2,1)S(1)}, bf16[8,2,8,896]{3,2,1,0:T(8,128)(2,1)S(1)}, u32[]{:S(2)}, u32[]{:S(2)}) collective-permute-start(bf16[8,2,8,896]{3,2,1,0:T(8,128)(2,1)S(1)} %bitcast.70), channel_id=1, source_target_pairs={{0,32},{1,33},{2,34},{3,35},{4,36},{5,37},{6,38},{7,39},{8,40},{9,... | collective-permute-start | bytes 688136 | tf_op jit(solution)/shard_map/ppermute | solution.py:43
  9.6 10.1 %collective-permute-start.3 = (bf16[2,576,128]{2,1,0:T(8,128)(2,1)S(1)}, bf16[2,576,128]{2,1,0:T(8,128)(2,1)S(1)}, u32[]{:S(2)}, u32[]{:S(2)}) collective-permute-start(bf16[2,576,128]{2,1,0:T(8,128)(2,1)S(1)} %pad_maximum_fusion.refs_0_), channel_id=1, source_target_pairs={{0,64},{1,65},{2,66},{3,67},{4,68},{5,69},{6,70},{7,71},{8,72},{9,... | collective-permute-start | bytes 884744 | tf_op jit(solution)/shard_map/ppermute | solution.py:43
  11.2 15.7 %collective-permute-start.2 = (bf16[2,576,128]{2,1,0:T(8,128)(2,1)S(1)}, bf16[2,576,128]{2,1,0:T(8,128)(2,1)S(1)}, u32[]{:S(2)}, u32[]{:S(2)}) collective-permute-start(bf16[2,576,128]{2,1,0:T(8,128)(2,1)S(1)} %pad_maximum_fusion.refs_0_), channel_id=1, source_target_pairs={{0,128},{1,129},{2,130},{3,131},{4,132},{5,133},{6,134},{7,135},{8... | collective-permute-start | bytes 884744 | tf_op jit(solution)/shard_map/ppermute | solution.py:43
  14.1 12.8 %collective-permute-start.1 = (bf16[2,576,128]{2,1,0:T(8,128)(2,1)S(1)}, bf16[2,576,128]{2,1,0:T(8,128)(2,1)S(1)}, u32[]{:S(2)}, u32[]{:S(2)}) collective-permute-start(bf16[2,576,128]{2,1,0:T(8,128)(2,1)S(1)} %pad_maximum_fusion.refs_0_), channel_id=1, source_target_pairs={{0,192},{1,193},{2,194},{3,195},{4,196},{5,197},{6,198},{7,199},{8... | collective-permute-start | bytes 884744 | tf_op jit(solution)/shard_map/ppermute | solution.py:43
  15.5 11.4 %collective-permute-start.11 = (bf16[8,2,8,896]{3,2,1,0:T(8,128)(2,1)S(1)}, bf16[8,2,8,896]{3,2,1,0:T(8,128)(2,1)S(1)}, u32[]{:S(2)}, u32[]{:S(2)}) collective-permute-start(bf16[8,2,8,896]{3,2,1,0:T(8,128)(2,1)S(1)} %bitcast.71), channel_id=1, source_target_pairs={{0,33},{1,32},{2,35},{3,34},{4,37},{5,36},{6,39},{7,38},{8,41},{9,... | collective-permute-start | bytes 688136 | tf_op jit(solution)/shard_map/ppermute | solution.py:43
  16.1 10.8 %collective-permute-start.10 = (bf16[8,2,8,896]{3,2,1,0:T(8,128)(2,1)S(1)}, bf16[8,2,8,896]{3,2,1,0:T(8,128)(2,1)S(1)}, u32[]{:S(2)}, u32[]{:S(2)}) collective-permute-start(bf16[8,2,8,896]{3,2,1,0:T(8,128)(2,1)S(1)} %bitcast.69), channel_id=1, source_target_pairs={{0,1},{1,0},{2,3},{3,2},{4,5},{5,4},{6,7},{7,6},{8,9},{9,8},{10,11... | collective-permute-start | bytes 688136 | tf_op jit(solution)/shard_map/ppermute | solution.py:43
  27.2 6.8 %copy-start.4 = (s32[16]{0:T(128)S(1)}, s32[16]{0:T(128)}, u32[]{:S(2)}) copy-start(s32[16]{0:T(128)} %param.11) | copy-start | bytes 196
  27.2 7.1 %copy-start = (bf16[128,576]{0,1:T(8,128)(2,1)S(1)}, bf16[128,576]{0,1:T(8,128)(2,1)}, u32[]{:S(2)}) copy-start(bf16[128,576]{0,1:T(8,128)(2,1)} %param.9) | copy-start | bytes 442372
  27.3 23.5 %collective-permute-start.13 = (bf16[2,256,896]{2,1,0:T(8,128)(2,1)S(1)}, bf16[2,256,896]{2,1,0:T(8,128)(2,1)S(1)}, u32[]{:S(2)}, u32[]{:S(2)}) collective-permute-start(bf16[2,256,896]{2,1,0:T(8,128)(2,1)S(1)} %bitcast.59), channel_id=1, source_target_pairs={{0,64},{1,65},{2,66},{3,67},{4,68},{5,69},{6,70},{7,71},{8,72},{9,... | collective-permute-start | bytes 2752520 | tf_op jit(solution)/shard_map/ppermute | solution.py:43
  28.6 23.0 %collective-permute-start.12 = (bf16[2,256,896]{2,1,0:T(8,128)(2,1)S(1)}, bf16[2,256,896]{2,1,0:T(8,128)(2,1)}, u32[]{:S(2)}, u32[]{:S(2)}) collective-permute-start(bf16[2,256,896]{2,1,0:T(8,128)(2,1)S(1)} %bitcast.60), channel_id=1, source_target_pairs={{0,192},{1,193},{2,194},{3,195},{4,196},{5,197},{6,198},{7,199},{8... | collective-permute-start | bytes 2752520 | tf_op jit(solution)/shard_map/ppermute | solution.py:43
  30.7 2.0 %collective-permute-start.4 = (bf16[2,576,128]{2,1,0:T(8,128)(2,1)S(1)}, bf16[2,576,128]{2,1,0:T(8,128)(2,1)S(1)}, u32[]{:S(2)}, u32[]{:S(2)}) collective-permute-start(bf16[2,576,128]{2,1,0:T(8,128)(2,1)S(1)} %pad_maximum_fusion.refs_0_), channel_id=1, source_target_pairs={{0,16},{1,17},{2,18},{3,19},{4,20},{5,21},{6,22},{7,23},{8,24},{9,... | collective-permute-start | bytes 884744 | tf_op jit(solution)/shard_map/ppermute | solution.py:43
  30.7 3.5 %collective-permute-start.7 = (bf16[2,576,128]{2,1,0:T(8,128)(2,1)S(1)}, bf16[2,576,128]{2,1,0:T(8,128)(2,1)}, u32[]{:S(2)}, u32[]{:S(2)}) collective-permute-start(bf16[2,576,128]{2,1,0:T(8,128)(2,1)S(1)} %collective-permute-done.3.refs_3_), channel_id=1, source_target_pairs={{0,16},{1,17},{2,18},{3,19},{4,20},{5,21},{6,22},{7,23},{8,24},{9,... | collective-permute-start | bytes 884744 | tf_op jit(solution)/shard_map/ppermute | solution.py:43
  31.2 3.0 %collective-permute-start.6 = (bf16[2,576,128]{2,1,0:T(8,128)(2,1)S(1)}, bf16[2,576,128]{2,1,0:T(8,128)(2,1)}, u32[]{:S(2)}, u32[]{:S(2)}) collective-permute-start(bf16[2,576,128]{2,1,0:T(8,128)(2,1)S(1)} %collective-permute-done.2.refs_2_), channel_id=1, source_target_pairs={{0,16},{1,17},{2,18},{3,19},{4,20},{5,21},{6,22},{7,23},{8,24},{9,... | collective-permute-start | bytes 884744 | tf_op jit(solution)/shard_map/ppermute | solution.py:43
  32.6 1.7 %collective-permute-start.5 = (bf16[2,576,128]{2,1,0:T(8,128)(2,1)S(1)}, bf16[2,576,128]{2,1,0:T(8,128)(2,1)}, u32[]{:S(2)}, u32[]{:S(2)}) collective-permute-start(bf16[2,576,128]{2,1,0:T(8,128)(2,1)S(1)} %collective-permute-done.1.refs_1_), channel_id=1, source_target_pairs={{0,16},{1,17},{2,18},{3,19},{4,20},{5,21},{6,22},{7,23},{8,24},{9,... | collective-permute-start | bytes 884744 | tf_op jit(solution)/shard_map/ppermute | solution.py:43
  45.7 17.7 %all-to-all-start = ((bf16[4,4,128,256]{3,2,1,0:T(8,128)(2,1)}), bf16[4,4,128,256]{3,2,1,0:T(8,128)(2,1)S(1)}, u32[]{:S(2)}, u32[]{:S(2)}) async-start(bf16[4,4,128,256]{3,2,1,0:T(8,128)(2,1)} %attention.1), calls=%async_computation | async-start | bytes 2097152 | tf_op jit(solution)/shard_map/all_to_all | solution.py:338
  53.5 11.8 %collective-permute-start.14 = (bf16[256,896]{1,0:T(8,128)(2,1)}, bf16[256,896]{1,0:T(8,128)(2,1)S(1)}, u32[]{:S(2)}, u32[]{:S(2)}) collective-permute-start(bf16[256,896]{1,0:T(8,128)(2,1)} %slice_bitcast_fusion.1), channel_id=1, source_target_pairs={{0,192},{1,193},{2,194},{3,195},{4,196},{5,197},{6,198},{7,199},{8... | collective-permute-start | bytes 1376264 | tf_op jit(solution)/shard_map/ppermute | solution.py:43
  55.1 12.4 %collective-permute-start.15 = (bf16[256,896]{1,0:T(8,128)(2,1)}, bf16[256,896]{1,0:T(8,128)(2,1)}, u32[]{:S(2)}, u32[]{:S(2)}) collective-permute-start(bf16[256,896]{1,0:T(8,128)(2,1)} %slice_bitcast_fusion), channel_id=1, source_target_pairs={{0,64},{1,65},{2,66},{3,67},{4,68},{5,69},{6,70},{7,71},{8,72},{9,... | collective-permute-start | bytes 1376264 | tf_op jit(solution)/shard_map/ppermute | solution.py:43
  67.5 2.7 %collective-permute-start.16 = (bf16[4,4,128,256]{3,2,1,0:T(8,128)(2,1)S(1)}, bf16[4,4,128,256]{3,2,1,0:T(8,128)(2,1)S(1)}, u32[]{:S(2)}, u32[]{:S(2)}) collective-permute-start(bf16[4,4,128,256]{3,2,1,0:T(8,128)(2,1)S(1)} %all-to-all-done.refs_0_), channel_id=1, source_target_pairs={{0,16},{1,17},{2,18},{3,19},{4,20},{5,21},{6,22},{7,23},{8,24},{9,... | collective-permute-start | bytes 3145736 | tf_op jit(solution)/shard_map/ppermute | solution.py:43
  76.4 0.6 copy-start.1
  77.1 0.6 copy-start.2
  77.7 10.7 %collective-permute-start.17 = (bf16[2,448,128]{2,1,0:T(8,128)(2,1)}, bf16[2,448,128]{2,1,0:T(8,128)(2,1)S(1)}, u32[]{:S(2)}, u32[]{:S(2)}) collective-permute-start(bf16[2,448,128]{2,1,0:T(8,128)(2,1)} %get-tuple-element.36), channel_id=1, source_target_pairs={{0,2},{1,3},{2,4},{3,5},{4,6},{5,7},{6,8},{7,9},{8,10},{9,11},{10,... | collective-permute-start | bytes 688136 | tf_op jit(solution)/shard_map/ppermute | solution.py:43
  79.6 9.8 %collective-permute-start.18 = (bf16[2,448,128]{2,1,0:T(8,128)(2,1)}, bf16[2,448,128]{2,1,0:T(8,128)(2,1)S(1)}, u32[]{:S(2)}, u32[]{:S(2)}) collective-permute-start(bf16[2,448,128]{2,1,0:T(8,128)(2,1)} %get-tuple-element.37), channel_id=1, source_target_pairs={{0,14},{1,15},{2,0},{3,1},{4,2},{5,3},{6,4},{7,5},{8,6},{9,7},{10,... | collective-permute-start | bytes 688136 | tf_op jit(solution)/shard_map/ppermute | solution.py:43
  79.8 8.7 %collective-permute-start.20 = (bf16[448,128]{1,0:T(8,128)(2,1)}, bf16[448,128]{1,0:T(8,128)(2,1)S(1)}, u32[]{:S(2)}, u32[]{:S(2)}) collective-permute-start(bf16[448,128]{1,0:T(8,128)(2,1)} %get-tuple-element.39), channel_id=1, source_target_pairs={{0,4},{1,5},{2,6},{3,7},{4,8},{5,9},{6,10},{7,11},{8,12},{9,13},{1... | collective-permute-start | bytes 344072 | tf_op jit(solution)/shard_map/ppermute | solution.py:43
  90.5 9.1 %collective-permute-start.19 = (bf16[448,128]{1,0:T(8,128)(2,1)S(1)}, bf16[448,128]{1,0:T(8,128)(2,1)S(1)}, u32[]{:S(2)}, u32[]{:S(2)}) collective-permute-start(bf16[448,128]{1,0:T(8,128)(2,1)S(1)} %get-tuple-element.45), channel_id=1, source_target_pairs={{0,32},{1,33},{2,48},{3,49},{4,16},{5,17},{6,8},{7,9},{8,40},{9,41... | collective-permute-start | bytes 344072 | tf_op jit(solution)/shard_map/ppermute | solution.py:43
  92.1 10.9 %collective-permute-start.21 = (bf16[448,128]{1,0:T(8,128)(2,1)S(1)}, bf16[448,128]{1,0:T(8,128)(2,1)S(1)}, u32[]{:S(2)}, u32[]{:S(2)}) collective-permute-start(bf16[448,128]{1,0:T(8,128)(2,1)S(1)} %get-tuple-element.46), channel_id=1, source_target_pairs={{0,16},{1,17},{2,8},{3,9},{4,40},{5,41},{6,56},{7,57},{8,24},{9,25... | collective-permute-start | bytes 344072 | tf_op jit(solution)/shard_map/ppermute | solution.py:43
  99.6 11.1 %collective-permute-start.22 = (bf16[448,128]{1,0:T(8,128)(2,1)S(1)}, bf16[448,128]{1,0:T(8,128)(2,1)S(1)}, u32[]{:S(2)}, u32[]{:S(2)}) collective-permute-start(bf16[448,128]{1,0:T(8,128)(2,1)S(1)} %get-tuple-element.47), channel_id=1, source_target_pairs={{0,24},{1,25},{2,0},{3,1},{4,32},{5,33},{6,48},{7,49},{8,16},{9,17... | collective-permute-start | bytes 344072 | tf_op jit(solution)/shard_map/ppermute | solution.py:43

commit v4 on v3

--- a/solution.py
+++ b/solution.py
@@ -63,7 +63,7 @@
     def to(y, xl, c, z, xh):
         for half in range(2):
             owner = xl * 2 + c + 4 * half
-            step = (z + k - owner) % 8
+            step = (z + k - owner) * (1 - 2 * c) % 8
             if step in NEAR:
                 return (y, xl ^ NEAR[step][0], c ^ NEAR[step][1], owner, xh)
 
@@ -91,6 +91,7 @@
         out_shape=[jax.ShapeDtypeStruct(x, jnp.bfloat16) for x in shapes],
         in_specs=[pl.BlockSpec(memory_space=pltpu.SMEM)] + [vmem] * (len(args) - 1),
         out_specs=[vmem] * len(shapes),
+        compiler_params=pltpu.CompilerParams(vmem_limit_bytes=12 * 2**20),
         cost_estimate=pl.CostEstimate(flops=0, bytes_accessed=2 * 2**20, transcendentals=0),
         name=name,
     )(*args)
@@ -243,22 +244,16 @@
             for r in range(4):
                 cols = slice(b * 1024 + r * 256, b * 1024 + r * 256 + 256)
                 left[t * SEG_LEN : (t + 1) * SEG_LEN, cols] = heads[t % 2][source, r]
-    for n in range(7):
-        cols = slice(n * 128, (n + 1) * 128)
-        value = None
-        for b in range(2):
-            for r in range(4):
-                term = jnp.dot(
-                    left[:, b * 1024 + r * 256 : b * 1024 + r * 256 + 256],
-                    weights[b][r][:, cols],
-                    preferred_element_type=jnp.float32,
-                )
-                value = term if value is None else value + term
+    for start in range(0, 896, 256):
+        width = min(256, 896 - start)
+        cols = slice(start, start + width)
+        right = jnp.concatenate([weights[b][r][:, cols] for b in range(2) for r in range(4)], axis=0)
+        value = jnp.dot(left[...], right, preferred_element_type=jnp.float32)
         for t in range(4):
             partial[t, cols] = value[t * SEG_LEN : (t + 1) * SEG_LEN].T.astype(jnp.bfloat16)
     places = {0: (0, None), 1: (1, 0), 3: (1, 1), 7: (2, 0), 5: (2, 1), 4: (3, None), 2: (4, None), 6: (5, None)}
     for k, (out, part) in places.items():
-        step = lax.bitwise_and(z + k - xl * 2 - c, 7)
+        step = lax.bitwise_and((z + k - xl * 2 - c) * (1 - 2 * c), 7)
         upper = (step >= 3) & (step <= 6)
         near = lax.bitwise_and(jnp.where(upper, step - 4, step), 7)
         t = sum(jnp.where(near == n, a * 2 + d, 0) for n, (a, d) in NEAR.items())

time: 112 us -> 109 us (0.973)
  Pallas kernels: 20 us -> 17.9 us
  other arithmetic: 3.4 us -> 2.24 us
    pallas_call x1, Pallas kernels: 6.31 us -> 4.7 us  [project(): pl.pallas_call(project_kernel, out_shape=[one, two, two, one, one, one],...]
    pallas_call x1, Pallas kernels: 2.34 us -> 0.75 us  [small_call(): pl.pallas_call(kernel, out_shape=[jax.ShapeDtypeStruct(x, jnp.bfloat16) f...]
    unnamed x10 -> x12, local copies, waits for them, and re-layouts: 1.31 us -> 2.48 us
    select_n x1, other arithmetic: 1.32 us -> 0.16 us  [per_device(): jnp.where(c == 0, jnp.stack([keep, other], 3), jnp.stack([other, keep], 3))]
  transfers between devices with their start and end apart: 24 -> 24, of which waited for: 14 -> 14; matrix products, arithmetic and copies ran while one was open for 4% -> 3% of each run, Pallas kernels for 10% -> 11%
where the time goes in v4:
time: 109 us; the launch traced here: 108 us
  waiting for transfers between devices  42 us (39%)
  starting transfers between devices  39.2 us (36%)
  Pallas kernels  17.9 us (16%)
  local copies, waits for them, and re-layouts  5.54 us (5%)
  other arithmetic  2.24 us (2%)
  between operations  1.46 us (1%)
    ppermute x23, starting transfers between devices, move(): return lax.ppermute(x, AXES, pairs)  33.9 us
    ppermute x23, waiting for transfers between devices, move(): return lax.ppermute(x, AXES, pairs)  33.2 us
    pallas_call x1, Pallas kernels, attention(): pl.pallas_call(attention_kernel, out_shape=jax.ShapeDtypeStruct((4, 4, SE...  12.4 us
    all_to_all x1, waiting for transfers between devices, per_device(): heads = lax.all_to_all(head_out, ('xl', 'xh'), 0, 0)  8.85 us
    all_to_all x1, starting transfers between devices, per_device(): heads = lax.all_to_all(head_out, ('xl', 'xh'), 0, 0)  5.25 us
    pallas_call x1, Pallas kernels, project(): pl.pallas_call(project_kernel, out_shape=[one, two, two, one, one, one],...  4.7 us
    squeeze x2, local copies, waits for them, and re-layouts, per_device(): w2a, w2b = (w1[0], w3[1])  2.64 us
    unnamed x12, local copies, waits for them, and re-layouts  2.48 us
  transfers between devices with their start and end apart: 24, of which 14 were waited for; matrix products, arithmetic and copies ran while one was open for 3% of the time, Pallas kernels for 11%

profile of v4, /device:TPU:68, one launch (start us, length us, event | category | flops | bytes accessed | tf_op | source)
XLA Modules:
  0.0 108.4 jit_solution(18353703119456399574)
XLA Ops:
  0.1 1.2 %copy-done = bf16[8,8,7168]{2,1,0:T(8,128)(2,1)S(1)} copy-done((bf16[8,8,7168]{2,1,0:T(8,128)(2,1)S(1)}, bf16[8,8,7168]{2,1,0:T(8,128)(2,1)}, u32[]{:S(2)}) %copy-start) | copy-done | bytes 917528
  1.3 0.8 cut.1
  2.0 0.1 collective-permute-start.8
  2.1 1.3 %collective-permute-start = (bf16[576,128]{1,0:T(8,128)(2,1)}, bf16[576,128]{1,0:T(8,128)(2,1)S(1)}, u32[]{:S(2)}, u32[]{:S(2)}) collective-permute-start(bf16[576,128]{1,0:T(8,128)(2,1)} %bitcast.72), channel_id=1, source_target_pairs={{0,32},{1,33},{2,34},{3,35},{4,36},{5,37},{6,38},{7,39},{8,40},{9,... | collective-permute-start | bytes 442376 | tf_op jit(solution)/shard_map/ppermute | solution.py:43
  3.4 0.5 collective-permute-done.8
  3.9 0.2 maximum_select_fusion
  4.1 0.1 constant_dynamic-slice_fusion
  4.2 1.3 %collective-permute-start.9 = (bf16[8,2,8,896]{3,2,1,0:T(8,128)(2,1)S(1)}, bf16[8,2,8,896]{3,2,1,0:T(8,128)(2,1)S(1)}, u32[]{:S(2)}, u32[]{:S(2)}) collective-permute-start(bf16[8,2,8,896]{3,2,1,0:T(8,128)(2,1)S(1)} %bitcast.70), channel_id=1, source_target_pairs={{0,32},{1,33},{2,34},{3,35},{4,36},{5,37},{6,38},{7,39},{8,40},{9,... | collective-permute-start | bytes 688136 | tf_op jit(solution)/shard_map/ppermute | solution.py:43
  5.5 3.6 %collective-permute-done = bf16[576,128]{1,0:T(8,128)(2,1)S(1)} collective-permute-done((bf16[576,128]{1,0:T(8,128)(2,1)}, bf16[576,128]{1,0:T(8,128)(2,1)S(1)}, u32[]{:S(2)}, u32[]{:S(2)}) %collective-permute-start) | collective-permute-done | bytes 147488 | tf_op jit(solution)/shard_map/ppermute | solution.py:43
  9.1 1.7 %collective-permute-start.3 = (bf16[2,576,128]{2,1,0:T(8,128)(2,1)S(1)}, bf16[2,576,128]{2,1,0:T(8,128)(2,1)S(1)}, u32[]{:S(2)}, u32[]{:S(2)}) collective-permute-start(bf16[2,576,128]{2,1,0:T(8,128)(2,1)S(1)} %pad_maximum_fusion.refs_0_), channel_id=1, source_target_pairs={{0,64},{1,65},{2,66},{3,67},{4,68},{5,69},{6,70},{7,71},{8,72},{9,... | collective-permute-start | bytes 884744 | tf_op jit(solution)/shard_map/ppermute | solution.py:43
  10.8 2.9 %collective-permute-start.2 = (bf16[2,576,128]{2,1,0:T(8,128)(2,1)S(1)}, bf16[2,576,128]{2,1,0:T(8,128)(2,1)S(1)}, u32[]{:S(2)}, u32[]{:S(2)}) collective-permute-start(bf16[2,576,128]{2,1,0:T(8,128)(2,1)S(1)} %pad_maximum_fusion.refs_0_), channel_id=1, source_target_pairs={{0,128},{1,129},{2,130},{3,131},{4,132},{5,133},{6,134},{7,135},{8... | collective-permute-start | bytes 884744 | tf_op jit(solution)/shard_map/ppermute | solution.py:43
  13.7 1.3 %collective-permute-start.1 = (bf16[2,576,128]{2,1,0:T(8,128)(2,1)S(1)}, bf16[2,576,128]{2,1,0:T(8,128)(2,1)S(1)}, u32[]{:S(2)}, u32[]{:S(2)}) collective-permute-start(bf16[2,576,128]{2,1,0:T(8,128)(2,1)S(1)} %pad_maximum_fusion.refs_0_), channel_id=1, source_target_pairs={{0,192},{1,193},{2,194},{3,195},{4,196},{5,197},{6,198},{7,199},{8... | collective-permute-start | bytes 884744 | tf_op jit(solution)/shard_map/ppermute | solution.py:43
  15.1 0.6 collective-permute-start.11
  15.7 2.7 %collective-permute-start.10 = (bf16[8,2,8,896]{3,2,1,0:T(8,128)(2,1)S(1)}, bf16[8,2,8,896]{3,2,1,0:T(8,128)(2,1)S(1)}, u32[]{:S(2)}, u32[]{:S(2)}) collective-permute-start(bf16[8,2,8,896]{3,2,1,0:T(8,128)(2,1)S(1)} %bitcast.69), channel_id=1, source_target_pairs={{0,1},{1,0},{2,3},{3,2},{4,5},{5,4},{6,7},{7,6},{8,9},{9,8},{10,11... | collective-permute-start | bytes 688136 | tf_op jit(solution)/shard_map/ppermute | solution.py:43
  18.4 0.8 collective-permute-done.3.refs_3_
  19.2 6.8 %collective-permute-done.2.refs_2_ = bf16[2,576,128]{2,1,0:T(8,128)(2,1)S(1)} collective-permute-done((bf16[2,576,128]{2,1,0:T(8,128)(2,1)S(1)}, bf16[2,576,128]{2,1,0:T(8,128)(2,1)S(1)}, u32[]{:S(2)}, u32[]{:S(2)}) %collective-permute-start.2) | collective-permute-done | bytes 294944 | tf_op jit(solution)/shard_map/ppermute | solution.py:43
  26.1 0.1 maximum_bitcast_fusion
  26.2 0.2 maximum_select_fusion.1
  26.4 1.3 %collective-permute-start.13 = (bf16[2,256,896]{2,1,0:T(8,128)(2,1)S(1)}, bf16[2,256,896]{2,1,0:T(8,128)(2,1)S(1)}, u32[]{:S(2)}, u32[]{:S(2)}) collective-permute-start(bf16[2,256,896]{2,1,0:T(8,128)(2,1)S(1)} %bitcast.59), channel_id=1, source_target_pairs={{0,64},{1,65},{2,66},{3,67},{4,68},{5,69},{6,70},{7,71},{8,72},{9,... | collective-permute-start | bytes 2752520 | tf_op jit(solution)/shard_map/ppermute | solution.py:43
  27.7 2.0 %collective-permute-start.12 = (bf16[2,256,896]{2,1,0:T(8,128)(2,1)S(1)}, bf16[2,256,896]{2,1,0:T(8,128)(2,1)}, u32[]{:S(2)}, u32[]{:S(2)}) collective-permute-start(bf16[2,256,896]{2,1,0:T(8,128)(2,1)S(1)} %bitcast.60), channel_id=1, source_target_pairs={{0,192},{1,193},{2,194},{3,195},{4,196},{5,197},{6,198},{7,199},{8... | collective-permute-start | bytes 2752520 | tf_op jit(solution)/shard_map/ppermute | solution.py:43
  29.8 0.5 collective-permute-start.7
  30.3 1.5 %collective-permute-done.4.refs_4_ = bf16[2,576,128]{2,1,0:T(8,128)(2,1)S(1)} collective-permute-done((bf16[2,576,128]{2,1,0:T(8,128)(2,1)S(1)}, bf16[2,576,128]{2,1,0:T(8,128)(2,1)S(1)}, u32[]{:S(2)}, u32[]{:S(2)}) %collective-permute-start.4) | collective-permute-done | bytes 294944 | tf_op jit(solution)/shard_map/ppermute | solution.py:43
  31.7 0.1 collective-permute-start.5
  33.3 0.2 collective-permute-done.5.refs_5_
  33.4 12.4 %attention.1 = bf16[4,4,128,256]{3,2,1,0:T(8,128)(2,1)} custom-call(s32[23]{0:T(128)S(1)} %concatenate.4.meta, bf16[128,4608]{1,0:T(8,128)(2,1)} %q_hbm.1, bf16[576,128]{1,0:T(8,128)(2,1)S(1)} %bitcast.63, bf16[2,576,128]{2,1,0:T(8,128)(2,1)S(1)} %pad_maximum_fusion.refs_0_, bf16[2,576,128]{2,1,0:T(8,128)(2,1)S(1)} %collective-permute-done.1.refs_1_, ...), custom_call_target="tpu_custom_call" | custom-call | flops 1000000 | bytes 65536 | tf_op jit(solution)/shard_map/attention/pallas_call | solution.py:209
  45.9 5.3 %all-to-all-start = ((bf16[4,4,128,256]{3,2,1,0:T(8,128)(2,1)}), bf16[4,4,128,256]{3,2,1,0:T(8,128)(2,1)S(1)}, u32[]{:S(2)}, u32[]{:S(2)}) async-start(bf16[4,4,128,256]{3,2,1,0:T(8,128)(2,1)} %attention.1), calls=%async_computation | async-start | bytes 2097152 | tf_op jit(solution)/shard_map/all_to_all | solution.py:333
  51.1 0.8 slice_bitcast_fusion
  51.9 1.8 %slice_bitcast_fusion.1 = bf16[256,896]{1,0:T(8,128)(2,1)} fusion(bf16[2,256,896]{2,1,0:T(8,128)(2,1)} %collective-permute-done.12.refs_3_), kind=kLoop, calls=%fused_computation.3 | loop fusion | bytes 917504 | tf_op jit(solution)/shard_map/squeeze | solution.py:327
  53.8 0.4 collective-permute-start.14
  54.2 1.6 %collective-permute-start.15 = (bf16[256,896]{1,0:T(8,128)(2,1)}, bf16[256,896]{1,0:T(8,128)(2,1)}, u32[]{:S(2)}, u32[]{:S(2)}) collective-permute-start(bf16[256,896]{1,0:T(8,128)(2,1)} %slice_bitcast_fusion), channel_id=1, source_target_pairs={{0,64},{1,65},{2,66},{3,67},{4,68},{5,69},{6,70},{7,71},{8,72},{9,... | collective-permute-start | bytes 1376264 | tf_op jit(solution)/shard_map/ppermute | solution.py:43
  55.8 8.9 %all-to-all-done.refs_0_ = bf16[4,4,128,256]{3,2,1,0:T(8,128)(2,1)S(1)} async-done(((bf16[4,4,128,256]{3,2,1,0:T(8,128)(2,1)}), bf16[4,4,128,256]{3,2,1,0:T(8,128)(2,1)S(1)}, u32[]{:S(2)}, u32[]{:S(2)}) %all-to-all-start) | async-done | bytes 1048608 | tf_op jit(solution)/shard_map/all_to_all | solution.py:333
  64.7 1.8 %collective-permute-done.14.refs_5_ = bf16[256,896]{1,0:T(8,128)(2,1)S(1)} collective-permute-done((bf16[256,896]{1,0:T(8,128)(2,1)}, bf16[256,896]{1,0:T(8,128)(2,1)S(1)}, u32[]{:S(2)}, u32[]{:S(2)}) %collective-permute-start.14) | collective-permute-done | bytes 458784 | tf_op jit(solution)/shard_map/ppermute | solution.py:43
  66.4 1.3 %collective-permute-done.15.refs_6_ = bf16[256,896]{1,0:T(8,128)(2,1)} collective-permute-done((bf16[256,896]{1,0:T(8,128)(2,1)}, bf16[256,896]{1,0:T(8,128)(2,1)}, u32[]{:S(2)}, u32[]{:S(2)}) %collective-permute-start.15) | collective-permute-done | bytes 458784 | tf_op jit(solution)/shard_map/ppermute | solution.py:43
  67.8 2.7 %collective-permute-done.16.refs_1_ = bf16[4,4,128,256]{3,2,1,0:T(8,128)(2,1)S(1)} collective-permute-done((bf16[4,4,128,256]{3,2,1,0:T(8,128)(2,1)S(1)}, bf16[4,4,128,256]{3,2,1,0:T(8,128)(2,1)S(1)}, u32[]{:S(2)}, u32[]{:S(2)}) %collective-permute-start.16) | collective-permute-done | bytes 1048608 | tf_op jit(solution)/shard_map/ppermute | solution.py:43
  70.4 4.7 %project.1 = (bf16[448,128]{1,0:T(8,128)(2,1)S(1)}, bf16[2,448,128]{2,1,0:T(8,128)(2,1)}, bf16[2,448,128]{2,1,0:T(8,128)(2,1)}, bf16[448,128]{1,0:T(8,128)(2,1)}...) custom-call(s32[23]{0:T(128)S(1)} %concatenate.4.meta, bf16[4,4,128,256]{3,2,1,0:T(8,128)(2,1)S(1)} %all-to-all-done.refs_0_, ...), custom_call_target="tpu_custom_call" | custom-call | flops 1000000 | bytes 65536 | tf_op jit(solution)/shard_map/project/pallas_call | solution.py:275
  75.1 0.6 copy-done.2
  75.8 0.6 copy-done.3
  76.4 1.9 %collective-permute-start.17 = (bf16[2,448,128]{2,1,0:T(8,128)(2,1)}, bf16[2,448,128]{2,1,0:T(8,128)(2,1)S(1)}, u32[]{:S(2)}, u32[]{:S(2)}) collective-permute-start(bf16[2,448,128]{2,1,0:T(8,128)(2,1)} %get-tuple-element.36), channel_id=1, source_target_pairs={{0,2},{1,3},{2,4},{3,5},{4,6},{5,7},{6,8},{7,9},{8,10},{9,11},{10,... | collective-permute-start | bytes 688136 | tf_op jit(solution)/shard_map/ppermute | solution.py:43
  78.3 0.1 collective-permute-start.18
  78.4 5.7 %collective-permute-start.20 = (bf16[448,128]{1,0:T(8,128)(2,1)}, bf16[448,128]{1,0:T(8,128)(2,1)S(1)}, u32[]{:S(2)}, u32[]{:S(2)}) collective-permute-start(bf16[448,128]{1,0:T(8,128)(2,1)} %get-tuple-element.39), channel_id=1, source_target_pairs={{0,4},{1,5},{2,6},{3,7},{4,8},{5,9},{6,10},{7,11},{8,12},{9,13},{1... | collective-permute-start | bytes 344072 | tf_op jit(solution)/shard_map/ppermute | solution.py:43
  84.1 3.0 %collective-permute-done.20 = bf16[448,128]{1,0:T(8,128)(2,1)S(1)} collective-permute-done((bf16[448,128]{1,0:T(8,128)(2,1)}, bf16[448,128]{1,0:T(8,128)(2,1)S(1)}, u32[]{:S(2)}, u32[]{:S(2)}) %collective-permute-start.20) | collective-permute-done | bytes 114720 | tf_op jit(solution)/shard_map/ppermute | solution.py:43
  87.1 1.0 collective-permute-done.18
  88.1 1.1 %fusion.4 = (bf16[448,128]{1,0:T(8,128)(2,1)S(1)}, bf16[448,128]{1,0:T(8,128)(2,1)S(1)}, bf16[448,128]{1,0:T(8,128)(2,1)S(1)}) fusion(bf16[448,128]{1,0:T(8,128)(2,1)S(1)} %get-tuple-element.35, bf16[2,448,128]{2,1,0:T(8,128)(2,1)S(1)} %collective-permute-done.18, bf16[2,448,128]{2,1,0:T(8,128)(2,1)S(1)} %collective-permute-done.17, ...), kind=kLoop, calls=%fused_computation.16 | loop fusion | flops 1089536 | bytes 1261570 | tf_op jit(solution)/shard_map/convert_element_type | solution.py:346
  89.2 1.6 %collective-permute-start.19 = (bf16[448,128]{1,0:T(8,128)(2,1)S(1)}, bf16[448,128]{1,0:T(8,128)(2,1)S(1)}, u32[]{:S(2)}, u32[]{:S(2)}) collective-permute-start(bf16[448,128]{1,0:T(8,128)(2,1)S(1)} %get-tuple-element.45), channel_id=1, source_target_pairs={{0,32},{1,33},{2,48},{3,49},{4,16},{5,17},{6,8},{7,9},{8,40},{9,41... | collective-permute-start | bytes 344072 | tf_op jit(solution)/shard_map/ppermute | solution.py:43
  90.8 6.7 %collective-permute-start.21 = (bf16[448,128]{1,0:T(8,128)(2,1)S(1)}, bf16[448,128]{1,0:T(8,128)(2,1)S(1)}, u32[]{:S(2)}, u32[]{:S(2)}) collective-permute-start(bf16[448,128]{1,0:T(8,128)(2,1)S(1)} %get-tuple-element.46), channel_id=1, source_target_pairs={{0,16},{1,17},{2,8},{3,9},{4,40},{5,41},{6,56},{7,57},{8,24},{9,25... | collective-permute-start | bytes 344072 | tf_op jit(solution)/shard_map/ppermute | solution.py:43
  97.5 3.2 %collective-permute-done.21 = bf16[448,128]{1,0:T(8,128)(2,1)S(1)} collective-permute-done((bf16[448,128]{1,0:T(8,128)(2,1)S(1)}, bf16[448,128]{1,0:T(8,128)(2,1)S(1)}, u32[]{:S(2)}, u32[]{:S(2)}) %collective-permute-start.21) | collective-permute-done | bytes 114720 | tf_op jit(solution)/shard_map/ppermute | solution.py:43
  100.7 6.9 %collective-permute-done.22 = bf16[448,128]{1,0:T(8,128)(2,1)S(1)} collective-permute-done((bf16[448,128]{1,0:T(8,128)(2,1)S(1)}, bf16[448,128]{1,0:T(8,128)(2,1)S(1)}, u32[]{:S(2)}, u32[]{:S(2)}) %collective-permute-start.22) | collective-permute-done | bytes 114720 | tf_op jit(solution)/shard_map/ppermute | solution.py:43
  107.7 0.7 fusion.5
  (31 shorter events, 0.4 us)
Async XLA Ops:
  0.1 1.2 %copy-start = (bf16[8,8,7168]{2,1,0:T(8,128)(2,1)S(1)}, bf16[8,8,7168]{2,1,0:T(8,128)(2,1)}, u32[]{:S(2)}) copy-start(bf16[8,8,7168]{2,1,0:T(8,128)(2,1)} %w_ref.1) | copy-start | bytes 2752516
  2.0 1.9 %collective-permute-start.8 = (bf16[2,2,8,8,896]{4,3,2,1,0:T(8,128)(2,1)S(1)}, bf16[2,2,8,8,896]{4,3,2,1,0:T(8,128)(2,1)S(1)}, u32[]{:S(2)}, u32[]{:S(2)}) collective-permute-start(bf16[2,2,8,8,896]{4,3,2,1,0:T(8,128)(2,1)S(1)} %get-tuple-element.24), channel_id=1, source_target_pairs={{0,16},{1,17},{2,18},{3,19},{4,20},{5,21},{6,22},{7,23},{8,24},{9,... | collective-permute-start | bytes 1376264 | tf_op jit(solution)/shard_map/ppermute | solution.py:43
  2.1 7.0 %collective-permute-start = (bf16[576,128]{1,0:T(8,128)(2,1)}, bf16[576,128]{1,0:T(8,128)(2,1)S(1)}, u32[]{:S(2)}, u32[]{:S(2)}) collective-permute-start(bf16[576,128]{1,0:T(8,128)(2,1)} %bitcast.72), channel_id=1, source_target_pairs={{0,32},{1,33},{2,34},{3,35},{4,36},{5,37},{6,38},{7,39},{8,40},{9,... | collective-permute-start | bytes 442376 | tf_op jit(solution)/shard_map/ppermute | solution.py:43
  4.1 5.0 %copy-start.4 = (bf16[128,576]{0,1:T(8,128)(2,1)S(1)}, bf16[128,576]{0,1:T(8,128)(2,1)}, u32[]{:S(2)}) copy-start(bf16[128,576]{0,1:T(8,128)(2,1)} %param.10) | copy-start | bytes 442372
  4.2 11.5 %collective-permute-start.9 = (bf16[8,2,8,896]{3,2,1,0:T(8,128)(2,1)S(1)}, bf16[8,2,8,896]{3,2,1,0:T(8,128)(2,1)S(1)}, u32[]{:S(2)}, u32[]{:S(2)}) collective-permute-start(bf16[8,2,8,896]{3,2,1,0:T(8,128)(2,1)S(1)} %bitcast.70), channel_id=1, source_target_pairs={{0,32},{1,33},{2,34},{3,35},{4,36},{5,37},{6,38},{7,39},{8,40},{9,... | collective-permute-start | bytes 688136 | tf_op jit(solution)/shard_map/ppermute | solution.py:43
  9.1 10.1 %collective-permute-start.3 = (bf16[2,576,128]{2,1,0:T(8,128)(2,1)S(1)}, bf16[2,576,128]{2,1,0:T(8,128)(2,1)S(1)}, u32[]{:S(2)}, u32[]{:S(2)}) collective-permute-start(bf16[2,576,128]{2,1,0:T(8,128)(2,1)S(1)} %pad_maximum_fusion.refs_0_), channel_id=1, source_target_pairs={{0,64},{1,65},{2,66},{3,67},{4,68},{5,69},{6,70},{7,71},{8,72},{9,... | collective-permute-start | bytes 884744 | tf_op jit(solution)/shard_map/ppermute | solution.py:43
  10.8 15.3 %collective-permute-start.2 = (bf16[2,576,128]{2,1,0:T(8,128)(2,1)S(1)}, bf16[2,576,128]{2,1,0:T(8,128)(2,1)S(1)}, u32[]{:S(2)}, u32[]{:S(2)}) collective-permute-start(bf16[2,576,128]{2,1,0:T(8,128)(2,1)S(1)} %pad_maximum_fusion.refs_0_), channel_id=1, source_target_pairs={{0,128},{1,129},{2,130},{3,131},{4,132},{5,133},{6,134},{7,135},{8... | collective-permute-start | bytes 884744 | tf_op jit(solution)/shard_map/ppermute | solution.py:43
  13.7 12.4 %collective-permute-start.1 = (bf16[2,576,128]{2,1,0:T(8,128)(2,1)S(1)}, bf16[2,576,128]{2,1,0:T(8,128)(2,1)S(1)}, u32[]{:S(2)}, u32[]{:S(2)}) collective-permute-start(bf16[2,576,128]{2,1,0:T(8,128)(2,1)S(1)} %pad_maximum_fusion.refs_0_), channel_id=1, source_target_pairs={{0,192},{1,193},{2,194},{3,195},{4,196},{5,197},{6,198},{7,199},{8... | collective-permute-start | bytes 884744 | tf_op jit(solution)/shard_map/ppermute | solution.py:43
  15.1 11.0 %collective-permute-start.11 = (bf16[8,2,8,896]{3,2,1,0:T(8,128)(2,1)S(1)}, bf16[8,2,8,896]{3,2,1,0:T(8,128)(2,1)S(1)}, u32[]{:S(2)}, u32[]{:S(2)}) collective-permute-start(bf16[8,2,8,896]{3,2,1,0:T(8,128)(2,1)S(1)} %bitcast.71), channel_id=1, source_target_pairs={{0,33},{1,32},{2,35},{3,34},{4,37},{5,36},{6,39},{7,38},{8,41},{9,... | collective-permute-start | bytes 688136 | tf_op jit(solution)/shard_map/ppermute | solution.py:43
  15.7 10.4 %collective-permute-start.10 = (bf16[8,2,8,896]{3,2,1,0:T(8,128)(2,1)S(1)}, bf16[8,2,8,896]{3,2,1,0:T(8,128)(2,1)S(1)}, u32[]{:S(2)}, u32[]{:S(2)}) collective-permute-start(bf16[8,2,8,896]{3,2,1,0:T(8,128)(2,1)S(1)} %bitcast.69), channel_id=1, source_target_pairs={{0,1},{1,0},{2,3},{3,2},{4,5},{5,4},{6,7},{7,6},{8,9},{9,8},{10,11... | collective-permute-start | bytes 688136 | tf_op jit(solution)/shard_map/ppermute | solution.py:43
  26.3 6.8 %copy-start.5 = (s32[16]{0:T(128)S(1)}, s32[16]{0:T(128)}, u32[]{:S(2)}) copy-start(s32[16]{0:T(128)} %param.11) | copy-start | bytes 196
  26.3 7.1 %copy-start.1 = (bf16[128,576]{0,1:T(8,128)(2,1)S(1)}, bf16[128,576]{0,1:T(8,128)(2,1)}, u32[]{:S(2)}) copy-start(bf16[128,576]{0,1:T(8,128)(2,1)} %param.9) | copy-start | bytes 442372
  26.4 24.7 %collective-permute-start.13 = (bf16[2,256,896]{2,1,0:T(8,128)(2,1)S(1)}, bf16[2,256,896]{2,1,0:T(8,128)(2,1)S(1)}, u32[]{:S(2)}, u32[]{:S(2)}) collective-permute-start(bf16[2,256,896]{2,1,0:T(8,128)(2,1)S(1)} %bitcast.59), channel_id=1, source_target_pairs={{0,64},{1,65},{2,66},{3,67},{4,68},{5,69},{6,70},{7,71},{8,72},{9,... | collective-permute-start | bytes 2752520 | tf_op jit(solution)/shard_map/ppermute | solution.py:43
  27.7 24.2 %collective-permute-start.12 = (bf16[2,256,896]{2,1,0:T(8,128)(2,1)S(1)}, bf16[2,256,896]{2,1,0:T(8,128)(2,1)}, u32[]{:S(2)}, u32[]{:S(2)}) collective-permute-start(bf16[2,256,896]{2,1,0:T(8,128)(2,1)S(1)} %bitcast.60), channel_id=1, source_target_pairs={{0,192},{1,193},{2,194},{3,195},{4,196},{5,197},{6,198},{7,199},{8... | collective-permute-start | bytes 2752520 | tf_op jit(solution)/shard_map/ppermute | solution.py:43
  29.8 2.0 %collective-permute-start.4 = (bf16[2,576,128]{2,1,0:T(8,128)(2,1)S(1)}, bf16[2,576,128]{2,1,0:T(8,128)(2,1)S(1)}, u32[]{:S(2)}, u32[]{:S(2)}) collective-permute-start(bf16[2,576,128]{2,1,0:T(8,128)(2,1)S(1)} %pad_maximum_fusion.refs_0_), channel_id=1, source_target_pairs={{0,16},{1,17},{2,18},{3,19},{4,20},{5,21},{6,22},{7,23},{8,24},{9,... | collective-permute-start | bytes 884744 | tf_op jit(solution)/shard_map/ppermute | solution.py:43
  29.8 3.5 %collective-permute-start.7 = (bf16[2,576,128]{2,1,0:T(8,128)(2,1)S(1)}, bf16[2,576,128]{2,1,0:T(8,128)(2,1)}, u32[]{:S(2)}, u32[]{:S(2)}) collective-permute-start(bf16[2,576,128]{2,1,0:T(8,128)(2,1)S(1)} %collective-permute-done.3.refs_3_), channel_id=1, source_target_pairs={{0,16},{1,17},{2,18},{3,19},{4,20},{5,21},{6,22},{7,23},{8,24},{9,... | collective-permute-start | bytes 884744 | tf_op jit(solution)/shard_map/ppermute | solution.py:43
  30.3 3.0 %collective-permute-start.6 = (bf16[2,576,128]{2,1,0:T(8,128)(2,1)S(1)}, bf16[2,576,128]{2,1,0:T(8,128)(2,1)}, u32[]{:S(2)}, u32[]{:S(2)}) collective-permute-start(bf16[2,576,128]{2,1,0:T(8,128)(2,1)S(1)} %collective-permute-done.2.refs_2_), channel_id=1, source_target_pairs={{0,16},{1,17},{2,18},{3,19},{4,20},{5,21},{6,22},{7,23},{8,24},{9,... | collective-permute-start | bytes 884744 | tf_op jit(solution)/shard_map/ppermute | solution.py:43
  31.7 1.7 %collective-permute-start.5 = (bf16[2,576,128]{2,1,0:T(8,128)(2,1)S(1)}, bf16[2,576,128]{2,1,0:T(8,128)(2,1)}, u32[]{:S(2)}, u32[]{:S(2)}) collective-permute-start(bf16[2,576,128]{2,1,0:T(8,128)(2,1)S(1)} %collective-permute-done.1.refs_1_), channel_id=1, source_target_pairs={{0,16},{1,17},{2,18},{3,19},{4,20},{5,21},{6,22},{7,23},{8,24},{9,... | collective-permute-start | bytes 884744 | tf_op jit(solution)/shard_map/ppermute | solution.py:43
  45.9 18.8 %all-to-all-start = ((bf16[4,4,128,256]{3,2,1,0:T(8,128)(2,1)}), bf16[4,4,128,256]{3,2,1,0:T(8,128)(2,1)S(1)}, u32[]{:S(2)}, u32[]{:S(2)}) async-start(bf16[4,4,128,256]{3,2,1,0:T(8,128)(2,1)} %attention.1), calls=%async_computation | async-start | bytes 2097152 | tf_op jit(solution)/shard_map/all_to_all | solution.py:333
  53.8 12.7 %collective-permute-start.14 = (bf16[256,896]{1,0:T(8,128)(2,1)}, bf16[256,896]{1,0:T(8,128)(2,1)S(1)}, u32[]{:S(2)}, u32[]{:S(2)}) collective-permute-start(bf16[256,896]{1,0:T(8,128)(2,1)} %slice_bitcast_fusion.1), channel_id=1, source_target_pairs={{0,192},{1,193},{2,194},{3,195},{4,196},{5,197},{6,198},{7,199},{8... | collective-permute-start | bytes 1376264 | tf_op jit(solution)/shard_map/ppermute | solution.py:43
  54.2 13.6 %collective-permute-start.15 = (bf16[256,896]{1,0:T(8,128)(2,1)}, bf16[256,896]{1,0:T(8,128)(2,1)}, u32[]{:S(2)}, u32[]{:S(2)}) collective-permute-start(bf16[256,896]{1,0:T(8,128)(2,1)} %slice_bitcast_fusion), channel_id=1, source_target_pairs={{0,64},{1,65},{2,66},{3,67},{4,68},{5,69},{6,70},{7,71},{8,72},{9,... | collective-permute-start | bytes 1376264 | tf_op jit(solution)/shard_map/ppermute | solution.py:43
  67.8 2.7 %collective-permute-start.16 = (bf16[4,4,128,256]{3,2,1,0:T(8,128)(2,1)S(1)}, bf16[4,4,128,256]{3,2,1,0:T(8,128)(2,1)S(1)}, u32[]{:S(2)}, u32[]{:S(2)}) collective-permute-start(bf16[4,4,128,256]{3,2,1,0:T(8,128)(2,1)S(1)} %all-to-all-done.refs_0_), channel_id=1, source_target_pairs={{0,16},{1,17},{2,18},{3,19},{4,20},{5,21},{6,22},{7,23},{8,24},{9,... | collective-permute-start | bytes 3145736 | tf_op jit(solution)/shard_map/ppermute | solution.py:43
  75.1 0.6 copy-start.2
  75.8 0.6 copy-start.3
  76.4 10.7 %collective-permute-start.17 = (bf16[2,448,128]{2,1,0:T(8,128)(2,1)}, bf16[2,448,128]{2,1,0:T(8,128)(2,1)S(1)}, u32[]{:S(2)}, u32[]{:S(2)}) collective-permute-start(bf16[2,448,128]{2,1,0:T(8,128)(2,1)} %get-tuple-element.36), channel_id=1, source_target_pairs={{0,2},{1,3},{2,4},{3,5},{4,6},{5,7},{6,8},{7,9},{8,10},{9,11},{10,... | collective-permute-start | bytes 688136 | tf_op jit(solution)/shard_map/ppermute | solution.py:43
  78.3 9.8 %collective-permute-start.18 = (bf16[2,448,128]{2,1,0:T(8,128)(2,1)}, bf16[2,448,128]{2,1,0:T(8,128)(2,1)S(1)}, u32[]{:S(2)}, u32[]{:S(2)}) collective-permute-start(bf16[2,448,128]{2,1,0:T(8,128)(2,1)} %get-tuple-element.37), channel_id=1, source_target_pairs={{0,14},{1,15},{2,0},{3,1},{4,2},{5,3},{6,4},{7,5},{8,6},{9,7},{10,... | collective-permute-start | bytes 688136 | tf_op jit(solution)/shard_map/ppermute | solution.py:43
  78.4 8.7 %collective-permute-start.20 = (bf16[448,128]{1,0:T(8,128)(2,1)}, bf16[448,128]{1,0:T(8,128)(2,1)S(1)}, u32[]{:S(2)}, u32[]{:S(2)}) collective-permute-start(bf16[448,128]{1,0:T(8,128)(2,1)} %get-tuple-element.39), channel_id=1, source_target_pairs={{0,4},{1,5},{2,6},{3,7},{4,8},{5,9},{6,10},{7,11},{8,12},{9,13},{1... | collective-permute-start | bytes 344072 | tf_op jit(solution)/shard_map/ppermute | solution.py:43
  89.2 8.3 %collective-permute-start.19 = (bf16[448,128]{1,0:T(8,128)(2,1)S(1)}, bf16[448,128]{1,0:T(8,128)(2,1)S(1)}, u32[]{:S(2)}, u32[]{:S(2)}) collective-permute-start(bf16[448,128]{1,0:T(8,128)(2,1)S(1)} %get-tuple-element.45), channel_id=1, source_target_pairs={{0,32},{1,33},{2,48},{3,49},{4,16},{5,17},{6,8},{7,9},{8,40},{9,41... | collective-permute-start | bytes 344072 | tf_op jit(solution)/shard_map/ppermute | solution.py:43
  90.8 10.0 %collective-permute-start.21 = (bf16[448,128]{1,0:T(8,128)(2,1)S(1)}, bf16[448,128]{1,0:T(8,128)(2,1)S(1)}, u32[]{:S(2)}, u32[]{:S(2)}) collective-permute-start(bf16[448,128]{1,0:T(8,128)(2,1)S(1)} %get-tuple-element.46), channel_id=1, source_target_pairs={{0,16},{1,17},{2,8},{3,9},{4,40},{5,41},{6,56},{7,57},{8,24},{9,25... | collective-permute-start | bytes 344072 | tf_op jit(solution)/shard_map/ppermute | solution.py:43
  97.5 10.2 %collective-permute-start.22 = (bf16[448,128]{1,0:T(8,128)(2,1)S(1)}, bf16[448,128]{1,0:T(8,128)(2,1)S(1)}, u32[]{:S(2)}, u32[]{:S(2)}) collective-permute-start(bf16[448,128]{1,0:T(8,128)(2,1)S(1)} %get-tuple-element.47), channel_id=1, source_target_pairs={{0,24},{1,25},{2,0},{3,1},{4,32},{5,33},{6,48},{7,49},{8,16},{9,17... | collective-permute-start | bytes 344072 | tf_op jit(solution)/shard_map/ppermute | solution.py:43

commit v5 on v4

--- a/solution.py
+++ b/solution.py
@@ -223,7 +223,7 @@
             pltpu.SMEM((ANC_SEGS,), jnp.int32),
             pltpu.SemaphoreType.DMA((2,)),
         ],
-        compiler_params=pltpu.CompilerParams(vmem_limit_bytes=51 * 2**20),
+        compiler_params=pltpu.CompilerParams(vmem_limit_bytes=52 * 2**20),
         cost_estimate=pl.CostEstimate(
             flops=10**6, bytes_accessed=2**16, transcendentals=0
         ),
@@ -231,62 +231,66 @@
     )(meta, q, own, *anc, up)
 
 
-def project_kernel(meta, *refs):
-    heads = refs[:2]
-    w0, w1, w3, w2a, w2b = refs[2:7]
-    outs = refs[7:13]
-    left, partial = refs[13:]
-    xl, c, z, xh = meta[19], meta[20], meta[21], meta[22]
+def projected(meta, heads, weights, left, partial):
+    xl, xh = meta[19], meta[22]
+    w0, w1, w3, w2a, w2b = weights
     weights = [[w0.at[0], w1.at[0], w2a, w3.at[0]], [w0.at[1], w1.at[1], w2b, w3.at[1]]]
     for b in range(2):
-        for t in range(4):
-            source = lax.bitwise_xor(xl, t // 2) * 2 + lax.bitwise_xor(xh, b)
+        for a in range(2):
+            source = lax.bitwise_xor(xl, a) * 2 + lax.bitwise_xor(xh, b)
             for r in range(4):
                 cols = slice(b * 1024 + r * 256, b * 1024 + r * 256 + 256)
-                left[t * SEG_LEN : (t + 1) * SEG_LEN, cols] = heads[t % 2][source, r]
-    for start in range(0, 896, 256):
-        width = min(256, 896 - start)
-        cols = slice(start, start + width)
+                left[a * SEG_LEN : (a + 1) * SEG_LEN, cols] = heads[source, r]
+    for start in range(0, 2 * COLS, 256):
+        cols = slice(start, min(start + 256, 2 * COLS))
         right = jnp.concatenate([weights[b][r][:, cols] for b in range(2) for r in range(4)], axis=0)
         value = jnp.dot(left[...], right, preferred_element_type=jnp.float32)
-        for t in range(4):
-            partial[t, cols] = value[t * SEG_LEN : (t + 1) * SEG_LEN].T.astype(jnp.bfloat16)
+        for a in range(2):
+            partial[a, cols] = value[a * SEG_LEN : (a + 1) * SEG_LEN].T.astype(jnp.bfloat16)
+
+
+def own_kernel(meta, heads, w0, w1, w3, w2a, w2b, partial, left):
+    projected(meta, heads, (w0, w1, w3, w2a, w2b), left, partial)
+
+
+def other_kernel(meta, heads, w0, w1, w3, w2a, w2b, own, *refs):
+    outs = refs[:6]
+    partial, left = refs[6:]
+    projected(meta, heads, (w0, w1, w3, w2a, w2b), left, partial)
+    xl, c, z = meta[19], meta[20], meta[21]
     places = {0: (0, None), 1: (1, 0), 3: (1, 1), 7: (2, 0), 5: (2, 1), 4: (3, None), 2: (4, None), 6: (5, None)}
     for k, (out, part) in places.items():
         step = lax.bitwise_and((z + k - xl * 2 - c) * (1 - 2 * c), 7)
         upper = (step >= 3) & (step <= 6)
         near = lax.bitwise_and(jnp.where(upper, step - 4, step), 7)
-        t = sum(jnp.where(near == n, a * 2 + d, 0) for n, (a, d) in NEAR.items())
+        a = sum(jnp.where(near == n, x, 0) for n, (x, d) in NEAR.items())
+        core = sum(jnp.where(near == n, d, 0) for n, (x, d) in NEAR.items())
         ref = outs[out] if part is None else outs[out].at[part]
-
-        @pl.when(jnp.logical_not(upper))
-        def _(ref=ref, t=t):
-            ref[...] = partial[t, :COLS]
-
-        @pl.when(upper)
-        def _(ref=ref, t=t):
-            ref[...] = partial[t, COLS:]
-
-
-def project(meta, heads, weights):
+        for half in range(2):
+            for d, tiles in enumerate((own, partial)):
+
+                @pl.when((upper == (half == 1)) & (core == d))
+                def _(ref=ref, a=a, half=half, tiles=tiles):
+                    ref[...] = tiles[a, half * COLS : (half + 1) * COLS]
+
+
+def project(meta, heads, weights, own=None):
     vmem = pl.BlockSpec(memory_space=pltpu.VMEM)
+    half = jax.ShapeDtypeStruct((2, 2 * COLS, SEG_LEN), jnp.bfloat16)
     one = jax.ShapeDtypeStruct((COLS, SEG_LEN), jnp.bfloat16)
     two = jax.ShapeDtypeStruct((2, COLS, SEG_LEN), jnp.bfloat16)
+    left = pltpu.VMEM((2 * SEG_LEN, 2048), jnp.bfloat16)
+    args = (meta, heads, *weights) if own is None else (meta, heads, *weights, own)
     return pl.pallas_call(
-        project_kernel,
-        out_shape=[one, two, two, one, one, one],
-        in_specs=[pl.BlockSpec(memory_space=pltpu.SMEM)] + [vmem] * 7,
-        out_specs=[vmem] * 6,
-        scratch_shapes=[
-            pltpu.VMEM((4 * SEG_LEN, 2048), jnp.bfloat16),
-            pltpu.VMEM((4, 2 * COLS, SEG_LEN), jnp.bfloat16),
-        ],
+        own_kernel if own is None else other_kernel,
+        out_shape=half if own is None else [one, two, two, one, one, one],
+        in_specs=[pl.BlockSpec(memory_space=pltpu.SMEM)] + [vmem] * (len(args) - 1),
+        out_specs=vmem if own is None else [vmem] * 6,
+        scratch_shapes=[left] if own is None else [pltpu.VMEM(half.shape, half.dtype), left],
         compiler_params=pltpu.CompilerParams(vmem_limit_bytes=20 * 2**20),
-        cost_estimate=pl.CostEstimate(
-            flops=10**6, bytes_accessed=2**16, transcendentals=0
-        ),
-        name="project",
-    )(meta, *heads, *weights)
+        cost_estimate=pl.CostEstimate(flops=10**6, bytes_accessed=2**16, transcendentals=0),
+        name="project_own" if own is None else "project",
+    )(*args)
 
 
 def per_device(
@@ -332,8 +336,10 @@
     w2a, w2b = from_y(w2a, 1), from_y(w2b, 3)
     heads = lax.all_to_all(head_out, ("xl", "xh"), 0, 0)
     heads, w2a, w2b = lax.optimization_barrier((heads, w2a, w2b))
-    heads = (heads, swap_core(heads))
-    mine, right, left, far, right2, left2 = project(meta, heads, (w0, w1, w3, w2a, w2b))
+    other = swap_core(heads)
+    weights = (w0, w1, w3, w2a, w2b)
+    own = project(meta, heads, weights)
+    mine, right, left, far, right2, left2 = project(meta, other, weights, own)
     right, left = to_z(right, 1), to_z(left, -1)
     far = move(far, lambda y, xl, c, z, xh: (y, xl, c, (z + 2 - 4 * c) % 8, xh))
 

time: 109 us -> 109 us (level)
  the two profiles are of different devices: /device:TPU:68 before, /device:TPU:4 now
where the time goes in v5:
time: 109 us; the launch traced here: 108 us
  waiting for transfers between devices  50.2 us (46%)
  starting transfers between devices  31.2 us (29%)
  Pallas kernels  18.4 us (17%)
  local copies, waits for them, and re-layouts  5.56 us (5%)
  between operations  1.47 us (1%)
  other arithmetic  1.3 us (1%)
    ppermute x23, waiting for transfers between devices, move(): return lax.ppermute(x, AXES, pairs)  40.6 us
    ppermute x23, starting transfers between devices, move(): return lax.ppermute(x, AXES, pairs)  26.4 us
    pallas_call x1, Pallas kernels, attention(): pl.pallas_call(attention_kernel, out_shape=jax.ShapeDtypeStruct((4, 4, SE...  11.5 us
    all_to_all x1, waiting for transfers between devices, per_device(): heads = lax.all_to_all(head_out, ('xl', 'xh'), 0, 0)  9.55 us
    pallas_call x2, Pallas kernels, project(): pl.pallas_call(own_kernel if own is None else other_kernel, out_shape=hal...  6.1 us
    all_to_all x1, starting transfers between devices, per_device(): heads = lax.all_to_all(head_out, ('xl', 'xh'), 0, 0)  4.81 us
    unnamed x16, local copies, waits for them, and re-layouts  3.53 us
  transfers between devices with their start and end apart: 24, of which 14 were waited for; matrix products, arithmetic and copies ran while one was open for 2% of the time, Pallas kernels for 13%

profile of v5, /device:TPU:4, one launch (start us, length us, event | category | flops | bytes accessed | tf_op | source)
XLA Modules:
  0.0 108.1 jit_solution(16576323403752540078)
XLA Ops:
  0.1 1.2 %copy-done = bf16[8,8,7168]{2,1,0:T(8,128)(2,1)S(1)} copy-done((bf16[8,8,7168]{2,1,0:T(8,128)(2,1)S(1)}, bf16[8,8,7168]{2,1,0:T(8,128)(2,1)}, u32[]{:S(2)}) %copy-start) | copy-done | bytes 917528
  1.3 0.8 cut.1
  2.0 0.1 collective-permute-start.8
  2.1 1.3 %collective-permute-start = (bf16[576,128]{1,0:T(8,128)(2,1)}, bf16[576,128]{1,0:T(8,128)(2,1)S(1)}, u32[]{:S(2)}, u32[]{:S(2)}) collective-permute-start(bf16[576,128]{1,0:T(8,128)(2,1)} %bitcast.73), channel_id=1, source_target_pairs={{0,32},{1,33},{2,34},{3,35},{4,36},{5,37},{6,38},{7,39},{8,40},{9,... | collective-permute-start | bytes 442376 | tf_op jit(solution)/shard_map/ppermute | solution.py:43
  3.4 0.5 collective-permute-done.8
  3.9 0.2 maximum_select_fusion
  4.1 0.1 constant_dynamic-slice_fusion
  4.2 1.3 %collective-permute-start.9 = (bf16[8,2,8,896]{3,2,1,0:T(8,128)(2,1)S(1)}, bf16[8,2,8,896]{3,2,1,0:T(8,128)(2,1)S(1)}, u32[]{:S(2)}, u32[]{:S(2)}) collective-permute-start(bf16[8,2,8,896]{3,2,1,0:T(8,128)(2,1)S(1)} %bitcast.71), channel_id=1, source_target_pairs={{0,32},{1,33},{2,34},{3,35},{4,36},{5,37},{6,38},{7,39},{8,40},{9,... | collective-permute-start | bytes 688136 | tf_op jit(solution)/shard_map/ppermute | solution.py:43
  5.5 3.5 %collective-permute-done = bf16[576,128]{1,0:T(8,128)(2,1)S(1)} collective-permute-done((bf16[576,128]{1,0:T(8,128)(2,1)}, bf16[576,128]{1,0:T(8,128)(2,1)S(1)}, u32[]{:S(2)}, u32[]{:S(2)}) %collective-permute-start) | collective-permute-done | bytes 147488 | tf_op jit(solution)/shard_map/ppermute | solution.py:43
  9.1 3.1 %collective-permute-start.1 = (bf16[2,576,128]{2,1,0:T(8,128)(2,1)S(1)}, bf16[2,576,128]{2,1,0:T(8,128)(2,1)S(1)}, u32[]{:S(2)}, u32[]{:S(2)}) collective-permute-start(bf16[2,576,128]{2,1,0:T(8,128)(2,1)S(1)} %pad_maximum_fusion.refs_0_), channel_id=1, source_target_pairs={{0,192},{1,193},{2,194},{3,195},{4,196},{5,197},{6,198},{7,199},{8... | collective-permute-start | bytes 884744 | tf_op jit(solution)/shard_map/ppermute | solution.py:43
  12.2 0.6 collective-permute-start.2
  12.8 1.0 collective-permute-start.3
  13.9 0.6 collective-permute-start.11
  14.5 2.7 %collective-permute-start.10 = (bf16[8,2,8,896]{3,2,1,0:T(8,128)(2,1)S(1)}, bf16[8,2,8,896]{3,2,1,0:T(8,128)(2,1)S(1)}, u32[]{:S(2)}, u32[]{:S(2)}) collective-permute-start(bf16[8,2,8,896]{3,2,1,0:T(8,128)(2,1)S(1)} %bitcast.70), channel_id=1, source_target_pairs={{0,1},{1,0},{2,3},{3,2},{4,5},{5,4},{6,7},{7,6},{8,9},{9,8},{10,11... | collective-permute-start | bytes 688136 | tf_op jit(solution)/shard_map/ppermute | solution.py:43
  17.2 6.9 %collective-permute-done.1.refs_1_ = bf16[2,576,128]{2,1,0:T(8,128)(2,1)S(1)} collective-permute-done((bf16[2,576,128]{2,1,0:T(8,128)(2,1)S(1)}, bf16[2,576,128]{2,1,0:T(8,128)(2,1)S(1)}, u32[]{:S(2)}, u32[]{:S(2)}) %collective-permute-start.1) | collective-permute-done | bytes 294944 | tf_op jit(solution)/shard_map/ppermute | solution.py:43
  24.1 3.8 %collective-permute-done.3.refs_3_ = bf16[2,576,128]{2,1,0:T(8,128)(2,1)} collective-permute-done((bf16[2,576,128]{2,1,0:T(8,128)(2,1)S(1)}, bf16[2,576,128]{2,1,0:T(8,128)(2,1)}, u32[]{:S(2)}, u32[]{:S(2)}) %collective-permute-start.3) | collective-permute-done | bytes 294944 | tf_op jit(solution)/shard_map/ppermute | solution.py:43
  27.9 0.1 maximum_bitcast_fusion
  28.0 0.2 maximum_select_fusion.1
  28.3 0.7 collective-permute-start.12
  29.0 1.4 %collective-permute-start.13 = (bf16[2,256,896]{2,1,0:T(8,128)(2,1)S(1)}, bf16[2,256,896]{2,1,0:T(8,128)(2,1)S(1)}, u32[]{:S(2)}, u32[]{:S(2)}) collective-permute-start(bf16[2,256,896]{2,1,0:T(8,128)(2,1)S(1)} %bitcast.60), channel_id=1, source_target_pairs={{0,64},{1,65},{2,66},{3,67},{4,68},{5,69},{6,70},{7,71},{8,72},{9,... | collective-permute-start | bytes 2752520 | tf_op jit(solution)/shard_map/ppermute | solution.py:43
  30.4 0.5 collective-permute-start.5
  30.9 1.5 %collective-permute-done.4.refs_4_ = bf16[2,576,128]{2,1,0:T(8,128)(2,1)S(1)} collective-permute-done((bf16[2,576,128]{2,1,0:T(8,128)(2,1)S(1)}, bf16[2,576,128]{2,1,0:T(8,128)(2,1)S(1)}, u32[]{:S(2)}, u32[]{:S(2)}) %collective-permute-start.4) | collective-permute-done | bytes 294944 | tf_op jit(solution)/shard_map/ppermute | solution.py:43
  32.4 0.7 copy-done.1
  33.1 0.1 collective-permute-start.7
  34.7 0.4 collective-permute-done.7.refs_7_
  35.0 1.0 copy-done.2
  36.0 11.5 %attention.1 = bf16[4,4,128,256]{3,2,1,0:T(8,128)(2,1)} custom-call(s32[23]{0:T(128)S(1)} %concatenate.4.meta, bf16[128,4608]{1,0:T(8,128)(2,1)} %q_hbm.1, bf16[576,128]{1,0:T(8,128)(2,1)S(1)} %bitcast.64, bf16[2,576,128]{2,1,0:T(8,128)(2,1)S(1)} %pad_maximum_fusion.refs_0_, bf16[2,576,128]{2,1,0:T(8,128)(2,1)S(1)} %collective-permute-done.1.refs_1_, ...), custom_call_target="tpu_custom_call" | custom-call | flops 1000000 | bytes 65536 | tf_op jit(solution)/shard_map/attention/pallas_call | solution.py:209
  47.5 4.8 %all-to-all-start = ((bf16[4,4,128,256]{3,2,1,0:T(8,128)(2,1)}), bf16[4,4,128,256]{3,2,1,0:T(8,128)(2,1)}, u32[]{:S(2)}, u32[]{:S(2)}) async-start(bf16[4,4,128,256]{3,2,1,0:T(8,128)(2,1)} %attention.1), calls=%async_computation | async-start | bytes 2097152 | tf_op jit(solution)/shard_map/all_to_all | solution.py:337
  52.4 0.8 slice_bitcast_fusion.1
  53.2 0.8 slice_bitcast_fusion
  54.0 1.6 %collective-permute-start.14 = (bf16[256,896]{1,0:T(8,128)(2,1)}, bf16[256,896]{1,0:T(8,128)(2,1)S(1)}, u32[]{:S(2)}, u32[]{:S(2)}) collective-permute-start(bf16[256,896]{1,0:T(8,128)(2,1)} %slice_bitcast_fusion.1), channel_id=1, source_target_pairs={{0,192},{1,193},{2,194},{3,195},{4,196},{5,197},{6,198},{7,199},{8... | collective-permute-start | bytes 1376264 | tf_op jit(solution)/shard_map/ppermute | solution.py:43
  55.5 0.5 collective-permute-start.15
  56.0 9.6 %all-to-all-done.heads = bf16[4,4,128,256]{3,2,1,0:T(8,128)(2,1)} async-done(((bf16[4,4,128,256]{3,2,1,0:T(8,128)(2,1)}), bf16[4,4,128,256]{3,2,1,0:T(8,128)(2,1)}, u32[]{:S(2)}, u32[]{:S(2)}) %all-to-all-start) | async-done | bytes 1048608 | tf_op jit(solution)/shard_map/all_to_all | solution.py:337
  65.6 0.4 collective-permute-done.14.w2a
  65.9 3.3 %collective-permute-done.15.w2b = bf16[256,896]{1,0:T(8,128)(2,1)} collective-permute-done((bf16[256,896]{1,0:T(8,128)(2,1)}, bf16[256,896]{1,0:T(8,128)(2,1)}, u32[]{:S(2)}, u32[]{:S(2)}) %collective-permute-start.15) | collective-permute-done | bytes 458784 | tf_op jit(solution)/shard_map/ppermute | solution.py:43
  69.2 2.7 %project_own.1.own = bf16[2,896,128]{2,1,0:T(8,128)(2,1)S(1)} custom-call(s32[23]{0:T(128)S(1)} %concatenate.4.meta, bf16[4,4,128,256]{3,2,1,0:T(8,128)(2,1)} %all-to-all-done.heads, bf16[2,256,896]{2,1,0:T(8,128)(2,1)S(1)} %bitcast.61, bf16[2,256,896]{2,1,0:T(8,128)(2,1)S(1)} %collective-permute-done.12.w1, ...), custom_call_target="tpu_custom_call" | custom-call | flops 1000000 | bytes 65536 | tf_op jit(solution)/shard_map/project_own/pallas_call | solution.py:284
  71.9 0.2 collective-permute-done.16.heads
  72.1 0.7 copy-done.5
  72.7 3.4 %project.1 = (bf16[448,128]{1,0:T(8,128)(2,1)S(1)}, bf16[2,448,128]{2,1,0:T(8,128)(2,1)}, bf16[2,448,128]{2,1,0:T(8,128)(2,1)}, bf16[448,128]{1,0:T(8,128)(2,1)}...) custom-call(s32[23]{0:T(128)S(1)} %copy-done.5, bf16[4,4,128,256]{3,2,1,0:T(8,128)(2,1)S(1)} %collective-permute-done.16.heads, ...), custom_call_target="tpu_custom_call" | custom-call | flops 1000000 | bytes 65536 | tf_op jit(solution)/shard_map/project/pallas_call | solution.py:284
  76.2 5.9 %collective-permute-start.18 = (bf16[2,448,128]{2,1,0:T(8,128)(2,1)}, bf16[2,448,128]{2,1,0:T(8,128)(2,1)S(1)}, u32[]{:S(2)}, u32[]{:S(2)}) collective-permute-start(bf16[2,448,128]{2,1,0:T(8,128)(2,1)} %get-tuple-element.37), channel_id=1, source_target_pairs={{0,14},{1,15},{2,0},{3,1},{4,2},{5,3},{6,4},{7,5},{8,6},{9,7},{10,... | collective-permute-start | bytes 688136 | tf_op jit(solution)/shard_map/ppermute | solution.py:43
  82.0 10.0 %collective-permute-done.20 = bf16[448,128]{1,0:T(8,128)(2,1)S(1)} collective-permute-done((bf16[448,128]{1,0:T(8,128)(2,1)}, bf16[448,128]{1,0:T(8,128)(2,1)S(1)}, u32[]{:S(2)}, u32[]{:S(2)}) %collective-permute-start.20) | collective-permute-done | bytes 114720 | tf_op jit(solution)/shard_map/ppermute | solution.py:43
  92.1 0.2 collective-permute-done.17
  92.2 0.1 fusion.4
  92.4 1.6 %collective-permute-start.22 = (bf16[448,128]{1,0:T(8,128)(2,1)S(1)}, bf16[448,128]{1,0:T(8,128)(2,1)S(1)}, u32[]{:S(2)}, u32[]{:S(2)}) collective-permute-start(bf16[448,128]{1,0:T(8,128)(2,1)S(1)} %get-tuple-element.47), channel_id=1, source_target_pairs={{0,24},{1,25},{2,0},{3,1},{4,32},{5,33},{6,48},{7,49},{8,16},{9,17... | collective-permute-start | bytes 344072 | tf_op jit(solution)/shard_map/ppermute | solution.py:43
  94.0 3.5 %collective-permute-start.19 = (bf16[448,128]{1,0:T(8,128)(2,1)S(1)}, bf16[448,128]{1,0:T(8,128)(2,1)S(1)}, u32[]{:S(2)}, u32[]{:S(2)}) collective-permute-start(bf16[448,128]{1,0:T(8,128)(2,1)S(1)} %get-tuple-element.45), channel_id=1, source_target_pairs={{0,32},{1,33},{2,48},{3,49},{4,16},{5,17},{6,8},{7,9},{8,40},{9,41... | collective-permute-start | bytes 344072 | tf_op jit(solution)/shard_map/ppermute | solution.py:43
  97.5 5.0 %collective-permute-done.22 = bf16[448,128]{1,0:T(8,128)(2,1)S(1)} collective-permute-done((bf16[448,128]{1,0:T(8,128)(2,1)S(1)}, bf16[448,128]{1,0:T(8,128)(2,1)S(1)}, u32[]{:S(2)}, u32[]{:S(2)}) %collective-permute-start.22) | collective-permute-done | bytes 114720 | tf_op jit(solution)/shard_map/ppermute | solution.py:43
  102.5 4.9 %collective-permute-done.19 = bf16[448,128]{1,0:T(8,128)(2,1)S(1)} collective-permute-done((bf16[448,128]{1,0:T(8,128)(2,1)S(1)}, bf16[448,128]{1,0:T(8,128)(2,1)S(1)}, u32[]{:S(2)}, u32[]{:S(2)}) %collective-permute-start.19) | collective-permute-done | bytes 114720 | tf_op jit(solution)/shard_map/ppermute | solution.py:43
  107.4 0.7 fusion.5
  (36 shorter events, 0.4 us)
Async XLA Ops:
  0.1 1.2 %copy-start = (bf16[8,8,7168]{2,1,0:T(8,128)(2,1)S(1)}, bf16[8,8,7168]{2,1,0:T(8,128)(2,1)}, u32[]{:S(2)}) copy-start(bf16[8,8,7168]{2,1,0:T(8,128)(2,1)} %w_ref.1) | copy-start | bytes 2752516
  2.0 1.9 %collective-permute-start.8 = (bf16[2,2,8,8,896]{4,3,2,1,0:T(8,128)(2,1)S(1)}, bf16[2,2,8,8,896]{4,3,2,1,0:T(8,128)(2,1)S(1)}, u32[]{:S(2)}, u32[]{:S(2)}) collective-permute-start(bf16[2,2,8,8,896]{4,3,2,1,0:T(8,128)(2,1)S(1)} %get-tuple-element.24), channel_id=1, source_target_pairs={{0,16},{1,17},{2,18},{3,19},{4,20},{5,21},{6,22},{7,23},{8,24},{9,... | collective-permute-start | bytes 1376264 | tf_op jit(solution)/shard_map/ppermute | solution.py:43
  2.1 7.0 %collective-permute-start = (bf16[576,128]{1,0:T(8,128)(2,1)}, bf16[576,128]{1,0:T(8,128)(2,1)S(1)}, u32[]{:S(2)}, u32[]{:S(2)}) collective-permute-start(bf16[576,128]{1,0:T(8,128)(2,1)} %bitcast.73), channel_id=1, source_target_pairs={{0,32},{1,33},{2,34},{3,35},{4,36},{5,37},{6,38},{7,39},{8,40},{9,... | collective-permute-start | bytes 442376 | tf_op jit(solution)/shard_map/ppermute | solution.py:43
  4.1 5.0 %copy-start.6 = (bf16[128,576]{0,1:T(8,128)(2,1)S(1)}, bf16[128,576]{0,1:T(8,128)(2,1)}, u32[]{:S(2)}) copy-start(bf16[128,576]{0,1:T(8,128)(2,1)} %param.10) | copy-start | bytes 442372
  4.2 10.2 %collective-permute-start.9 = (bf16[8,2,8,896]{3,2,1,0:T(8,128)(2,1)S(1)}, bf16[8,2,8,896]{3,2,1,0:T(8,128)(2,1)S(1)}, u32[]{:S(2)}, u32[]{:S(2)}) collective-permute-start(bf16[8,2,8,896]{3,2,1,0:T(8,128)(2,1)S(1)} %bitcast.71), channel_id=1, source_target_pairs={{0,32},{1,33},{2,34},{3,35},{4,36},{5,37},{6,38},{7,39},{8,40},{9,... | collective-permute-start | bytes 688136 | tf_op jit(solution)/shard_map/ppermute | solution.py:43
  9.1 15.0 %collective-permute-start.1 = (bf16[2,576,128]{2,1,0:T(8,128)(2,1)S(1)}, bf16[2,576,128]{2,1,0:T(8,128)(2,1)S(1)}, u32[]{:S(2)}, u32[]{:S(2)}) collective-permute-start(bf16[2,576,128]{2,1,0:T(8,128)(2,1)S(1)} %pad_maximum_fusion.refs_0_), channel_id=1, source_target_pairs={{0,192},{1,193},{2,194},{3,195},{4,196},{5,197},{6,198},{7,199},{8... | collective-permute-start | bytes 884744 | tf_op jit(solution)/shard_map/ppermute | solution.py:43
  12.2 11.9 %collective-permute-start.2 = (bf16[2,576,128]{2,1,0:T(8,128)(2,1)S(1)}, bf16[2,576,128]{2,1,0:T(8,128)(2,1)}, u32[]{:S(2)}, u32[]{:S(2)}) collective-permute-start(bf16[2,576,128]{2,1,0:T(8,128)(2,1)S(1)} %pad_maximum_fusion.refs_0_), channel_id=1, source_target_pairs={{0,128},{1,129},{2,130},{3,131},{4,132},{5,133},{6,134},{7,135},{8... | collective-permute-start | bytes 884744 | tf_op jit(solution)/shard_map/ppermute | solution.py:43
  12.8 15.1 %collective-permute-start.3 = (bf16[2,576,128]{2,1,0:T(8,128)(2,1)S(1)}, bf16[2,576,128]{2,1,0:T(8,128)(2,1)}, u32[]{:S(2)}, u32[]{:S(2)}) collective-permute-start(bf16[2,576,128]{2,1,0:T(8,128)(2,1)S(1)} %pad_maximum_fusion.refs_0_), channel_id=1, source_target_pairs={{0,64},{1,65},{2,66},{3,67},{4,68},{5,69},{6,70},{7,71},{8,72},{9,... | collective-permute-start | bytes 884744 | tf_op jit(solution)/shard_map/ppermute | solution.py:43
  13.9 14.1 %collective-permute-start.11 = (bf16[8,2,8,896]{3,2,1,0:T(8,128)(2,1)S(1)}, bf16[8,2,8,896]{3,2,1,0:T(8,128)(2,1)S(1)}, u32[]{:S(2)}, u32[]{:S(2)}) collective-permute-start(bf16[8,2,8,896]{3,2,1,0:T(8,128)(2,1)S(1)} %bitcast.72), channel_id=1, source_target_pairs={{0,33},{1,32},{2,35},{3,34},{4,37},{5,36},{6,39},{7,38},{8,41},{9,... | collective-permute-start | bytes 688136 | tf_op jit(solution)/shard_map/ppermute | solution.py:43
  14.5 13.5 %collective-permute-start.10 = (bf16[8,2,8,896]{3,2,1,0:T(8,128)(2,1)S(1)}, bf16[8,2,8,896]{3,2,1,0:T(8,128)(2,1)S(1)}, u32[]{:S(2)}, u32[]{:S(2)}) collective-permute-start(bf16[8,2,8,896]{3,2,1,0:T(8,128)(2,1)S(1)} %bitcast.70), channel_id=1, source_target_pairs={{0,1},{1,0},{2,3},{3,2},{4,5},{5,4},{6,7},{7,6},{8,9},{9,8},{10,11... | collective-permute-start | bytes 688136 | tf_op jit(solution)/shard_map/ppermute | solution.py:43
  28.2 6.3 %copy-start.7 = (s32[16]{0:T(128)S(1)}, s32[16]{0:T(128)}, u32[]{:S(2)}) copy-start(s32[16]{0:T(128)} %param.11) | copy-start | bytes 196
  28.2 6.8 %copy-start.3 = (bf16[128,576]{0,1:T(8,128)(2,1)S(1)}, bf16[128,576]{0,1:T(8,128)(2,1)}, u32[]{:S(2)}) copy-start(bf16[128,576]{0,1:T(8,128)(2,1)} %param.9) | copy-start | bytes 442372
  28.3 24.0 %collective-permute-start.12 = (bf16[2,256,896]{2,1,0:T(8,128)(2,1)S(1)}, bf16[2,256,896]{2,1,0:T(8,128)(2,1)S(1)}, u32[]{:S(2)}, u32[]{:S(2)}) collective-permute-start(bf16[2,256,896]{2,1,0:T(8,128)(2,1)S(1)} %bitcast.59), channel_id=1, source_target_pairs={{0,192},{1,193},{2,194},{3,195},{4,196},{5,197},{6,198},{7,199},{8... | collective-permute-start | bytes 2752520 | tf_op jit(solution)/shard_map/ppermute | solution.py:43
  29.0 24.2 %collective-permute-start.13 = (bf16[2,256,896]{2,1,0:T(8,128)(2,1)S(1)}, bf16[2,256,896]{2,1,0:T(8,128)(2,1)S(1)}, u32[]{:S(2)}, u32[]{:S(2)}) collective-permute-start(bf16[2,256,896]{2,1,0:T(8,128)(2,1)S(1)} %bitcast.60), channel_id=1, source_target_pairs={{0,64},{1,65},{2,66},{3,67},{4,68},{5,69},{6,70},{7,71},{8,72},{9,... | collective-permute-start | bytes 2752520 | tf_op jit(solution)/shard_map/ppermute | solution.py:43
  30.4 2.0 %collective-permute-start.4 = (bf16[2,576,128]{2,1,0:T(8,128)(2,1)S(1)}, bf16[2,576,128]{2,1,0:T(8,128)(2,1)S(1)}, u32[]{:S(2)}, u32[]{:S(2)}) collective-permute-start(bf16[2,576,128]{2,1,0:T(8,128)(2,1)S(1)} %pad_maximum_fusion.refs_0_), channel_id=1, source_target_pairs={{0,16},{1,17},{2,18},{3,19},{4,20},{5,21},{6,22},{7,23},{8,24},{9,... | collective-permute-start | bytes 884744 | tf_op jit(solution)/shard_map/ppermute | solution.py:43
  30.4 4.2 %collective-permute-start.5 = (bf16[2,576,128]{2,1,0:T(8,128)(2,1)S(1)}, bf16[2,576,128]{2,1,0:T(8,128)(2,1)}, u32[]{:S(2)}, u32[]{:S(2)}) collective-permute-start(bf16[2,576,128]{2,1,0:T(8,128)(2,1)S(1)} %collective-permute-done.1.refs_1_), channel_id=1, source_target_pairs={{0,16},{1,17},{2,18},{3,19},{4,20},{5,21},{6,22},{7,23},{8,24},{9,... | collective-permute-start | bytes 884744 | tf_op jit(solution)/shard_map/ppermute | solution.py:43
  30.9 3.7 %collective-permute-start.6 = (bf16[2,576,128]{2,1,0:T(8,128)(2,1)}, bf16[2,576,128]{2,1,0:T(8,128)(2,1)}, u32[]{:S(2)}, u32[]{:S(2)}) collective-permute-start(bf16[2,576,128]{2,1,0:T(8,128)(2,1)} %collective-permute-done.2.refs_2_), channel_id=1, source_target_pairs={{0,16},{1,17},{2,18},{3,19},{4,20},{5,21},{6,22},{7,23},{8,24},{9,... | collective-permute-start | bytes 884744 | tf_op jit(solution)/shard_map/ppermute | solution.py:43
  32.4 0.7 copy-start.1
  33.1 1.9 %collective-permute-start.7 = (bf16[2,576,128]{2,1,0:T(8,128)(2,1)}, bf16[2,576,128]{2,1,0:T(8,128)(2,1)}, u32[]{:S(2)}, u32[]{:S(2)}) collective-permute-start(bf16[2,576,128]{2,1,0:T(8,128)(2,1)} %collective-permute-done.3.refs_3_), channel_id=1, source_target_pairs={{0,16},{1,17},{2,18},{3,19},{4,20},{5,21},{6,22},{7,23},{8,24},{9,... | collective-permute-start | bytes 884744 | tf_op jit(solution)/shard_map/ppermute | solution.py:43
  34.6 34.6 %copy-start.4 = (s32[23]{0:T(128)}, s32[23]{0:T(128)S(1)}, u32[]{:S(2)}) copy-start(s32[23]{0:T(128)S(1)} %concatenate.4.meta) | copy-start | bytes 280
  35.0 1.0 copy-start.2
  47.5 18.0 %all-to-all-start = ((bf16[4,4,128,256]{3,2,1,0:T(8,128)(2,1)}), bf16[4,4,128,256]{3,2,1,0:T(8,128)(2,1)}, u32[]{:S(2)}, u32[]{:S(2)}) async-start(bf16[4,4,128,256]{3,2,1,0:T(8,128)(2,1)} %attention.1), calls=%async_computation | async-start | bytes 2097152 | tf_op jit(solution)/shard_map/all_to_all | solution.py:337
  54.0 11.9 %collective-permute-start.14 = (bf16[256,896]{1,0:T(8,128)(2,1)}, bf16[256,896]{1,0:T(8,128)(2,1)S(1)}, u32[]{:S(2)}, u32[]{:S(2)}) collective-permute-start(bf16[256,896]{1,0:T(8,128)(2,1)} %slice_bitcast_fusion.1), channel_id=1, source_target_pairs={{0,192},{1,193},{2,194},{3,195},{4,196},{5,197},{6,198},{7,199},{8... | collective-permute-start | bytes 1376264 | tf_op jit(solution)/shard_map/ppermute | solution.py:43
  55.5 13.7 %collective-permute-start.15 = (bf16[256,896]{1,0:T(8,128)(2,1)}, bf16[256,896]{1,0:T(8,128)(2,1)}, u32[]{:S(2)}, u32[]{:S(2)}) collective-permute-start(bf16[256,896]{1,0:T(8,128)(2,1)} %slice_bitcast_fusion), channel_id=1, source_target_pairs={{0,64},{1,65},{2,66},{3,67},{4,68},{5,69},{6,70},{7,71},{8,72},{9,... | collective-permute-start | bytes 1376264 | tf_op jit(solution)/shard_map/ppermute | solution.py:43
  69.2 2.9 %collective-permute-start.16 = (bf16[4,4,128,256]{3,2,1,0:T(8,128)(2,1)}, bf16[4,4,128,256]{3,2,1,0:T(8,128)(2,1)S(1)}, u32[]{:S(2)}, u32[]{:S(2)}) collective-permute-start(bf16[4,4,128,256]{3,2,1,0:T(8,128)(2,1)} %all-to-all-done.heads), channel_id=1, source_target_pairs={{0,16},{1,17},{2,18},{3,19},{4,20},{5,21},{6,22},{7,23},{8,24},{9,... | collective-permute-start | bytes 3145736 | tf_op jit(solution)/shard_map/ppermute | solution.py:43
  72.1 0.7 copy-start.5
  76.2 15.9 %collective-permute-start.18 = (bf16[2,448,128]{2,1,0:T(8,128)(2,1)}, bf16[2,448,128]{2,1,0:T(8,128)(2,1)S(1)}, u32[]{:S(2)}, u32[]{:S(2)}) collective-permute-start(bf16[2,448,128]{2,1,0:T(8,128)(2,1)} %get-tuple-element.37), channel_id=1, source_target_pairs={{0,14},{1,15},{2,0},{3,1},{4,2},{5,3},{6,4},{7,5},{8,6},{9,7},{10,... | collective-permute-start | bytes 688136 | tf_op jit(solution)/shard_map/ppermute | solution.py:43
  82.0 10.2 %collective-permute-start.17 = (bf16[2,448,128]{2,1,0:T(8,128)(2,1)}, bf16[2,448,128]{2,1,0:T(8,128)(2,1)S(1)}, u32[]{:S(2)}, u32[]{:S(2)}) collective-permute-start(bf16[2,448,128]{2,1,0:T(8,128)(2,1)} %get-tuple-element.36), channel_id=1, source_target_pairs={{0,2},{1,3},{2,4},{3,5},{4,6},{5,7},{6,8},{7,9},{8,10},{9,11},{10,... | collective-permute-start | bytes 688136 | tf_op jit(solution)/shard_map/ppermute | solution.py:43
  82.0 10.0 %collective-permute-start.20 = (bf16[448,128]{1,0:T(8,128)(2,1)}, bf16[448,128]{1,0:T(8,128)(2,1)S(1)}, u32[]{:S(2)}, u32[]{:S(2)}) collective-permute-start(bf16[448,128]{1,0:T(8,128)(2,1)} %get-tuple-element.39), channel_id=1, source_target_pairs={{0,4},{1,5},{2,6},{3,7},{4,8},{5,9},{6,10},{7,11},{8,12},{9,13},{1... | collective-permute-start | bytes 344072 | tf_op jit(solution)/shard_map/ppermute | solution.py:43
  92.4 10.1 %collective-permute-start.22 = (bf16[448,128]{1,0:T(8,128)(2,1)S(1)}, bf16[448,128]{1,0:T(8,128)(2,1)S(1)}, u32[]{:S(2)}, u32[]{:S(2)}) collective-permute-start(bf16[448,128]{1,0:T(8,128)(2,1)S(1)} %get-tuple-element.47), channel_id=1, source_target_pairs={{0,24},{1,25},{2,0},{3,1},{4,32},{5,33},{6,48},{7,49},{8,16},{9,17... | collective-permute-start | bytes 344072 | tf_op jit(solution)/shard_map/ppermute | solution.py:43
  94.0 8.5 %collective-permute-start.21 = (bf16[448,128]{1,0:T(8,128)(2,1)S(1)}, bf16[448,128]{1,0:T(8,128)(2,1)S(1)}, u32[]{:S(2)}, u32[]{:S(2)}) collective-permute-start(bf16[448,128]{1,0:T(8,128)(2,1)S(1)} %get-tuple-element.46), channel_id=1, source_target_pairs={{0,16},{1,17},{2,8},{3,9},{4,40},{5,41},{6,56},{7,57},{8,24},{9,25... | collective-permute-start | bytes 344072 | tf_op jit(solution)/shard_map/ppermute | solution.py:43
  94.0 13.4 %collective-permute-start.19 = (bf16[448,128]{1,0:T(8,128)(2,1)S(1)}, bf16[448,128]{1,0:T(8,128)(2,1)S(1)}, u32[]{:S(2)}, u32[]{:S(2)}) collective-permute-start(bf16[448,128]{1,0:T(8,128)(2,1)S(1)} %get-tuple-element.45), channel_id=1, source_target_pairs={{0,32},{1,33},{2,48},{3,49},{4,16},{5,17},{6,8},{7,9},{8,40},{9,41... | collective-permute-start | bytes 344072 | tf_op jit(solution)/shard_map/ppermute | solution.py:43
